TPU v7x, 256 devices: a whole 4x4x8 slice. The times are simulated.
256 devices in a mesh: wide: 32 (over z, y), narrow: 8 (over x, core).
Axes of the slice: x: 4, y: 4, z: 8, core: 2. Of those that a mesh axis runs over, the one named last changes fastest.
Arguments:
- solution: float32 [8, 131072], P(None, ('wide', 'narrow')), may hold values from -6 to 6
- residual: float32 [8, 131072], P(None, ('wide', 'narrow')), may hold values from -600 to 600
- direction: float32 [8, 131072], P(None, ('wide', 'narrow')), may hold values from -600 to 600
- error_var: float32 [131072], P(('wide', 'narrow')), may hold values from 0.25 to 2
- footprint: bfloat16 [131072, 4, 128], P(('wide', 'narrow')), may hold values from -0.25 to 0.25
- tiles: int32 [131072, 4], P(('wide', 'narrow')), may hold values from 0 to 159
- window: int32 [131072, 1], P(('wide', 'narrow')), may hold values from 0 to 31; in each aligned block of 512 rows (0 to 511, 512 to 1023, ...) at most 40 rows name the same one
- temporal: bfloat16 [320, 320], replicated, may hold values from -40 to 40, as said below
- spatial_lat: bfloat16 [128, 128], replicated, may hold values from -40 to 40, as said below
- spatial_lon: bfloat16 [128, 128], replicated, may hold values from -40 to 40, as said below
Outputs:
- solution_new: float32 [8, 131072], P(None, ('wide', 'narrow'))
- residual_new: float32 [8, 131072], P(None, ('wide', 'narrow'))
- direction_new: float32 [8, 131072], P(None, ('wide', 'narrow'))
Inputs may be any that keep to these rules, and one draw needn't show every extreme that they name: At most 40 of the observations held by one device share a window, and some device reaches that in every draw. `temporal`: A symmetric positive definite covariance. `spatial_lat`: A symmetric positive definite covariance. `spatial_lon`: A symmetric positive definite covariance.
All inputs are finite; a program needn't handle non-finite values.
Results may differ from a plain program's by a relative error of at most 0.004.
Values may be sent and summed in bfloat16 or wider, within the bound.
No kernel may reach another device: no remote copies, remote signals or barrier semaphores. Data moves between devices by JAX's collectives and lax.ppermute only.
A program may use at most 128 MiB of HBM per device.

v0:
```python
import math

import jax
import jax.numpy as jnp
from jax import lax
from jax.sharding import PartitionSpec as P

HIGHEST = lax.Precision.HIGHEST


def chol_solve(matrix, right):
    chol_low = jnp.linalg.cholesky(matrix)
    half_solve = lax.linalg.triangular_solve(chol_low, right, left_side=True, lower=True)
    return lax.linalg.triangular_solve(
        chol_low, half_solve, left_side=True, lower=True, transpose_a=True
    )


def gram_matrix(left, right):
    return jnp.dot(left, right.T, precision=HIGHEST)


def on_device(
    solution,
    residual,
    direction,
    error_var,
    footprint,
    tiles,
    window,
    temporal,
    spatial_lat,
    spatial_lon,
):
    n_wide = lax.axis_size("wide")
    n_narrow = lax.axis_size("narrow")
    rhs_count, obs_dev = direction.shape
    days_total = temporal.shape[0]
    day_dev = days_total // n_wide
    lat_total = spatial_lat.shape[0]
    lat_band = lat_total // n_narrow
    lon_count = spatial_lon.shape[0]
    tile_count = tiles.shape[1]
    capacity = obs_dev * 5 // (2 * n_wide)
    slot_total = n_wide * capacity
    tiles_local = day_dev * lat_band
    window_id = window[:, 0]
    dir_half = direction.astype(jnp.bfloat16)
    matches = (window_id[:, None] == jnp.arange(n_wide, dtype=jnp.int32)[None, :]).astype(jnp.int32)
    before = jnp.cumsum(matches, axis=0) - matches
    position = jnp.sum(before * matches, axis=1)
    slot_index = window_id * capacity + position
    source = (
        jnp.full((slot_total,), obs_dev, jnp.int32)
        .at[slot_index]
        .set(jnp.arange(obs_dev, dtype=jnp.int32))
    )
    foot_rows = jnp.concatenate(
        [
            footprint.reshape(obs_dev, tile_count * lon_count),
            jnp.zeros((1, tile_count * lon_count), jnp.bfloat16),
        ],
        0,
    )
    dir_rows = jnp.concatenate([dir_half.T, jnp.zeros((1, rhs_count), jnp.bfloat16)], 0)
    tile_rows = jnp.concatenate([tiles, jnp.zeros((1, tile_count), jnp.int32)], 0)
    recv_foot, recv_dir, recv_tiles = (
        lax.all_to_all(
            foot_rows[source].reshape(n_wide, capacity, tile_count * lon_count),
            "wide",
            split_axis=0,
            concat_axis=0,
            tiled=True,
        ),
        lax.all_to_all(
            dir_rows[source].reshape(n_wide, capacity, rhs_count),
            "wide",
            split_axis=0,
            concat_axis=0,
            tiled=True,
        ),
        lax.all_to_all(
            tile_rows[source].reshape(n_wide, capacity, tile_count),
            "wide",
            split_axis=0,
            concat_axis=0,
            tiled=True,
        ),
    )
    block_size = math.gcd(slot_total, 128)
    block_count = slot_total // block_size
    rows_block = block_size * tile_count
    foot_blocks = recv_foot.reshape(block_count, rows_block, lon_count)
    dir_blocks = jnp.repeat(recv_dir.reshape(slot_total, rhs_count), tile_count, axis=0).reshape(
        block_count, rows_block, rhs_count
    )
    id_blocks = recv_tiles.reshape(block_count, rows_block)
    tile_range = jnp.arange(tiles_local, dtype=jnp.int32)

    def adjoint_step(accum, inputs):
        foot_block, dir_block, id_block = inputs
        onehot = (id_block[None, :] == tile_range[:, None]).astype(jnp.bfloat16)
        weighted = (onehot[:, None, :] * dir_block.T[None, :, :]).reshape(
            tiles_local * rhs_count, rows_block
        )
        return (accum + jnp.dot(weighted, foot_block, preferred_element_type=jnp.float32), None)

    start_accum = jnp.zeros((tiles_local * rhs_count, lon_count), jnp.float32)
    accum, _ = lax.scan(adjoint_step, start_accum, (foot_blocks, dir_blocks, id_blocks))
    flat_flux = accum.astype(jnp.bfloat16).reshape(day_dev, lat_band * rhs_count * lon_count)
    wide_index = lax.axis_index("wide")
    day_rows = lax.dynamic_slice_in_dim(temporal, wide_index * day_dev, day_dev, 0)
    columns = day_rows
    timed_sum = jnp.dot(
        columns,
        lax.all_gather(flat_flux, "wide", axis=0, tiled=True),
        preferred_element_type=jnp.float32,
    )
    timed_flux = timed_sum.astype(jnp.bfloat16)
    timed_flux = timed_flux.reshape(day_dev, lat_band, rhs_count, lon_count)
    narrow_index = lax.axis_index("narrow")
    lat_rows = lax.dynamic_slice_in_dim(spatial_lat, narrow_index * lat_band, lat_band, 0)
    columns = lat_rows
    lat_sum = jnp.einsum(
        "ab,dbrl->darl",
        columns,
        lax.all_gather(timed_flux, "narrow", axis=1, tiled=True),
        preferred_element_type=jnp.float32,
    )
    spread_lat = lat_sum.astype(jnp.bfloat16)
    smoothed = jnp.dot(
        spread_lat.reshape(-1, lon_count), spatial_lon.T, preferred_element_type=jnp.float32
    ).astype(jnp.bfloat16)
    flux_table = smoothed.reshape(tiles_local, rhs_count * lon_count)

    def forward_step(accum_dummy, inputs):
        foot_block, id_block = inputs
        picked = flux_table[id_block].reshape(rows_block, rhs_count, lon_count)
        return (
            accum_dummy,
            jnp.einsum("jrl,jl->jr", picked, foot_block, preferred_element_type=jnp.float32),
        )

    _, model_rows = lax.scan(forward_step, jnp.zeros((), jnp.float32), (foot_blocks, id_blocks))
    back_rows = (
        model_rows.reshape(slot_total, tile_count, rhs_count)
        .sum(axis=1)
        .reshape(n_wide, capacity, rhs_count)
    )
    home_rows = lax.all_to_all(back_rows, "wide", split_axis=0, concat_axis=0, tiled=True).reshape(
        slot_total, rhs_count
    )
    model_part = home_rows[slot_index].T
    model_image = model_part + error_var[None, :] * direction
    curvature, res_norm = lax.psum(
        (gram_matrix(direction, model_image), gram_matrix(residual, residual)), ("wide", "narrow")
    )
    sym = 0.5 * (curvature + curvature.T)
    step_matrix = chol_solve(sym, res_norm)
    residual_new = residual - jnp.dot(step_matrix.T, model_image, precision=HIGHEST)
    norm_new = lax.psum(gram_matrix(residual_new, residual_new), ("wide", "narrow"))
    solution_new = solution + jnp.dot(step_matrix.T, direction, precision=HIGHEST)
    ratio_matrix = chol_solve(res_norm, norm_new)
    direction_new = residual_new + jnp.dot(ratio_matrix.T, direction, precision=HIGHEST)
    return (solution_new, residual_new, direction_new)


def solution(mesh):
    in_specs = (
        P(None, ("wide", "narrow")),
        P(None, ("wide", "narrow")),
        P(None, ("wide", "narrow")),
        P(("wide", "narrow")),
        P(("wide", "narrow"), None, None),
        P(("wide", "narrow"), None),
        P(("wide", "narrow"), None),
        P(),
        P(),
        P(),
    )
    out_specs = (
        P(None, ("wide", "narrow")),
        P(None, ("wide", "narrow")),
        P(None, ("wide", "narrow")),
    )
    return jax.shard_map(
        on_device, mesh=mesh, in_specs=in_specs, out_specs=out_specs, check_vma=False
    )
```

profile of v0, /device:TPU:1, one launch (start us, length us, event | category | flops | bytes accessed | tf_op | source)
XLA Modules:
  0.0 534.6 jit_solution(1596305415718390507)
XLA Ops:
  11.4 2.4 scatter_custom_fusion
  14.8 2.4 gather_fusion.1
  18.1 12.0 %all-to-all-start = ((s32[32,1,160]{2,1,0:T(1,128)}), s32[32,1,160]{2,1,0:T(1,128)S(1)}, u32[]{:S(2)}, u32[]{:S(2)}) async-start(s32[32,1,160]{2,1,0:T(1,128)} %reshape.240), calls=%async_computation | async-start | bytes 65536 | tf_op jit(solution)/shard_map/all_to_all | solution.py:82
  30.4 2.8 gather_fusion.2
  34.1 4.7 all-to-all-done
  38.9 4.5 all-to-all-start.1
  43.5 4.7 gather_fusion.3
  48.2 3.8 all-to-all-done.1
  52.1 5.4 %all-to-all-start.2 = ((bf16[32,40,512]{2,1,0:T(8,128)(2,1)}), bf16[32,40,512]{2,1,0:T(8,128)(2,1)S(1)}, u32[]{:S(2)}, u32[]{:S(2)}) async-start(bf16[32,40,512]{2,1,0:T(8,128)(2,1)} %bitcast.16), calls=%async_computation.2 | async-start | bytes 2621440 | tf_op jit(solution)/shard_map/all_to_all | solution.py:68
  61.8 26.1 %all-to-all-done.2 = bf16[32,40,512]{2,1,0:T(8,128)(2,1)S(1)} async-done(((bf16[32,40,512]{2,1,0:T(8,128)(2,1)}), bf16[32,40,512]{2,1,0:T(8,128)(2,1)S(1)}, u32[]{:S(2)}, u32[]{:S(2)}) %all-to-all-start.2) | async-done | bytes 1310752 | tf_op jit(solution)/shard_map/all_to_all | solution.py:68
  88.7 21.2 %while.22 = (s32[]{:T(128)}, f32[1280,128]{1,0:T(8,128)S(1)}, s32[10,512]{1,0:T(8,128)}, bf16[10,512,8]{1,2,0:T(8,128)(2,1)}, bf16[10,512,128]{2,1,0:T(8,128)(2,1)S(1)}, /*index=5*/s32[]{:T(128)}, s32[]{:T(128)}) while((s32[]{:T(128)}, f32[1280,128]{1,0:T(8,128)S(1)}, s32[10,512]{1,0:T(8,128)}, bf16[10,512,8]{1,2,0:T(8,128)(2,1)}, ...), condition=%wide.region_5.6_spmd.clone, body=%wide.region_4.5_spmd.clone.sunk | while | flops 168919040 | bytes 1800291 | solution.py:109
  111.3 140.7 %all-gather.6.cloned.1.call-done = bf16[32,10,16384]{2,1,0:T(8,128)(2,1)} async-done(((bf16[1,10,16384]{2,1,0:T(8,128)(2,1)}), bf16[32,10,16384]{2,1,0:T(8,128)(2,1)}) %all-gather.6.cloned.1.call-update) | async-done | bytes 10485776 | tf_op jit(solution)/shard_map/all_gather | solution.py:116
  252.0 13.0 %reshape.224 = bf16[320,16384]{1,0:T(8,128)(2,1)} reshape(bf16[32,10,16384]{2,1,0:T(8,128)(2,1)} %all-gather.6.cloned.1.call-done) | data formatting | bytes 20971520
  265.0 5.7 %convolution_convert_fusion = bf16[10,16384]{1,0:T(8,128)(2,1)S(1)} fusion(bf16[320,16384]{1,0:T(8,128)(2,1)} %reshape.224, bf16[320,320]{1,0:T(8,128)(2,1)S(1)} %copy-done, s32[]{:T(128)S(6)} %select_n.31), kind=kOutput, calls=%fused_computation.25 | convolution fusion | flops 105021440 | bytes 10825732 | tf_op jit(solution)/shard_map/dot_general | solution.py:114
  272.4 29.2 %all-gather.4.cloned.1.call-done = bf16[10,128,8,128]{3,1,2,0:T(8,128)(2,1)} async-done(((bf16[10,16,8,128]{3,1,2,0:T(8,128)(2,1)}), bf16[10,128,8,128]{3,1,2,0:T(8,128)(2,1)}) %all-gather.4.cloned.1.call-update) | async-done | bytes 2621456 | tf_op jit(solution)/shard_map/all_gather | solution.py:127
  301.6 2.2 fusion.12
  304.3 39.0 %while.21 = (s32[]{:T(128)}, f32[10,512,8]{1,2,0:T(8,128)S(1)}, s32[10,512]{1,0:T(8,128)}, bf16[160,1024]{1,0:T(8,128)(2,1)S(1)}, bf16[10,512,128]{2,1,0:T(8,128)(2,1)S(1)}, /*index=5*/s32[]{:T(128)}) while((s32[]{:T(128)}, f32[10,512,8]{1,2,0:T(8,128)S(1)}, s32[10,512]{1,0:T(8,128)}, bf16[160,1024]{1,0:T(8,128)(2,1)S(1)}, ...), condition=%wide.region_7.8_spmd, body=%wide.region_6.7_spmd.sunk | while | flops 1051138 | bytes 5730385 | solution.py:144
  305.1 2.1 gather_fusion
  309.0 2.1 gather_fusion
  312.9 2.1 gather_fusion
  316.8 2.1 gather_fusion
  320.7 2.1 gather_fusion
  324.6 2.1 gather_fusion
  328.5 2.1 gather_fusion
  332.4 2.1 gather_fusion
  336.3 2.1 gather_fusion
  340.2 2.1 gather_fusion
  344.1 5.4 %reduce_sum.22 = f32[1280,8]{1,0:T(8,128)S(1)} reduce(f32[1280,4,8]{2,1,0:T(4,128)S(1)} %bitcast.161, f32[]{:T(128)} %constant.84.clone.1), dimensions={1}, to_apply=%region_8.9 | reduce | flops 30720 | bytes 204804 | tf_op jit(solution)/shard_map/reduce_sum | solution.py:147
  350.6 9.6 %all-to-all-start.3 = ((f32[32,1,320]{2,1,0:T(1,128)}), f32[32,1,320]{2,1,0:T(1,128)S(1)}, u32[]{:S(2)}, u32[]{:S(2)}) async-start(f32[32,1,320]{2,1,0:T(1,128)} %reshape.244), calls=%async_computation.3 | async-start | bytes 98304 | tf_op jit(solution)/shard_map/all_to_all | solution.py:150
  360.8 8.1 %all-to-all-done.3 = f32[32,1,320]{2,1,0:T(1,128)S(1)} async-done(((f32[32,1,320]{2,1,0:T(1,128)}), f32[32,1,320]{2,1,0:T(1,128)S(1)}, u32[]{:S(2)}, u32[]{:S(2)}) %all-to-all-start.3) | async-done | bytes 40992 | tf_op jit(solution)/shard_map/all_to_all | solution.py:150
  371.9 74.0 %all-reduce.3 = (f32[8,8]{0,1:T(8,128)S(1)}, f32[8,8]{1,0:T(8,128)S(1)}) all-reduce(f32[8,8]{0,1:T(8,128)S(1)} %copy-done.7, f32[8,8]{1,0:T(8,128)S(1)} %convolution_bitcast_fusion), channel_id=1, replica_groups=mesh['wide'=32,'narrow'=8] {'wide','narrow'}, use_global_device_ids=true, to_apply=%region_12.14 | all-reduce | flops 128 | bytes 1024 | tf_op jit(solution)/shard_map/psum | solution.py:155
  452.3 73.5 %psum.23 = f32[8,8]{1,0:T(8,128)S(1)} all-reduce(f32[8,8]{1,0:T(8,128)S(1)} %fusion.40), channel_id=1, replica_groups=mesh['wide'=32,'narrow'=8] {'wide','narrow'}, use_global_device_ids=true, to_apply=%region_13.17 | all-reduce | flops 64 | bytes 512 | tf_op jit(solution)/shard_map/psum | solution.py:161
  (213 shorter events, 68.5 us)
Async XLA Ops:
  7.2 257.8 %copy-start = (bf16[320,320]{1,0:T(8,128)(2,1)S(1)}, bf16[320,320]{1,0:T(8,128)(2,1)}, u32[]{:S(2)}) copy-start(bf16[320,320]{1,0:T(8,128)(2,1)} %param.26) | copy-start | bytes 614404
  10.8 0.6 copy-start.10
  14.7 15.4 %copy-start.2 = (f32[8,512]{1,0:T(8,128)S(1)}, f32[8,512]{1,0:T(8,128)}, u32[]{:S(2)}) copy-start(f32[8,512]{1,0:T(8,128)} %param.21) | copy-start | bytes 49156
  18.1 20.7 %all-to-all-start = ((s32[32,1,160]{2,1,0:T(1,128)}), s32[32,1,160]{2,1,0:T(1,128)S(1)}, u32[]{:S(2)}, u32[]{:S(2)}) async-start(s32[32,1,160]{2,1,0:T(1,128)} %reshape.240), calls=%async_computation | async-start | bytes 65536 | tf_op jit(solution)/shard_map/all_to_all | solution.py:82
  30.4 13.0 %copy-start.3 = (bf16[512,4,128]{2,1,0:T(4,128)(2,1)S(1)}, bf16[512,4,128]{2,1,0:T(4,128)(2,1)}, u32[]{:S(2)}) copy-start(bf16[512,4,128]{2,1,0:T(4,128)(2,1)} %param.23) | copy-start | bytes 1572868
  38.9 13.2 %all-to-all-start.1 = ((bf16[32,2,160]{2,1,0:T(2,128)(2,1)}), bf16[32,2,160]{2,1,0:T(2,128)(2,1)S(1)}, u32[]{:S(2)}, u32[]{:S(2)}) async-start(bf16[32,2,160]{2,1,0:T(2,128)(2,1)} %reshape.242), calls=%async_computation.1 | async-start | bytes 65536 | tf_op jit(solution)/shard_map/all_to_all | solution.py:75
  52.1 35.9 %all-to-all-start.2 = ((bf16[32,40,512]{2,1,0:T(8,128)(2,1)}), bf16[32,40,512]{2,1,0:T(8,128)(2,1)S(1)}, u32[]{:S(2)}, u32[]{:S(2)}) async-start(bf16[32,40,512]{2,1,0:T(8,128)(2,1)} %bitcast.16), calls=%async_computation.2 | async-start | bytes 2621440 | tf_op jit(solution)/shard_map/all_to_all | solution.py:68
  57.5 194.5 %all-gather.6.cloned.1.call-start = ((), (), s32[]{:S(2)}) async-start(), calls=%async_computation.5 | async-start | bytes 17301504 | tf_op jit(solution)/shard_map/all_gather | solution.py:116
  61.8 26.9 %copy-start.1 = (f32[1280,128]{1,0:T(8,128)S(1)}, f32[1280,128]{1,0:T(8,128)}, u32[]{:S(2)}) copy-start(f32[1280,128]{1,0:T(8,128)} %custom-call.10) | copy-start | bytes 1966084
  111.0 190.6 %all-gather.4.cloned.1.call-start = ((), (), s32[]{:S(2)}) async-start(), calls=%async_computation.4 | async-start | bytes 2949120 | tf_op jit(solution)/shard_map/all_gather | solution.py:127
  270.7 1.0 copy-start.5
  272.4 31.5 %copy-start.6 = (bf16[128,128]{1,0:T(8,128)(2,1)S(1)}, bf16[128,128]{1,0:T(8,128)(2,1)}, u32[]{:S(2)}) copy-start(bf16[128,128]{1,0:T(8,128)(2,1)} %param.28) | copy-start | bytes 98308
  350.6 18.4 %all-to-all-start.3 = ((f32[32,1,320]{2,1,0:T(1,128)}), f32[32,1,320]{2,1,0:T(1,128)S(1)}, u32[]{:S(2)}, u32[]{:S(2)}) async-start(f32[32,1,320]{2,1,0:T(1,128)} %reshape.244), calls=%async_computation.3 | async-start | bytes 98304 | tf_op jit(solution)/shard_map/all_to_all | solution.py:150
  370.6 1.2 copy-start.9
  370.6 1.3 copy-start.7
  370.6 156.3 %copy-start.8 = (f32[8,512]{1,0:T(8,128)S(1)}, f32[8,512]{1,0:T(8,128)}, u32[]{:S(2)}) copy-start(f32[8,512]{1,0:T(8,128)} %param.19) | copy-start | bytes 49156
  452.1 75.7 %copy-start.4 = (f32[8,512]{1,0:T(8,128)}, f32[8,512]{1,0:T(8,128)S(1)}, u32[]{:S(2)}) copy-start(f32[8,512]{1,0:T(8,128)S(1)} %convolution_subtract_fusion) | copy-start | bytes 49156
Sparse Core Ops, SparseCore 0:
  111.2 140.7 all-gather.5
  271.7 29.8 all-gather.3
where the time goes:
time: 537 us; the launch traced here: 535 us
  waiting for transfers between devices  213 us (40%)
  blocking collectives  148 us (28%)
  local copies, waits for them, and re-layouts  78.5 us (15%)
  starting transfers between devices  31.7 us (6%)
  matrix products  24.7 us (5%)
  other arithmetic  24.2 us (5%)
  between operations  14.5 us (3%)
    all_gather x1, waiting for transfers between devices, on_device(): lax.all_gather(flat_flux, 'wide', axis=0, tiled=True)  141 us
    psum x1, blocking collectives, on_device(): lax.psum((gram_matrix(direction, model_image), gram_matrix(residual, resi...  74 us
    psum x1, blocking collectives, on_device(): lax.psum(gram_matrix(residual_new, residual_new), ('wide', 'narrow'))  73.5 us
    all_gather x1, waiting for transfers between devices, on_device(): lax.all_gather(timed_flux, 'narrow', axis=1, tiled=True)  29.2 us
    all_to_all x1, waiting for transfers between devices, on_device(): lax.all_to_all(foot_rows[source].reshape(n_wide, capacity, tile_count * l...  26.1 us
    gather x10, local copies, waits for them, and re-layouts, forward_step(): picked = flux_table[id_block].reshape(rows_block, rhs_count, lon_count)  20.6 us
    unnamed x34, local copies, waits for them, and re-layouts  19.3 us
    all_to_all x1, starting transfers between devices, on_device(): lax.all_to_all(tile_rows[source].reshape(n_wide, capacity, tile_count), '...  12 us
  transfers between devices with their start and end apart: 6, of which 6 were waited for; matrix products, arithmetic and copies ran while one was open for 3% of the time, Pallas kernels for 0%

commit v1 on v0

v1 whole, which is shorter than its diff:
```python
import jax
import jax.numpy as jnp
from jax import lax
from jax.experimental import pallas as pl
from jax.experimental.pallas import tpu as pltpu
from jax.sharding import PartitionSpec as P

F32 = jnp.float32
BF16 = jnp.bfloat16
I32 = jnp.int32
HIGHEST = lax.Precision.HIGHEST
LANES = 128
RHS = 8
NT = 4
N_WIDE = 32
N_NARROW = 8
OBS_DEV = 512
CAP = 40
SLOTS = N_WIDE * CAP
DAY_DEV = 10
DAYS = N_WIDE * DAY_DEV
LAT = 128
CELLS = 160
QUAD = 4
CHUNK = DAY_DEV * QUAD
ROWS = RHS * CELLS
META = 48
PAYLOAD = NT * CAP + 16
GRAM_AT = CAP
VMEM_LIMIT = 48 * 1024 * 1024


def dot_rows(left, right, precision=None):
    return lax.dot_general(
        left, right, (((1,), (1,)), ((), ())), precision=precision, preferred_element_type=F32
    )


def dot(left, right, precision=None):
    return lax.dot_general(
        left, right, (((1,), (0,)), ((), ())), precision=precision, preferred_element_type=F32
    )


def lane_window(block):
    start = min(block * CAP // LANES * LANES, SLOTS - 2 * LANES)
    return start, block * CAP - start


def take_lanes(ref, row, rows, block):
    start, shift = lane_window(block)
    part = ref[row : row + rows, start : start + 2 * LANES]
    return pltpu.roll(part, (2 * LANES - shift) % (2 * LANES), 1)[:, :LANES]


def add_lanes(ref, row, rows, block, piece):
    start, shift = lane_window(block)
    wide = jnp.concatenate([piece, jnp.zeros((rows, LANES), F32)], axis=1)
    ref[row : row + rows, start : start + 2 * LANES] += pltpu.roll(wide, shift, 1)


def split_two(value):
    high = value.astype(BF16)
    return high.astype(F32), value - high.astype(F32)


def slot_matrix(slot_row):
    rows = lax.broadcasted_iota(I32, (SLOTS, OBS_DEV), 0)
    return jnp.where(rows == slot_row, 1.0, 0.0).astype(BF16)


def pack_kernel(
    window_ref, tiles_ref, foot_ref, dir_ref, res_ref, err_ref, send_ref, slot_ref, pick, moved, meta
):
    window = window_ref[...]
    named = lax.broadcasted_iota(I32, (N_WIDE, OBS_DEV), 0) == window
    named_f = jnp.where(named, 1.0, 0.0)
    earlier = lax.broadcasted_iota(I32, (OBS_DEV, OBS_DEV), 0) < lax.broadcasted_iota(
        I32, (OBS_DEV, OBS_DEV), 1
    )
    before = dot(named_f.astype(BF16), jnp.where(earlier, 1.0, 0.0).astype(BF16))
    position = jnp.sum(before * named_f, axis=0, keepdims=True).astype(I32)
    slot = window * CAP + position
    slot_ref[...] = slot
    pick[...] = slot_matrix(slot)
    moved[...] = dot(pick[...], foot_ref[...])
    tile = tiles_ref[...]
    day, row = tile >> 4, tile & 15
    cell = ((row >> 2) * CHUNK + day * QUAD + (row & 3)).astype(F32)
    dir_high, dir_low = split_two(dir_ref[...])
    res_high, res_low = split_two(res_ref[...])
    err_high, err_low = split_two(err_ref[...])
    zero = jnp.zeros((2, OBS_DEV), F32)
    values = jnp.concatenate(
        [
            dir_high,
            jnp.concatenate([cell, err_high, err_low, zero], axis=0),
            dir_low,
            res_high,
            res_low,
            jnp.zeros((8, OBS_DEV), F32),
        ],
        axis=0,
    ).astype(BF16)
    meta[...] = dot_rows(values, pick[...])
    lane = lax.broadcasted_iota(I32, (16, LANES), 1)
    for block in range(N_WIDE):
        rows = slice(block * CAP, (block + 1) * CAP)
        parts = [moved[rows, k * LANES : (k + 1) * LANES] for k in range(NT)]
        send_ref[block, : NT * CAP, :] = jnp.concatenate(parts, axis=0).astype(BF16)
        groups = [take_lanes(meta, 16 * g, 16, block) for g in range(3)]
        joined = jnp.where(
            lane < CAP,
            groups[0],
            jnp.where(
                lane < 2 * CAP,
                pltpu.roll(groups[1], CAP, 1),
                jnp.where(lane < 3 * CAP, pltpu.roll(groups[2], 2 * CAP, 1), 0.0),
            ),
        )
        send_ref[block, NT * CAP :, :] = joined.astype(BF16)


def adjoint_kernel(recv_ref, flux_ref, meta_ref, foot_ref, rows_f, hot, weighted, total):
    meta_ref[...] = jnp.zeros((META, SLOTS), F32)
    lane = lax.broadcasted_iota(I32, (16, LANES), 1)
    for block in range(N_WIDE):
        values = recv_ref[block, : NT * CAP, :].astype(F32)
        for k in range(NT):
            rows_f[k, block * CAP : (block + 1) * CAP, :] = values[k * CAP : (k + 1) * CAP, :]
        joined = recv_ref[block, NT * CAP :, :].astype(F32)
        for g in range(3):
            piece = joined if g == 0 else pltpu.roll(joined, LANES - g * CAP, 1)
            add_lanes(meta_ref, 16 * g, 16, block, jnp.where(lane < CAP, piece, 0.0))
    cells = lax.broadcasted_iota(I32, (CELLS, SLOTS), 0)
    for k in range(NT):
        foot = rows_f[k].astype(BF16)
        foot_ref[k] = foot
        ids = meta_ref[8 + k : 9 + k, :].astype(I32)
        hot[...] = jnp.where(cells == ids, 1.0, 0.0).astype(BF16)
        for r in range(RHS):
            row = jnp.broadcast_to(meta_ref[r : r + 1, :], (16, SLOTS)).astype(BF16)
            for t in range(CELLS // 16):
                weighted[r * CELLS + t * 16 : r * CELLS + (t + 1) * 16, :] = (
                    hot[t * 16 : (t + 1) * 16, :] * row
                )
        product = dot(weighted[...], foot)
        if k == 0:
            total[...] = product
        elif k < NT - 1:
            total[...] += product
        else:
            flux_ref[...] = (total[...] + product).astype(BF16)


def lat_kernel(mix_ref, flux_ref, out_ref, rows_f, columns):
    rows_f[...] = flux_ref[...].astype(F32)
    for a in range(QUAD):
        for d in range(DAY_DEV):
            columns[a * N_WIDE : (a + 1) * N_WIDE, d * LANES : (d + 1) * LANES] = rows_f[
                pl.ds(d * QUAD + a, N_WIDE, stride=CHUNK), :
            ].astype(BF16)
    mixed = dot(mix_ref[...], columns[...])
    for a in range(QUAD):
        for d in range(DAY_DEV):
            rows_f[pl.ds(d * QUAD + a, N_WIDE, stride=CHUNK), :] = mixed[
                a * N_WIDE : (a + 1) * N_WIDE, d * LANES : (d + 1) * LANES
            ]
    out_ref[...] = rows_f[...].astype(BF16)


def day_kernel(mix_ref, flux_ref, out_ref, rows_f, columns):
    rows_f[...] = flux_ref[...].astype(F32)
    for a in range(QUAD):
        columns[:, a * LANES : (a + 1) * LANES] = rows_f[
            pl.ds(a, DAYS, stride=QUAD), :
        ].astype(BF16)
    mixed = dot(mix_ref[...], columns[...])
    for a in range(QUAD):
        rows_f[pl.ds(a, DAYS, stride=QUAD), :] = mixed[:, a * LANES : (a + 1) * LANES]
    out_ref[...] = rows_f[...].astype(BF16)


def forward_kernel(
    lon_ref, spread_ref, foot_ref, meta_ref, dir_ref, res_ref, err_ref, send_ref, table, picked, model
):
    table[...] = dot_rows(spread_ref[...], lon_ref[...]).astype(BF16)
    width = 2 * LANES
    cells = lax.broadcasted_iota(I32, (CELLS, width), 0)
    for tile in range(SLOTS // width):
        at = slice(tile * width, (tile + 1) * width)
        sums = [jnp.zeros((1, width), F32)] * RHS
        for k in range(NT):
            picked[...] = dot_rows(table[...], foot_ref[k, at, :])
            mask = cells == meta_ref[8 + k : 9 + k, at].astype(I32)
            for r in range(RHS):
                rows = picked[r * CELLS : (r + 1) * CELLS, :]
                sums[r] = sums[r] + jnp.sum(jnp.where(mask, rows, 0.0), axis=0, keepdims=True)
        model[:, at] = jnp.concatenate(sums, axis=0)
    held_dir = meta_ref[0:8, :] + meta_ref[16:24, :]
    held_res = meta_ref[24:32, :] + meta_ref[32:40, :]
    held_err = meta_ref[12:13, :] + meta_ref[13:14, :]
    modelled = model[...]
    held = jnp.concatenate([modelled, held_dir, held_res, held_err * held_dir], axis=0)
    far = dot_rows(held, held, HIGHEST)
    direction = dir_ref[...]
    own = jnp.concatenate([direction, res_ref[...], err_ref[...] * direction], axis=0)
    near = dot_rows(own, own, HIGHEST)
    gram = jnp.concatenate(
        [
            jnp.zeros((RHS, GRAM_AT), F32),
            far[0:8, 8:16] + near[16:24, 0:8],
            far[8:16, 0:8] + near[0:8, 16:24],
            far[0:8, 16:24] + near[16:24, 8:16],
            far[16:24, 0:8] + near[8:16, 16:24],
            far[0:8, 0:8] + far[0:8, 24:32] + far[24:32, 0:8] + near[16:24, 16:24],
            near[8:16, 8:16],
            jnp.zeros((RHS, LANES - GRAM_AT - 48), F32),
        ],
        axis=1,
    )
    lane = lax.broadcasted_iota(I32, (RHS, LANES), 1)
    for block in range(N_WIDE):
        send_ref[block] = jnp.where(lane < CAP, take_lanes(model, 0, RHS, block), gram)


def gather_kernel(home_ref, slot_ref, dir_ref, err_ref, image_ref, lined):
    lined[...] = jnp.zeros((RHS, SLOTS), F32)
    lane = lax.broadcasted_iota(I32, (RHS, LANES), 1)
    for block in range(N_WIDE):
        add_lanes(lined, 0, RHS, block, jnp.where(lane < CAP, home_ref[block], 0.0))
    high, rest = split_two(lined[...])
    middle, low = split_two(rest)
    parts = jnp.concatenate([high, middle, low], axis=0).astype(BF16)
    placed = dot(parts, slot_matrix(slot_ref[...]))
    image_ref[...] = placed[0:8] + placed[8:16] + placed[16:24] + err_ref[...] * dir_ref[...]


def inverses(matrices):
    row = lax.broadcasted_iota(I32, (RHS, RHS), 0)
    column = lax.broadcasted_iota(I32, (RHS, RHS), 1)
    unit = jnp.where(row == column, 1.0, 0.0)
    state = [jnp.concatenate([m, unit], axis=1) for m in matrices]
    side = lax.broadcasted_iota(I32, (RHS, 2 * RHS), 0)
    for j in range(RHS):
        following = []
        for m in state:
            pivot = m[j : j + 1, :] / m[j : j + 1, j : j + 1]
            following.append(jnp.where(side == j, pivot, m - m[:, j : j + 1] * pivot))
        state = following
    return [m[:, RHS:] for m in state]


def update_kernel(gram_ref, sol_ref, res_ref, dir_ref, image_ref, sol_out, res_out, dir_out):
    total = gram_ref[0]
    for n in range(1, N_NARROW):
        total = total + gram_ref[n]
    block = lambda g: total[:, GRAM_AT + 8 * g : GRAM_AT + 8 * g + 8]
    image_dir, dir_image, image_res, res_image, image_image, res_norm = [block(g) for g in range(6)]
    sym = 0.5 * (image_dir + dir_image)
    sym_inverse, norm_inverse = inverses([sym, res_norm])
    step = dot(sym_inverse, res_norm, HIGHEST)
    step_t = dot(res_norm, sym_inverse, HIGHEST)
    crossed = dot(step_t, image_res, HIGHEST) + dot(res_image, step, HIGHEST)
    squared = dot(dot(step_t, image_image, HIGHEST), step, HIGHEST)
    norm_new = res_norm - crossed + squared
    ratio_t = dot(norm_new, norm_inverse, HIGHEST)
    direction = dir_ref[...]
    sol_out[...] = sol_ref[...] + dot(step_t, direction, HIGHEST)
    residual = res_ref[...] - dot(step_t, image_ref[...], HIGHEST)
    res_out[...] = residual
    dir_out[...] = residual + dot(ratio_t, direction, HIGHEST)


def call(kernel, outs, scratch, flops, moved):
    return pl.pallas_call(
        kernel,
        out_shape=[jax.ShapeDtypeStruct(shape, dtype) for shape, dtype in outs],
        scratch_shapes=[pltpu.VMEM(shape, dtype) for shape, dtype in scratch],
        compiler_params=pltpu.CompilerParams(vmem_limit_bytes=VMEM_LIMIT),
        cost_estimate=pl.CostEstimate(flops=flops, bytes_accessed=moved, transcendentals=0),
    )


def exchange(array, axis):
    return lax.all_to_all(array, axis, split_axis=0, concat_axis=0, tiled=True)


def on_device(
    solution,
    residual,
    direction,
    error_var,
    footprint,
    tiles,
    window,
    temporal,
    spatial_lat,
    spatial_lon,
):
    errors = error_var.reshape(1, OBS_DEV)
    with jax.named_scope("pack"):
        packed, slot = call(
            pack_kernel,
            [((N_WIDE, PAYLOAD, LANES), BF16), ((1, OBS_DEV), I32)],
            [
                ((SLOTS, OBS_DEV), BF16),
                ((SLOTS, NT * LANES), F32),
                ((META, SLOTS), F32),
            ],
            2 * SLOTS * OBS_DEV * NT * LANES,
            2 * SLOTS * OBS_DEV,
        )(
            window.reshape(1, OBS_DEV),
            tiles.T,
            footprint.reshape(OBS_DEV, NT * LANES),
            direction,
            residual,
            errors,
        )
    with jax.named_scope("route"):
        routed = exchange(packed, "wide")
    with jax.named_scope("adjoint"):
        flux, meta, foot = call(
            adjoint_kernel,
            [((ROWS, LANES), BF16), ((META, SLOTS), F32), ((NT, SLOTS, LANES), BF16)],
            [
                ((NT, SLOTS, LANES), F32),
                ((CELLS, SLOTS), BF16),
                ((ROWS, SLOTS), BF16),
                ((ROWS, LANES), F32),
            ],
            2 * ROWS * NT * SLOTS * LANES,
            4 * NT * SLOTS * LANES,
        )(routed)
    with jax.named_scope("to_rhs"):
        by_rhs = exchange(flux.reshape(N_NARROW, CELLS, LANES), "narrow")
    with jax.named_scope("lat_mix"):
        lat_mix = (
            spatial_lat.reshape(N_WIDE, QUAD, N_WIDE, QUAD).transpose(1, 0, 3, 2).reshape(LAT, LAT)
        )
        (spread,) = call(
            lat_kernel,
            [((ROWS, LANES), BF16)],
            [((ROWS, LANES), F32), ((LAT, DAY_DEV * LANES), BF16)],
            2 * LAT * LAT * DAY_DEV * LANES,
            4 * ROWS * LANES,
        )(lat_mix, by_rhs.reshape(ROWS, LANES))
    with jax.named_scope("to_days"):
        by_day = exchange(spread.reshape(N_WIDE, CHUNK, LANES), "wide")
    with jax.named_scope("day_mix"):
        (timed,) = call(
            day_kernel,
            [((ROWS, LANES), BF16)],
            [((ROWS, LANES), F32), ((DAYS, QUAD * LANES), BF16)],
            2 * DAYS * DAYS * QUAD * LANES,
            4 * ROWS * LANES,
        )(temporal, by_day.reshape(ROWS, LANES))
    with jax.named_scope("to_windows"):
        by_window = exchange(timed.reshape(N_WIDE, CHUNK, LANES), "wide")
    with jax.named_scope("to_bands"):
        by_band = exchange(by_window.reshape(N_NARROW, CELLS, LANES), "narrow")
    with jax.named_scope("forward"):
        (modelled,) = call(
            forward_kernel,
            [((N_WIDE, RHS, LANES), F32)],
            [((ROWS, LANES), BF16), ((ROWS, 2 * LANES), F32), ((RHS, SLOTS), F32)],
            2 * ROWS * NT * SLOTS * LANES,
            4 * NT * SLOTS * LANES,
        )(
            spatial_lon,
            by_band.reshape(ROWS, LANES),
            foot,
            meta,
            direction,
            residual,
            errors,
        )
    with jax.named_scope("home"):
        home = exchange(modelled, "wide")
    with jax.named_scope("gram_sum"):
        partial = jnp.broadcast_to(home.sum(axis=0)[None], (N_NARROW, RHS, LANES))
        grams = exchange(partial, "narrow")
    with jax.named_scope("image"):
        (image,) = call(
            gather_kernel,
            [((RHS, OBS_DEV), F32)],
            [((RHS, SLOTS), F32)],
            2 * 24 * SLOTS * OBS_DEV,
            4 * SLOTS * RHS,
        )(home, slot, direction, errors)
    with jax.named_scope("update"):
        return tuple(
            call(
                update_kernel,
                [((RHS, OBS_DEV), F32)] * 3,
                [],
                2 * 18 * 8 * 8 * OBS_DEV,
                28 * RHS * OBS_DEV,
            )(grams, solution, residual, direction, image)
        )


def solution(mesh):
    both = ("wide", "narrow")
    in_specs = (
        P(None, both),
        P(None, both),
        P(None, both),
        P(both),
        P(both, None, None),
        P(both, None),
        P(both, None),
        P(),
        P(),
        P(),
    )
    out_specs = (P(None, both), P(None, both), P(None, both))
    return jax.shard_map(
        on_device, mesh=mesh, in_specs=in_specs, out_specs=out_specs, check_vma=False
    )
```

time: 537 us -> 151 us (0.28)
  waiting for transfers between devices: 213 us -> 8.22 us
  local copies, waits for them, and re-layouts: 78.5 us -> 8.43 us
  blocking collectives: 148 us -> 107 us
  matrix products: 24.7 us -> 0 us
  other arithmetic: 24.2 us -> 0.04 us
  starting transfers between devices: 31.7 us -> 12.2 us
  Pallas kernels: 0 us -> 13.9 us
  between operations: 14.5 us -> 0.77 us
    all_gather x2 -> x0, waiting for transfers between devices: 170 us -> none  [the longest x1 141 us: on_device(): lax.all_gather(flat_flux, 'wide', axis=0, tiled=True)]
    psum x2 -> x0, blocking collectives: 148 us -> none  [the longest x1 74 us: on_device(): lax.psum((gram_matrix(direction, model_image), gram_matrix(residual, resi...]
    all_to_all x0 -> x5, blocking collectives: none -> 107 us  [exchange(): return lax.all_to_all(array, axis, split_axis=0, concat_axis=0, tiled=True)]
    all_to_all x4 -> x2, waiting for transfers between devices: 42.8 us -> 8.22 us  [exchange(): return lax.all_to_all(array, axis, split_axis=0, concat_axis=0, tiled=True)]
    gather x15 -> x0, local copies, waits for them, and re-layouts: 31.6 us -> none  [the longest x10 20.6 us: forward_step(): picked = flux_table[id_block].reshape(rows_block, rhs_count, lon_count)]
    dot_general x29 -> x0, matrix products: 24.1 us -> none  [the longest x10 6.77 us: forward_step(): jnp.einsum('jrl,jl->jr', picked, foot_block, preferred_element_type=jnp.f...]
    all_to_all x4 -> x2, starting transfers between devices: 31.5 us -> 12.2 us  [exchange(): return lax.all_to_all(array, axis, split_axis=0, concat_axis=0, tiled=True)]
    unnamed x34 -> x25, local copies, waits for them, and re-layouts: 19.3 us -> 4.65 us
  transfers between devices with their start and end apart: 6 -> 2, of which waited for: 6 -> 2; matrix products, arithmetic and copies ran while one was open for 3% -> 2% of each run, Pallas kernels for 0% -> 0%
where the time goes in v1:
time: 151 us; the launch traced here: 150 us
  blocking collectives  107 us (71%)
  Pallas kernels  13.9 us (9%)
  starting transfers between devices  12.2 us (8%)
  local copies, waits for them, and re-layouts  8.43 us (6%)
  waiting for transfers between devices  8.22 us (5%)
    all_to_all x5, blocking collectives, exchange(): return lax.all_to_all(array, axis, split_axis=0, concat_axis=0, tiled=True)  107 us
    all_to_all x2, starting transfers between devices, exchange(): return lax.all_to_all(array, axis, split_axis=0, concat_axis=0, tiled=True)  12.2 us
    all_to_all x2, waiting for transfers between devices, exchange(): return lax.all_to_all(array, axis, split_axis=0, concat_axis=0, tiled=True)  8.22 us
    unnamed x25, local copies, waits for them, and re-layouts  4.65 us
    pallas_call x1, Pallas kernels, on_device(): call(adjoint_kernel, [((ROWS, LANES), BF16), ((META, SLOTS), F32), ((NT,...  4.4 us
    pallas_call x1, Pallas kernels, on_device(): call(forward_kernel, [((N_WIDE, RHS, LANES), F32)], [((ROWS, LANES), BF16...  4.26 us
  transfers between devices with their start and end apart: 2, of which 2 were waited for; matrix products, arithmetic and copies ran while one was open for 2% of the time, Pallas kernels for 0%

profile of v1, /device:TPU:1, one launch (start us, length us, event | category | flops | bytes accessed | tf_op | source)
XLA Modules:
  0.0 150.5 jit_solution(3142722716830330812)
XLA Ops:
  0.6 1.1 copy.17
  1.8 0.0 copy-start.1
  1.8 0.7 copy-done.1
  2.5 0.7 copy-done.3
  3.2 0.7 copy-done.6
  3.9 0.7 copy-done.9
  4.6 0.7 copy-done.10
  5.3 1.5 %pack.1 = (bf16[32,176,128]{2,1,0:T(8,128)(2,1)S(1)}, s32[1,512]{1,0:T(1,128)S(1)}) custom-call(s32[1,512]{1,0:T(1,128)S(1)} %bitcast.25, s32[4,512]{1,0:T(4,128)S(1)} %bitcast.24, bf16[512,512]{1,0:T(8,128)(2,1)S(1)} %bitcast.19, f32[8,512]{1,0:T(8,128)S(1)} %copy-done.1, f32[8,512]{1,0:T(8,128)S(1)} %copy-done.3, f32[1,512]{1,0:T(1,128)S(1)} %bitcast.21), custom_call_target="tpu_custom_call" | custom-call | flops 671088640 | bytes 1310720 | tf_op jit(solution)/shard_map/pack/pallas_call | solution.py:303
  6.8 48.1 %all_to_all.35.recv_ref = bf16[32,176,128]{2,1,0:T(8,128)(2,1)S(1)} all-to-all(bf16[32,176,128]{2,1,0:T(8,128)(2,1)S(1)} %get-tuple-element.8), channel_id=1, replica_groups=mesh['wide'=32,'narrow'=8] {'wide'}, dimensions={0} | all-to-all | bytes 2883584 | tf_op jit(solution)/shard_map/route/all_to_all | solution.py:286
  54.9 4.4 %adjoint.1 = (bf16[1280,128]{1,0:T(8,128)(2,1)}, f32[48,1280]{1,0:T(8,128)S(1)}, bf16[4,1280,128]{2,1,0:T(8,128)(2,1)S(1)}) custom-call(bf16[32,176,128]{2,1,0:T(8,128)(2,1)S(1)} %all_to_all.35.recv_ref), custom_call_target="tpu_custom_call" | custom-call | flops 1677721600 | bytes 2621440 | tf_op jit(solution)/shard_map/adjoint/pallas_call | solution.py:324
  59.3 6.8 %all-to-all-start.1 = ((bf16[8,160,128]{2,1,0:T(8,128)(2,1)}), bf16[8,160,128]{2,1,0:T(8,128)(2,1)S(1)}, u32[]{:S(2)}, u32[]{:S(2)}) async-start(bf16[8,160,128]{2,1,0:T(8,128)(2,1)} %bitcast.4), calls=%async_computation.1 | async-start | bytes 655360 | tf_op jit(solution)/shard_map/to_rhs/all_to_all | solution.py:286
  66.1 2.2 %reshape.43 = bf16[32,4,32,4]{3,2,1,0:T(8,128)(2,1)S(1)} reshape(bf16[128,128]{1,0:T(8,128)(2,1)S(1)} %copy-done.11) | data formatting | bytes 65536 | tf_op jit(solution)/shard_map/lat_mix/reshape | solution.py:340
  68.3 0.0 copy-start
  68.4 0.8 copy.14
  69.2 0.1 reshape.44.mix_ref
  69.3 3.9 %all-to-all-done.1 = bf16[8,160,128]{2,1,0:T(8,128)(2,1)S(1)} async-done(((bf16[8,160,128]{2,1,0:T(8,128)(2,1)}), bf16[8,160,128]{2,1,0:T(8,128)(2,1)S(1)}, u32[]{:S(2)}, u32[]{:S(2)}) %all-to-all-start.1) | async-done | bytes 327712 | tf_op jit(solution)/shard_map/to_rhs/all_to_all | solution.py:286
  73.2 0.4 lat_mix.1
  73.6 0.0 copy-start.2
  73.7 0.0 copy-start.4
  73.7 0.0 copy-start.8
  73.7 16.0 %all_to_all.36 = bf16[32,40,128]{2,1,0:T(8,128)(2,1)S(1)} all-to-all(bf16[32,40,128]{2,1,0:T(8,128)(2,1)S(1)} %bitcast.18), channel_id=1, replica_groups=mesh['wide'=32,'narrow'=8] {'wide'}, dimensions={0} | all-to-all | bytes 655360 | tf_op jit(solution)/shard_map/to_days/all_to_all | solution.py:286
  89.7 0.5 day_mix.1
  90.2 15.7 %all_to_all.37 = bf16[32,40,128]{2,1,0:T(8,128)(2,1)S(1)} all-to-all(bf16[32,40,128]{2,1,0:T(8,128)(2,1)S(1)} %bitcast.16), channel_id=1, replica_groups=mesh['wide'=32,'narrow'=8] {'wide'}, dimensions={0} | all-to-all | bytes 655360 | tf_op jit(solution)/shard_map/to_windows/all_to_all | solution.py:286
  105.9 14.4 %all_to_all.38 = bf16[8,160,128]{2,1,0:T(8,128)(2,1)S(1)} all-to-all(bf16[8,160,128]{2,1,0:T(8,128)(2,1)S(1)} %bitcast.27), channel_id=1, replica_groups=mesh['wide'=32,'narrow'=8] {'narrow'}, dimensions={0} | all-to-all | bytes 655360 | tf_op jit(solution)/shard_map/to_bands/all_to_all | solution.py:286
  120.3 0.0 copy-start.5
  120.3 4.3 %forward.1 = f32[32,8,128]{2,1,0:T(8,128)S(1)} custom-call(bf16[128,128]{1,0:T(8,128)(2,1)S(1)} %copy-done.8, bf16[1280,128]{1,0:T(8,128)(2,1)S(1)} %bitcast.20, bf16[4,1280,128]{2,1,0:T(8,128)(2,1)S(1)} %get-tuple-element.10.foot_ref, f32[48,1280]{1,0:T(8,128)S(1)} %get-tuple-element.11.meta_ref, f32[8,512]{1,0:T(8,128)S(1)} %copy-done.2, ...), custom_call_target="tpu_custom_call" | custom-call | flops 1677721600 | bytes 2621440 | tf_op jit(solution)/shard_map/forward/pallas_call | solution.py:364
  124.5 12.7 %all_to_all.39.home_ref = f32[32,8,128]{2,1,0:T(8,128)S(1)} all-to-all(f32[32,8,128]{2,1,0:T(8,128)S(1)} %forward.1), channel_id=1, replica_groups=mesh['wide'=32,'narrow'=8] {'wide'}, dimensions={0} | all-to-all | bytes 262144 | tf_op jit(solution)/shard_map/home/all_to_all | solution.py:286
  137.3 0.6 broadcast_in_dim.2
  137.9 5.4 %all-to-all-start.6 = ((f32[8,8,128]{2,1,0:T(8,128)}), f32[8,8,128]{2,1,0:T(8,128)S(1)}, u32[]{:S(2)}, u32[]{:S(2)}) async-start(f32[8,8,128]{2,1,0:T(8,128)} %broadcast_in_dim.2), calls=%async_computation.6 | async-start | bytes 65536 | tf_op jit(solution)/shard_map/gram_sum/all_to_all | solution.py:286
  143.3 0.4 image.1.image_ref
  143.7 4.3 %all-to-all-done.6.gram_ref = f32[8,8,128]{2,1,0:T(8,128)S(1)} async-done(((f32[8,8,128]{2,1,0:T(8,128)}), f32[8,8,128]{2,1,0:T(8,128)S(1)}, u32[]{:S(2)}, u32[]{:S(2)}) %all-to-all-start.6) | async-done | bytes 32800 | tf_op jit(solution)/shard_map/gram_sum/all_to_all | solution.py:286
  148.0 2.4 %update.1 = (f32[8,512]{1,0:T(8,128)}, f32[8,512]{1,0:T(8,128)}, f32[8,512]{1,0:T(8,128)}) custom-call(f32[8,8,128]{2,1,0:T(8,128)S(1)} %all-to-all-done.6.gram_ref, f32[8,512]{1,0:T(8,128)S(1)} %copy-done.5, f32[8,512]{1,0:T(8,128)S(1)} %copy-done.4, f32[8,512]{1,0:T(8,128)S(1)} %copy-done.2, f32[8,512]{1,0:T(8,128)S(1)} %image.1.image_ref), custom_call_target="tpu_custom_call" | custom-call | flops 1179648 | bytes 114688 | tf_op jit(solution)/shard_map/update/pallas_call | solution.py:394
  (14 shorter events, 0.1 us)
Async XLA Ops:
  1.8 0.7 copy-start.1
  2.5 0.7 copy-start.3
  3.2 0.7 copy-start.6
  3.9 0.7 copy-start.9
  4.6 0.7 copy-start.10
  54.9 11.2 %copy-start.11 = (bf16[128,128]{1,0:T(8,128)(2,1)S(1)}, bf16[128,128]{1,0:T(8,128)(2,1)}, u32[]{:S(2)}) copy-start(bf16[128,128]{1,0:T(8,128)(2,1)} %param.18) | copy-start | bytes 98308
  59.3 13.9 %all-to-all-start.1 = ((bf16[8,160,128]{2,1,0:T(8,128)(2,1)}), bf16[8,160,128]{2,1,0:T(8,128)(2,1)S(1)}, u32[]{:S(2)}, u32[]{:S(2)}) async-start(bf16[8,160,128]{2,1,0:T(8,128)(2,1)} %bitcast.4), calls=%async_computation.1 | async-start | bytes 655360 | tf_op jit(solution)/shard_map/to_rhs/all_to_all | solution.py:286
  68.3 21.4 %copy-start = (bf16[320,320]{1,0:T(8,128)(2,1)S(1)}, bf16[320,320]{1,0:T(8,128)(2,1)}, u32[]{:S(2)}) copy-start(bf16[320,320]{1,0:T(8,128)(2,1)} %mix_ref.1) | copy-start | bytes 614404
  73.6 46.6 %copy-start.2 = (f32[8,512]{1,0:T(8,128)S(1)}, f32[8,512]{1,0:T(8,128)}, u32[]{:S(2)}) copy-start(f32[8,512]{1,0:T(8,128)} %dir_ref.7) | copy-start | bytes 49156
  73.7 46.6 %copy-start.4 = (f32[8,512]{1,0:T(8,128)S(1)}, f32[8,512]{1,0:T(8,128)}, u32[]{:S(2)}) copy-start(f32[8,512]{1,0:T(8,128)} %res_ref.5) | copy-start | bytes 49156
  73.7 46.6 %copy-start.7 = (f32[512]{0:T(512)S(1)}, f32[512]{0:T(512)}, u32[]{:S(2)}) copy-start(f32[512]{0:T(512)} %param.13) | copy-start | bytes 6148
  73.7 46.6 %copy-start.8 = (bf16[128,128]{1,0:T(8,128)(2,1)S(1)}, bf16[128,128]{1,0:T(8,128)(2,1)}, u32[]{:S(2)}) copy-start(bf16[128,128]{1,0:T(8,128)(2,1)} %lon_ref.1) | copy-start | bytes 98308
  120.3 27.8 %copy-start.5 = (f32[8,512]{1,0:T(8,128)S(1)}, f32[8,512]{1,0:T(8,128)}, u32[]{:S(2)}) copy-start(f32[8,512]{1,0:T(8,128)} %sol_ref.1) | copy-start | bytes 49156
  137.9 10.1 %all-to-all-start.6 = ((f32[8,8,128]{2,1,0:T(8,128)}), f32[8,8,128]{2,1,0:T(8,128)S(1)}, u32[]{:S(2)}, u32[]{:S(2)}) async-start(f32[8,8,128]{2,1,0:T(8,128)} %broadcast_in_dim.2), calls=%async_computation.6 | async-start | bytes 65536 | tf_op jit(solution)/shard_map/gram_sum/all_to_all | solution.py:286

commit v2 on v1

--- a/solution.py
+++ b/solution.py
@@ -27,7 +27,9 @@
 META = 48
 PAYLOAD = NT * CAP + 16
 GRAM_AT = CAP
+SEND_BLOCKS = 8
 VMEM_LIMIT = 48 * 1024 * 1024
+VMEM_WHOLE = 63 * 1024 * 1024
 
 
 def dot_rows(left, right, precision=None):
@@ -70,20 +72,72 @@
 
 
 def pack_kernel(
-    window_ref, tiles_ref, foot_ref, dir_ref, res_ref, err_ref, send_ref, slot_ref, pick, moved, meta
+    window_hbm,
+    tiles_hbm,
+    foot_hbm,
+    dir_hbm,
+    res_hbm,
+    err_hbm,
+    turn_ref,
+    send_hbm,
+    slot_ref,
+    send_ref,
+    window_ref,
+    tiles_ref,
+    foot_ref,
+    dir_ref,
+    res_ref,
+    err_ref,
+    by_tile,
+    pick,
+    moved,
+    meta,
+    sems,
+    send_sems,
 ):
-    window = window_ref[...]
-    named = lax.broadcasted_iota(I32, (N_WIDE, OBS_DEV), 0) == window
-    named_f = jnp.where(named, 1.0, 0.0)
+    copies = [
+        pltpu.make_async_copy(source, target, sems.at[i])
+        for i, (source, target) in enumerate(
+            [
+                (window_hbm, window_ref),
+                (foot_hbm, foot_ref),
+                (dir_hbm, dir_ref),
+                (res_hbm, res_ref),
+                (err_hbm, err_ref),
+                (tiles_hbm, tiles_ref),
+            ]
+        )
+    ]
+    for copy in copies:
+        copy.start()
     earlier = lax.broadcasted_iota(I32, (OBS_DEV, OBS_DEV), 0) < lax.broadcasted_iota(
         I32, (OBS_DEV, OBS_DEV), 1
     )
-    before = dot(named_f.astype(BF16), jnp.where(earlier, 1.0, 0.0).astype(BF16))
+    earlier = jnp.where(earlier, 1.0, 0.0).astype(BF16)
+    copies[0].wait()
+    owner = window_ref[...] ^ turn_ref[0]
+    named = lax.broadcasted_iota(I32, (N_WIDE, OBS_DEV), 0) == owner
+    named_f = jnp.where(named, 1.0, 0.0)
+    before = dot(named_f.astype(BF16), earlier)
     position = jnp.sum(before * named_f, axis=0, keepdims=True).astype(I32)
-    slot = window * CAP + position
+    slot = owner * CAP + position
     slot_ref[...] = slot
     pick[...] = slot_matrix(slot)
-    moved[...] = dot(pick[...], foot_ref[...])
+    group = 2 * LANES
+    share = group // NT
+    out_row = lax.broadcasted_iota(I32, (group, group), 0)
+    in_row = lax.broadcasted_iota(I32, (group, group), 1)
+    sort = jnp.where(in_row == out_row % share * NT + out_row // share, 1.0, 0.0).astype(BF16)
+    copies[1].wait()
+    for g in range(OBS_DEV // share):
+        rows = dot(sort, foot_ref[g * group : (g + 1) * group, :]).astype(BF16)
+        for k in range(NT):
+            by_tile[g * share : (g + 1) * share, k * LANES : (k + 1) * LANES] = rows[
+                k * share : (k + 1) * share, :
+            ]
+    moved[...] = dot(pick[...], by_tile[...])
+    for copy in copies[2:]:
+        copy.wait()
     tile = tiles_ref[...]
     day, row = tile >> 4, tile & 15
     cell = ((row >> 2) * CHUNK + day * QUAD + (row & 3)).astype(F32)
@@ -103,6 +157,7 @@
         axis=0,
     ).astype(BF16)
     meta[...] = dot_rows(values, pick[...])
+    sends = []
     lane = lax.broadcasted_iota(I32, (16, LANES), 1)
     for block in range(N_WIDE):
         rows = slice(block * CAP, (block + 1) * CAP)
@@ -119,6 +174,16 @@
             ),
         )
         send_ref[block, NT * CAP :, :] = joined.astype(BF16)
+        if block % SEND_BLOCKS == SEND_BLOCKS - 1:
+            part = pl.ds(block + 1 - SEND_BLOCKS, SEND_BLOCKS)
+            sends.append(
+                pltpu.make_async_copy(
+                    send_ref.at[part], send_hbm.at[part], send_sems.at[block // SEND_BLOCKS]
+                )
+            )
+            sends[-1].start()
+    for send in sends:
+        send.wait()
 
 
 def adjoint_kernel(recv_ref, flux_ref, meta_ref, foot_ref, rows_f, hot, weighted, total):
@@ -153,8 +218,10 @@
             flux_ref[...] = (total[...] + product).astype(BF16)
 
 
-def lat_kernel(mix_ref, flux_ref, out_ref, rows_f, columns):
-    rows_f[...] = flux_ref[...].astype(F32)
+def lat_kernel(turn_ref, mix_ref, flux_ref, out_ref, rows_f, columns):
+    turn = turn_ref[0]
+    for n in range(N_NARROW):
+        rows_f[n * CELLS : (n + 1) * CELLS, :] = flux_ref[n ^ turn].astype(F32)
     for a in range(QUAD):
         for d in range(DAY_DEV):
             columns[a * N_WIDE : (a + 1) * N_WIDE, d * LANES : (d + 1) * LANES] = rows_f[
@@ -169,8 +236,10 @@
     out_ref[...] = rows_f[...].astype(BF16)
 
 
-def day_kernel(mix_ref, flux_ref, out_ref, rows_f, columns):
-    rows_f[...] = flux_ref[...].astype(F32)
+def day_kernel(turn_ref, mix_ref, flux_ref, out_ref, rows_f, columns):
+    turn_in, turn_out = turn_ref[0], turn_ref[1]
+    for h in range(N_NARROW):
+        rows_f[h * CELLS : (h + 1) * CELLS, :] = flux_ref[h ^ turn_in].astype(F32)
     for a in range(QUAD):
         columns[:, a * LANES : (a + 1) * LANES] = rows_f[
             pl.ds(a, DAYS, stride=QUAD), :
@@ -178,7 +247,8 @@
     mixed = dot(mix_ref[...], columns[...])
     for a in range(QUAD):
         rows_f[pl.ds(a, DAYS, stride=QUAD), :] = mixed[:, a * LANES : (a + 1) * LANES]
-    out_ref[...] = rows_f[...].astype(BF16)
+    for h in range(N_NARROW):
+        out_ref[h ^ turn_out] = rows_f[h * CELLS : (h + 1) * CELLS, :].astype(BF16)
 
 
 def forward_kernel(
@@ -272,18 +342,40 @@
     dir_out[...] = residual + dot(ratio_t, direction, HIGHEST)
 
 
-def call(kernel, outs, scratch, flops, moved):
+VMEM = pl.BlockSpec(memory_space=pltpu.VMEM)
+SMEM = pl.BlockSpec(memory_space=pltpu.SMEM)
+HBM = pl.BlockSpec(memory_space=pltpu.HBM)
+
+
+def call(kernel, places, outs, scratch, flops, moved, out_places=None, limit=VMEM_LIMIT):
     return pl.pallas_call(
         kernel,
+        in_specs=places,
+        out_specs=out_places or [VMEM] * len(outs),
         out_shape=[jax.ShapeDtypeStruct(shape, dtype) for shape, dtype in outs],
-        scratch_shapes=[pltpu.VMEM(shape, dtype) for shape, dtype in scratch],
-        compiler_params=pltpu.CompilerParams(vmem_limit_bytes=VMEM_LIMIT),
+        scratch_shapes=scratch,
+        compiler_params=pltpu.CompilerParams(vmem_limit_bytes=limit),
         cost_estimate=pl.CostEstimate(flops=flops, bytes_accessed=moved, transcendentals=0),
     )
 
 
-def exchange(array, axis):
-    return lax.all_to_all(array, axis, split_axis=0, concat_axis=0, tiled=True)
+def exchange(array, axis, groups=None):
+    return lax.all_to_all(
+        array, axis, split_axis=0, concat_axis=0, tiled=True, axis_index_groups=groups
+    )
+
+
+BOTH = ("wide", "narrow")
+WINDOW_GROUPS = [
+    [((h ^ n) * QUAD + q) * N_NARROW + n for n in range(N_NARROW)]
+    for h in range(N_NARROW)
+    for q in range(QUAD)
+]
+WINDOW_GROUPS = [sorted(group) for group in WINDOW_GROUPS]
+PLANE_GROUPS = [
+    [(plane * QUAD + i % QUAD) * N_NARROW + i // QUAD for i in range(N_WIDE)]
+    for plane in range(N_NARROW)
+]
 
 
 def on_device(
@@ -299,77 +391,96 @@
     spatial_lon,
 ):
     errors = error_var.reshape(1, OBS_DEV)
+    plane = lax.axis_index("wide") >> 2
+    band = lax.axis_index("narrow")
+    vmem = lambda shape, dtype: pltpu.VMEM(shape, dtype)
     with jax.named_scope("pack"):
         packed, slot = call(
             pack_kernel,
+            [HBM] * 6 + [SMEM],
             [((N_WIDE, PAYLOAD, LANES), BF16), ((1, OBS_DEV), I32)],
             [
-                ((SLOTS, OBS_DEV), BF16),
-                ((SLOTS, NT * LANES), F32),
-                ((META, SLOTS), F32),
+                vmem((N_WIDE, PAYLOAD, LANES), BF16),
+                vmem((1, OBS_DEV), I32),
+                vmem((NT, OBS_DEV), I32),
+                vmem((OBS_DEV * NT, LANES), BF16),
+                vmem((RHS, OBS_DEV), F32),
+                vmem((RHS, OBS_DEV), F32),
+                vmem((1, OBS_DEV), F32),
+                vmem((OBS_DEV, NT * LANES), BF16),
+                vmem((SLOTS, OBS_DEV), BF16),
+                vmem((SLOTS, NT * LANES), F32),
+                vmem((META, SLOTS), F32),
+                pltpu.SemaphoreType.DMA((6,)),
+                pltpu.SemaphoreType.DMA((N_WIDE // SEND_BLOCKS,)),
             ],
             2 * SLOTS * OBS_DEV * NT * LANES,
             2 * SLOTS * OBS_DEV,
+            [HBM, VMEM],
+            VMEM_WHOLE,
         )(
             window.reshape(1, OBS_DEV),
             tiles.T,
-            footprint.reshape(OBS_DEV, NT * LANES),
+            footprint.reshape(OBS_DEV * NT, LANES),
             direction,
             residual,
             errors,
+            (band * QUAD).reshape(1),
         )
     with jax.named_scope("route"):
         routed = exchange(packed, "wide")
     with jax.named_scope("adjoint"):
         flux, meta, foot = call(
             adjoint_kernel,
+            [VMEM],
             [((ROWS, LANES), BF16), ((META, SLOTS), F32), ((NT, SLOTS, LANES), BF16)],
             [
-                ((NT, SLOTS, LANES), F32),
-                ((CELLS, SLOTS), BF16),
-                ((ROWS, SLOTS), BF16),
-                ((ROWS, LANES), F32),
+                vmem((NT, SLOTS, LANES), F32),
+                vmem((CELLS, SLOTS), BF16),
+                vmem((ROWS, SLOTS), BF16),
+                vmem((ROWS, LANES), F32),
             ],
             2 * ROWS * NT * SLOTS * LANES,
             4 * NT * SLOTS * LANES,
         )(routed)
     with jax.named_scope("to_rhs"):
-        by_rhs = exchange(flux.reshape(N_NARROW, CELLS, LANES), "narrow")
+        by_rhs = exchange(flux.reshape(N_NARROW, CELLS, LANES), BOTH, WINDOW_GROUPS)
     with jax.named_scope("lat_mix"):
         lat_mix = (
             spatial_lat.reshape(N_WIDE, QUAD, N_WIDE, QUAD).transpose(1, 0, 3, 2).reshape(LAT, LAT)
         )
         (spread,) = call(
             lat_kernel,
+            [SMEM, VMEM, VMEM],
             [((ROWS, LANES), BF16)],
-            [((ROWS, LANES), F32), ((LAT, DAY_DEV * LANES), BF16)],
+            [vmem((ROWS, LANES), F32), vmem((LAT, DAY_DEV * LANES), BF16)],
             2 * LAT * LAT * DAY_DEV * LANES,
             4 * ROWS * LANES,
-        )(lat_mix, by_rhs.reshape(ROWS, LANES))
+        )((plane ^ band).reshape(1), lat_mix, by_rhs)
     with jax.named_scope("to_days"):
-        by_day = exchange(spread.reshape(N_WIDE, CHUNK, LANES), "wide")
+        by_day = exchange(spread.reshape(N_WIDE, CHUNK, LANES), BOTH, PLANE_GROUPS)
     with jax.named_scope("day_mix"):
         (timed,) = call(
             day_kernel,
-            [((ROWS, LANES), BF16)],
-            [((ROWS, LANES), F32), ((DAYS, QUAD * LANES), BF16)],
+            [SMEM, VMEM, VMEM],
+            [((N_NARROW, CELLS, LANES), BF16)],
+            [vmem((ROWS, LANES), F32), vmem((DAYS, QUAD * LANES), BF16)],
             2 * DAYS * DAYS * QUAD * LANES,
             4 * ROWS * LANES,
-        )(temporal, by_day.reshape(ROWS, LANES))
+        )(jnp.stack([plane, band]), temporal, by_day.reshape(N_NARROW, CELLS, LANES))
     with jax.named_scope("to_windows"):
         by_window = exchange(timed.reshape(N_WIDE, CHUNK, LANES), "wide")
-    with jax.named_scope("to_bands"):
-        by_band = exchange(by_window.reshape(N_NARROW, CELLS, LANES), "narrow")
     with jax.named_scope("forward"):
         (modelled,) = call(
             forward_kernel,
+            [VMEM] * 7,
             [((N_WIDE, RHS, LANES), F32)],
-            [((ROWS, LANES), BF16), ((ROWS, 2 * LANES), F32), ((RHS, SLOTS), F32)],
+            [vmem((ROWS, LANES), BF16), vmem((ROWS, 2 * LANES), F32), vmem((RHS, SLOTS), F32)],
             2 * ROWS * NT * SLOTS * LANES,
             4 * NT * SLOTS * LANES,
         )(
             spatial_lon,
-            by_band.reshape(ROWS, LANES),
+            by_window.reshape(ROWS, LANES),
             foot,
             meta,
             direction,
@@ -384,8 +495,9 @@
     with jax.named_scope("image"):
         (image,) = call(
             gather_kernel,
+            [VMEM] * 4,
             [((RHS, OBS_DEV), F32)],
-            [((RHS, SLOTS), F32)],
+            [vmem((RHS, SLOTS), F32)],
             2 * 24 * SLOTS * OBS_DEV,
             4 * SLOTS * RHS,
         )(home, slot, direction, errors)
@@ -393,6 +505,7 @@
         return tuple(
             call(
                 update_kernel,
+                [VMEM] * 5,
                 [((RHS, OBS_DEV), F32)] * 3,
                 [],
                 2 * 18 * 8 * 8 * OBS_DEV,
@@ -402,7 +515,7 @@
 
 
 def solution(mesh):
-    both = ("wide", "narrow")
+    both = BOTH
     in_specs = (
         P(None, both),
         P(None, both),

time: 151 us -> 145 us (0.960)
  blocking collectives: 107 us -> 77.8 us
  waiting for transfers between devices: 8.22 us -> 24.9 us
  starting transfers between devices: 12.2 us -> 19 us
  local copies, waits for them, and re-layouts: 8.43 us -> 3.83 us
  Pallas kernels: 13.9 us -> 18.4 us
    all_to_all x5 -> x3, blocking collectives: 107 us -> 77.8 us  [exchange(): lax.all_to_all(array, axis, split_axis=0, concat_axis=0, tiled=True, axis...]
    all_to_all x2 -> x3, waiting for transfers between devices: 8.22 us -> 24.9 us  [exchange(): lax.all_to_all(array, axis, split_axis=0, concat_axis=0, tiled=True, axis...]
    all_to_all x2 -> x3, starting transfers between devices: 12.2 us -> 19 us  [exchange(): lax.all_to_all(array, axis, split_axis=0, concat_axis=0, tiled=True, axis...]
    unnamed x25 -> x16, local copies, waits for them, and re-layouts: 4.65 us -> 0.04 us
    pallas_call x7, Pallas kernels: 13.9 us -> 18.4 us  [the longest x1 4.77 us: on_device(): call(pack_kernel, [HBM] * 6 + [SMEM], [((N_WIDE, PAYLOAD, LANES), BF16),...]
  transfers between devices with their start and end apart: 2 -> 3, of which waited for: 2 -> 3; matrix products, arithmetic and copies ran while one was open for 2% -> 2% of each run, Pallas kernels for 0% -> 0%
where the time goes in v2:
time: 145 us
  blocking collectives  77.8 us (54%)
  waiting for transfers between devices  24.9 us (17%)
  starting transfers between devices  19 us (13%)
  Pallas kernels  18.4 us (13%)
  local copies, waits for them, and re-layouts  3.83 us (3%)
    all_to_all x3, blocking collectives, exchange(): lax.all_to_all(array, axis, split_axis=0, concat_axis=0, tiled=True, axis...  77.8 us
    all_to_all x3, waiting for transfers between devices, exchange(): lax.all_to_all(array, axis, split_axis=0, concat_axis=0, tiled=True, axis...  24.9 us
    all_to_all x3, starting transfers between devices, exchange(): lax.all_to_all(array, axis, split_axis=0, concat_axis=0, tiled=True, axis...  19 us
    pallas_call x1, Pallas kernels, on_device(): call(pack_kernel, [HBM] * 6 + [SMEM], [((N_WIDE, PAYLOAD, LANES), BF16),...  4.77 us
    pallas_call x1, Pallas kernels, on_device(): call(adjoint_kernel, [VMEM], [((ROWS, LANES), BF16), ((META, SLOTS), F32)...  4.4 us
    pallas_call x1, Pallas kernels, on_device(): call(forward_kernel, [VMEM] * 7, [((N_WIDE, RHS, LANES), F32)], [vmem((RO...  4.23 us
  transfers between devices with their start and end apart: 3, of which 3 were waited for; matrix products, arithmetic and copies ran while one was open for 2% of the time, Pallas kernels for 0%

profile of v2, /device:TPU:1, one launch (start us, length us, event | category | flops | bytes accessed | tf_op | source)
XLA Modules:
  0.0 144.9 jit_solution(5072853194977604979)
XLA Ops:
  0.6 4.8 %pack.1 = (bf16[32,176,128]{2,1,0:T(8,128)(2,1)}, s32[1,512]{1,0:T(1,128)}) custom-call(s32[1,512]{1,0:T(1,128)} %bitcast.23, s32[4,512]{1,0:T(4,128)} %bitcast.22, bf16[2048,128]{1,0:T(8,128)(2,1)} %bitcast.21, f32[8,512]{1,0:T(8,128)} %dir_ref.5, f32[8,512]{1,0:T(8,128)} %res_ref.3, f32[1,512]{1,0:T(1,128)} %bitcast.17, s32[1]{0:T(128)} %bitcast.8.turn_ref), custom_call_target="tpu_custom_call" | custom-call | flops 671088640 | bytes 1310720 | tf_op jit(solution)/shard_map/pack/pallas_call | solution.py:398
  5.4 48.3 %all_to_all.30.recv_ref = bf16[32,176,128]{2,1,0:T(8,128)(2,1)S(1)} all-to-all(bf16[32,176,128]{2,1,0:T(8,128)(2,1)} %get-tuple-element.8), channel_id=1, replica_groups=mesh['wide'=32,'narrow'=8] {'wide'}, dimensions={0} | all-to-all | bytes 2883584 | tf_op jit(solution)/shard_map/route/all_to_all | solution.py:363
  53.7 4.4 %adjoint.1 = (bf16[1280,128]{1,0:T(8,128)(2,1)}, f32[48,1280]{1,0:T(8,128)S(1)}, bf16[4,1280,128]{2,1,0:T(8,128)(2,1)S(1)}) custom-call(bf16[32,176,128]{2,1,0:T(8,128)(2,1)S(1)} %all_to_all.30.recv_ref), custom_call_target="tpu_custom_call" | custom-call | flops 1677721600 | bytes 2621440 | tf_op jit(solution)/shard_map/adjoint/pallas_call | solution.py:433
  58.1 7.2 %all-to-all-start.1 = ((bf16[8,160,128]{2,1,0:T(8,128)(2,1)}), bf16[8,160,128]{2,1,0:T(8,128)(2,1)S(1)}, u32[]{:S(2)}, u32[]{:S(2)}) async-start(bf16[8,160,128]{2,1,0:T(8,128)(2,1)} %bitcast.9), calls=%async_computation.1 | async-start | bytes 655360 | tf_op jit(solution)/shard_map/to_rhs/all_to_all | solution.py:363
  65.3 0.0 copy-done.7
  65.3 2.2 %reshape.44 = bf16[32,4,32,4]{3,2,1,0:T(8,128)(2,1)S(1)} reshape(bf16[128,128]{1,0:T(8,128)(2,1)S(1)} %copy-done.7) | data formatting | bytes 65536 | tf_op jit(solution)/shard_map/lat_mix/reshape | solution.py:450
  67.5 0.0 copy-start
  67.5 0.8 copy.14
  68.4 0.1 reshape.45.mix_ref
  68.5 11.2 %all-to-all-done.1.flux_ref = bf16[8,160,128]{2,1,0:T(8,128)(2,1)S(1)} async-done(((bf16[8,160,128]{2,1,0:T(8,128)(2,1)}), bf16[8,160,128]{2,1,0:T(8,128)(2,1)S(1)}, u32[]{:S(2)}, u32[]{:S(2)}) %all-to-all-start.1) | async-done | bytes 327712 | tf_op jit(solution)/shard_map/to_rhs/all_to_all | solution.py:363
  79.8 1.1 lat_mix.1
  80.9 5.8 %all-to-all-start.2 = ((bf16[32,40,128]{2,1,0:T(8,128)(2,1)}), bf16[32,40,128]{2,1,0:T(8,128)(2,1)S(1)}, u32[]{:S(2)}, u32[]{:S(2)}) async-start(bf16[32,40,128]{2,1,0:T(8,128)(2,1)} %bitcast.10), calls=%async_computation.2 | async-start | bytes 655360 | tf_op jit(solution)/shard_map/to_days/all_to_all | solution.py:363
  86.6 0.1 pad_add_fusion.turn_ref
  86.7 9.4 %all-to-all-done.2 = bf16[32,40,128]{2,1,0:T(8,128)(2,1)S(1)} async-done(((bf16[32,40,128]{2,1,0:T(8,128)(2,1)}), bf16[32,40,128]{2,1,0:T(8,128)(2,1)S(1)}, u32[]{:S(2)}, u32[]{:S(2)}) %all-to-all-start.2) | async-done | bytes 327712 | tf_op jit(solution)/shard_map/to_days/all_to_all | solution.py:363
  96.1 0.0 copy-done
  96.1 1.0 day_mix.1
  97.1 15.8 %all_to_all.31 = bf16[32,40,128]{2,1,0:T(8,128)(2,1)S(1)} all-to-all(bf16[32,40,128]{2,1,0:T(8,128)(2,1)S(1)} %bitcast.15), channel_id=1, replica_groups=mesh['wide'=32,'narrow'=8] {'wide'}, dimensions={0} | all-to-all | bytes 655360 | tf_op jit(solution)/shard_map/to_windows/all_to_all | solution.py:363
  112.9 0.0 copy-done.1
  112.9 0.0 copy-done.2
  112.9 0.0 copy-done.4
  112.9 0.0 copy-done.6
  112.9 0.0 copy-start.5
  112.9 0.0 copy-start.3
  112.9 4.2 %forward.1 = f32[32,8,128]{2,1,0:T(8,128)S(1)} custom-call(bf16[128,128]{1,0:T(8,128)(2,1)S(1)} %copy-done.6, bf16[1280,128]{1,0:T(8,128)(2,1)S(1)} %bitcast.16, bf16[4,1280,128]{2,1,0:T(8,128)(2,1)S(1)} %get-tuple-element.10.foot_ref, f32[48,1280]{1,0:T(8,128)S(1)} %get-tuple-element.11.meta_ref, f32[8,512]{1,0:T(8,128)S(1)} %copy-done.1, ...), custom_call_target="tpu_custom_call" | custom-call | flops 1677721600 | bytes 2621440 | tf_op jit(solution)/shard_map/forward/pallas_call | solution.py:474
  117.2 13.8 %all_to_all.32.home_ref = f32[32,8,128]{2,1,0:T(8,128)S(1)} all-to-all(f32[32,8,128]{2,1,0:T(8,128)S(1)} %forward.1), channel_id=1, replica_groups=mesh['wide'=32,'narrow'=8] {'wide'}, dimensions={0} | all-to-all | bytes 262144 | tf_op jit(solution)/shard_map/home/all_to_all | solution.py:363
  131.0 0.6 broadcast_in_dim.2
  131.6 6.1 %all-to-all-start.5 = ((f32[8,8,128]{2,1,0:T(8,128)}), f32[8,8,128]{2,1,0:T(8,128)S(1)}, u32[]{:S(2)}, u32[]{:S(2)}) async-start(f32[8,8,128]{2,1,0:T(8,128)} %broadcast_in_dim.2), calls=%async_computation.5 | async-start | bytes 65536 | tf_op jit(solution)/shard_map/gram_sum/all_to_all | solution.py:363
  137.7 0.0 copy-done.5
  137.7 0.4 image.1.image_ref
  138.1 4.3 %all-to-all-done.5.gram_ref = f32[8,8,128]{2,1,0:T(8,128)S(1)} async-done(((f32[8,8,128]{2,1,0:T(8,128)}), f32[8,8,128]{2,1,0:T(8,128)S(1)}, u32[]{:S(2)}, u32[]{:S(2)}) %all-to-all-start.5) | async-done | bytes 32800 | tf_op jit(solution)/shard_map/gram_sum/all_to_all | solution.py:363
  142.4 0.0 copy-done.3
  142.4 2.4 %update.1 = (f32[8,512]{1,0:T(8,128)}, f32[8,512]{1,0:T(8,128)}, f32[8,512]{1,0:T(8,128)}) custom-call(f32[8,8,128]{2,1,0:T(8,128)S(1)} %all-to-all-done.5.gram_ref, f32[8,512]{1,0:T(8,128)S(1)} %copy-done.3, f32[8,512]{1,0:T(8,128)S(1)} %copy-done.2, f32[8,512]{1,0:T(8,128)S(1)} %copy-done.1, f32[8,512]{1,0:T(8,128)S(1)} %image.1.image_ref), custom_call_target="tpu_custom_call" | custom-call | flops 1179648 | bytes 114688 | tf_op jit(solution)/shard_map/update/pallas_call | solution.py:506
  (6 shorter events, 0.0 us)
Async XLA Ops:
  53.7 11.6 %copy-start.7 = (bf16[128,128]{1,0:T(8,128)(2,1)S(1)}, bf16[128,128]{1,0:T(8,128)(2,1)}, u32[]{:S(2)}) copy-start(bf16[128,128]{1,0:T(8,128)(2,1)} %param.18) | copy-start | bytes 98308
  58.1 21.6 %all-to-all-start.1 = ((bf16[8,160,128]{2,1,0:T(8,128)(2,1)}), bf16[8,160,128]{2,1,0:T(8,128)(2,1)S(1)}, u32[]{:S(2)}, u32[]{:S(2)}) async-start(bf16[8,160,128]{2,1,0:T(8,128)(2,1)} %bitcast.9), calls=%async_computation.1 | async-start | bytes 655360 | tf_op jit(solution)/shard_map/to_rhs/all_to_all | solution.py:363
  67.5 28.6 %copy-start = (bf16[320,320]{1,0:T(8,128)(2,1)S(1)}, bf16[320,320]{1,0:T(8,128)(2,1)}, u32[]{:S(2)}) copy-start(bf16[320,320]{1,0:T(8,128)(2,1)} %mix_ref.1) | copy-start | bytes 614404
  79.7 33.1 %copy-start.1 = (f32[8,512]{1,0:T(8,128)S(1)}, f32[8,512]{1,0:T(8,128)}, u32[]{:S(2)}) copy-start(f32[8,512]{1,0:T(8,128)} %dir_ref.5) | copy-start | bytes 49156
  79.7 33.1 %copy-start.2 = (f32[8,512]{1,0:T(8,128)S(1)}, f32[8,512]{1,0:T(8,128)}, u32[]{:S(2)}) copy-start(f32[8,512]{1,0:T(8,128)} %res_ref.3) | copy-start | bytes 49156
  79.7 33.1 %copy-start.4 = (f32[512]{0:T(512)S(1)}, f32[512]{0:T(512)}, u32[]{:S(2)}) copy-start(f32[512]{0:T(512)} %param.13) | copy-start | bytes 6148
  79.7 33.1 %copy-start.6 = (bf16[128,128]{1,0:T(8,128)(2,1)S(1)}, bf16[128,128]{1,0:T(8,128)(2,1)}, u32[]{:S(2)}) copy-start(bf16[128,128]{1,0:T(8,128)(2,1)} %lon_ref.1) | copy-start | bytes 98308
  80.9 15.2 %all-to-all-start.2 = ((bf16[32,40,128]{2,1,0:T(8,128)(2,1)}), bf16[32,40,128]{2,1,0:T(8,128)(2,1)S(1)}, u32[]{:S(2)}, u32[]{:S(2)}) async-start(bf16[32,40,128]{2,1,0:T(8,128)(2,1)} %bitcast.10), calls=%async_computation.2 | async-start | bytes 655360 | tf_op jit(solution)/shard_map/to_days/all_to_all | solution.py:363
  112.9 24.8 %copy-start.5 = (s32[1,512]{1,0:T(1,128)S(1)}, s32[1,512]{1,0:T(1,128)}, u32[]{:S(2)}) copy-start(s32[1,512]{1,0:T(1,128)} %get-tuple-element.12.slot_ref) | copy-start | bytes 6148
  112.9 29.5 %copy-start.3 = (f32[8,512]{1,0:T(8,128)S(1)}, f32[8,512]{1,0:T(8,128)}, u32[]{:S(2)}) copy-start(f32[8,512]{1,0:T(8,128)} %sol_ref.1) | copy-start | bytes 49156
  131.6 10.9 %all-to-all-start.5 = ((f32[8,8,128]{2,1,0:T(8,128)}), f32[8,8,128]{2,1,0:T(8,128)S(1)}, u32[]{:S(2)}, u32[]{:S(2)}) async-start(f32[8,8,128]{2,1,0:T(8,128)} %broadcast_in_dim.2), calls=%async_computation.5 | async-start | bytes 65536 | tf_op jit(solution)/shard_map/gram_sum/all_to_all | solution.py:363

commit v3 on v2

--- a/solution.py
+++ b/solution.py
@@ -21,6 +21,7 @@
 DAYS = N_WIDE * DAY_DEV
 LAT = 128
 CELLS = 160
+HALF = CELLS // 2
 QUAD = 4
 CHUNK = DAY_DEV * QUAD
 ROWS = RHS * CELLS
@@ -78,7 +79,6 @@
     dir_hbm,
     res_hbm,
     err_hbm,
-    turn_ref,
     send_hbm,
     slot_ref,
     send_ref,
@@ -115,7 +115,7 @@
     )
     earlier = jnp.where(earlier, 1.0, 0.0).astype(BF16)
     copies[0].wait()
-    owner = window_ref[...] ^ turn_ref[0]
+    owner = window_ref[...] ^ (lax.axis_index("narrow") * QUAD)
     named = lax.broadcasted_iota(I32, (N_WIDE, OBS_DEV), 0) == owner
     named_f = jnp.where(named, 1.0, 0.0)
     before = dot(named_f.astype(BF16), earlier)
@@ -186,7 +186,13 @@
         send.wait()
 
 
-def adjoint_kernel(recv_ref, flux_ref, meta_ref, foot_ref, rows_f, hot, weighted, total):
+def half_cell(ids):
+    return jnp.where(ids >= HALF, ids - HALF, ids).astype(I32)
+
+
+def adjoint_kernel(
+    recv_ref, flux_ref, meta_ref, foot_ref, rows_f, sides, hot, weighted, total
+):
     meta_ref[...] = jnp.zeros((META, SLOTS), F32)
     lane = lax.broadcasted_iota(I32, (16, LANES), 1)
     for block in range(N_WIDE):
@@ -197,29 +203,43 @@
         for g in range(3):
             piece = joined if g == 0 else pltpu.roll(joined, LANES - g * CAP, 1)
             add_lanes(meta_ref, 16 * g, 16, block, jnp.where(lane < CAP, piece, 0.0))
-    cells = lax.broadcasted_iota(I32, (CELLS, SLOTS), 0)
+    upper = jnp.where(meta_ref[8:16, :] >= HALF, 1.0, 0.0).astype(BF16)
+    spread_to = lax.broadcasted_iota(I32, (8, NT * LANES), 1) // LANES
+    spread_to = spread_to == lax.broadcasted_iota(I32, (8, NT * LANES), 0)
+    sides[...] = lax.dot_general(
+        upper,
+        jnp.where(spread_to, 1.0, 0.0).astype(BF16),
+        (((0,), (0,)), ((), ())),
+        preferred_element_type=F32,
+    )
+    cells = lax.broadcasted_iota(I32, (HALF, SLOTS), 0)
     for k in range(NT):
-        foot = rows_f[k].astype(BF16)
-        foot_ref[k] = foot
-        ids = meta_ref[8 + k : 9 + k, :].astype(I32)
-        hot[...] = jnp.where(cells == ids, 1.0, 0.0).astype(BF16)
+        is_upper = sides[:, k * LANES : (k + 1) * LANES] > 0.5
+        foot = rows_f[k]
+        foot_ref[k, :, :LANES] = jnp.where(is_upper, 0.0, foot).astype(BF16)
+        foot_ref[k, :, LANES:] = jnp.where(is_upper, foot, 0.0).astype(BF16)
+        hot[...] = jnp.where(cells == half_cell(meta_ref[8 + k : 9 + k, :]), 1.0, 0.0).astype(BF16)
         for r in range(RHS):
             row = jnp.broadcast_to(meta_ref[r : r + 1, :], (16, SLOTS)).astype(BF16)
-            for t in range(CELLS // 16):
-                weighted[r * CELLS + t * 16 : r * CELLS + (t + 1) * 16, :] = (
+            for t in range(HALF // 16):
+                weighted[r * HALF + t * 16 : r * HALF + (t + 1) * 16, :] = (
                     hot[t * 16 : (t + 1) * 16, :] * row
                 )
-        product = dot(weighted[...], foot)
+        product = dot(weighted[...], foot_ref[k])
         if k == 0:
             total[...] = product
-        elif k < NT - 1:
+        else:
             total[...] += product
-        else:
-            flux_ref[...] = (total[...] + product).astype(BF16)
-
-
-def lat_kernel(turn_ref, mix_ref, flux_ref, out_ref, rows_f, columns):
-    turn = turn_ref[0]
+    for r in range(RHS):
+        for side in range(2):
+            at = r * CELLS + side * HALF
+            flux_ref[at : at + HALF, :] = total[
+                r * HALF : (r + 1) * HALF, side * LANES : (side + 1) * LANES
+            ].astype(BF16)
+
+
+def lat_kernel(mix_ref, flux_ref, out_ref, rows_f, columns):
+    turn = (lax.axis_index("wide") >> 2) ^ lax.axis_index("narrow")
     for n in range(N_NARROW):
         rows_f[n * CELLS : (n + 1) * CELLS, :] = flux_ref[n ^ turn].astype(F32)
     for a in range(QUAD):
@@ -236,8 +256,8 @@
     out_ref[...] = rows_f[...].astype(BF16)
 
 
-def day_kernel(turn_ref, mix_ref, flux_ref, out_ref, rows_f, columns):
-    turn_in, turn_out = turn_ref[0], turn_ref[1]
+def day_kernel(mix_ref, flux_ref, out_ref, rows_f, columns):
+    turn_in, turn_out = lax.axis_index("wide") >> 2, lax.axis_index("narrow")
     for h in range(N_NARROW):
         rows_f[h * CELLS : (h + 1) * CELLS, :] = flux_ref[h ^ turn_in].astype(F32)
     for a in range(QUAD):
@@ -254,17 +274,23 @@
 def forward_kernel(
     lon_ref, spread_ref, foot_ref, meta_ref, dir_ref, res_ref, err_ref, send_ref, table, picked, model
 ):
-    table[...] = dot_rows(spread_ref[...], lon_ref[...]).astype(BF16)
+    smoothed = dot_rows(spread_ref[...], lon_ref[...])
+    for r in range(RHS):
+        for side in range(2):
+            at = r * CELLS + side * HALF
+            table[r * HALF : (r + 1) * HALF, side * LANES : (side + 1) * LANES] = smoothed[
+                at : at + HALF, :
+            ].astype(BF16)
     width = 2 * LANES
-    cells = lax.broadcasted_iota(I32, (CELLS, width), 0)
+    cells = lax.broadcasted_iota(I32, (HALF, width), 0)
     for tile in range(SLOTS // width):
         at = slice(tile * width, (tile + 1) * width)
         sums = [jnp.zeros((1, width), F32)] * RHS
         for k in range(NT):
-            picked[...] = dot_rows(table[...], foot_ref[k, at, :])
-            mask = cells == meta_ref[8 + k : 9 + k, at].astype(I32)
+            picked[k % 2] = dot_rows(table[...], foot_ref[k, at, :])
+            mask = cells == half_cell(meta_ref[8 + k : 9 + k, at])
             for r in range(RHS):
-                rows = picked[r * CELLS : (r + 1) * CELLS, :]
+                rows = picked[k % 2, r * HALF : (r + 1) * HALF, :]
                 sums[r] = sums[r] + jnp.sum(jnp.where(mask, rows, 0.0), axis=0, keepdims=True)
         model[:, at] = jnp.concatenate(sums, axis=0)
     held_dir = meta_ref[0:8, :] + meta_ref[16:24, :]
@@ -306,6 +332,14 @@
     image_ref[...] = placed[0:8] + placed[8:16] + placed[16:24] + err_ref[...] * dir_ref[...]
 
 
+def sum_kernel(home_ref, out_ref):
+    total = home_ref[0]
+    for block in range(1, N_WIDE):
+        total = total + home_ref[block]
+    for n in range(N_NARROW):
+        out_ref[n] = total
+
+
 def inverses(matrices):
     row = lax.broadcasted_iota(I32, (RHS, RHS), 0)
     column = lax.broadcasted_iota(I32, (RHS, RHS), 1)
@@ -343,7 +377,6 @@
 
 
 VMEM = pl.BlockSpec(memory_space=pltpu.VMEM)
-SMEM = pl.BlockSpec(memory_space=pltpu.SMEM)
 HBM = pl.BlockSpec(memory_space=pltpu.HBM)
 
 
@@ -391,13 +424,11 @@
     spatial_lon,
 ):
     errors = error_var.reshape(1, OBS_DEV)
-    plane = lax.axis_index("wide") >> 2
-    band = lax.axis_index("narrow")
     vmem = lambda shape, dtype: pltpu.VMEM(shape, dtype)
     with jax.named_scope("pack"):
         packed, slot = call(
             pack_kernel,
-            [HBM] * 6 + [SMEM],
+            [HBM] * 6,
             [((N_WIDE, PAYLOAD, LANES), BF16), ((1, OBS_DEV), I32)],
             [
                 vmem((N_WIDE, PAYLOAD, LANES), BF16),
@@ -425,7 +456,6 @@
             direction,
             residual,
             errors,
-            (band * QUAD).reshape(1),
         )
     with jax.named_scope("route"):
         routed = exchange(packed, "wide")
@@ -433,12 +463,13 @@
         flux, meta, foot = call(
             adjoint_kernel,
             [VMEM],
-            [((ROWS, LANES), BF16), ((META, SLOTS), F32), ((NT, SLOTS, LANES), BF16)],
+            [((ROWS, LANES), BF16), ((META, SLOTS), F32), ((NT, SLOTS, 2 * LANES), BF16)],
             [
                 vmem((NT, SLOTS, LANES), F32),
-                vmem((CELLS, SLOTS), BF16),
-                vmem((ROWS, SLOTS), BF16),
-                vmem((ROWS, LANES), F32),
+                vmem((SLOTS, NT * LANES), F32),
+                vmem((HALF, SLOTS), BF16),
+                vmem((ROWS // 2, SLOTS), BF16),
+                vmem((ROWS // 2, 2 * LANES), F32),
             ],
             2 * ROWS * NT * SLOTS * LANES,
             4 * NT * SLOTS * LANES,
@@ -451,23 +482,23 @@
         )
         (spread,) = call(
             lat_kernel,
-            [SMEM, VMEM, VMEM],
+            [VMEM, VMEM],
             [((ROWS, LANES), BF16)],
             [vmem((ROWS, LANES), F32), vmem((LAT, DAY_DEV * LANES), BF16)],
             2 * LAT * LAT * DAY_DEV * LANES,
             4 * ROWS * LANES,
-        )((plane ^ band).reshape(1), lat_mix, by_rhs)
+        )(lat_mix, by_rhs)
     with jax.named_scope("to_days"):
         by_day = exchange(spread.reshape(N_WIDE, CHUNK, LANES), BOTH, PLANE_GROUPS)
     with jax.named_scope("day_mix"):
         (timed,) = call(
             day_kernel,
-            [SMEM, VMEM, VMEM],
+            [VMEM, VMEM],
             [((N_NARROW, CELLS, LANES), BF16)],
             [vmem((ROWS, LANES), F32), vmem((DAYS, QUAD * LANES), BF16)],
             2 * DAYS * DAYS * QUAD * LANES,
             4 * ROWS * LANES,
-        )(jnp.stack([plane, band]), temporal, by_day.reshape(N_NARROW, CELLS, LANES))
+        )(temporal, by_day.reshape(N_NARROW, CELLS, LANES))
     with jax.named_scope("to_windows"):
         by_window = exchange(timed.reshape(N_WIDE, CHUNK, LANES), "wide")
     with jax.named_scope("forward"):
@@ -475,7 +506,11 @@
             forward_kernel,
             [VMEM] * 7,
             [((N_WIDE, RHS, LANES), F32)],
-            [vmem((ROWS, LANES), BF16), vmem((ROWS, 2 * LANES), F32), vmem((RHS, SLOTS), F32)],
+            [
+                vmem((ROWS // 2, 2 * LANES), BF16),
+                vmem((2, ROWS // 2, 2 * LANES), F32),
+                vmem((RHS, SLOTS), F32),
+            ],
             2 * ROWS * NT * SLOTS * LANES,
             4 * NT * SLOTS * LANES,
         )(
@@ -490,7 +525,14 @@
     with jax.named_scope("home"):
         home = exchange(modelled, "wide")
     with jax.named_scope("gram_sum"):
-        partial = jnp.broadcast_to(home.sum(axis=0)[None], (N_NARROW, RHS, LANES))
+        (partial,) = call(
+            sum_kernel,
+            [VMEM],
+            [((N_NARROW, RHS, LANES), F32)],
+            [],
+            N_WIDE * RHS * LANES,
+            4 * N_WIDE * RHS * LANES,
+        )(home)
         grams = exchange(partial, "narrow")
     with jax.named_scope("image"):
         (image,) = call(

time: 145 us -> 141 us (0.972)
  blocking collectives: 77.8 us -> 92.9 us
  waiting for transfers between devices: 24.9 us -> 11.7 us
  starting transfers between devices: 19 us -> 13.3 us
  local copies, waits for them, and re-layouts: 3.83 us -> 7.04 us
  Pallas kernels: 18.4 us -> 15.3 us
    all_to_all x3 -> x4, blocking collectives: 77.8 us -> 92.9 us  [exchange(): lax.all_to_all(array, axis, split_axis=0, concat_axis=0, tiled=True, axis...]
    all_to_all x3 -> x2, waiting for transfers between devices: 24.9 us -> 11.7 us  [exchange(): lax.all_to_all(array, axis, split_axis=0, concat_axis=0, tiled=True, axis...]
    all_to_all x3 -> x2, starting transfers between devices: 19 us -> 13.3 us  [exchange(): lax.all_to_all(array, axis, split_axis=0, concat_axis=0, tiled=True, axis...]
    transpose x1, local copies, waits for them, and re-layouts: 0.83 us -> 2.74 us  [on_device(): spatial_lat.reshape(N_WIDE, QUAD, N_WIDE, QUAD).transpose(1, 0, 3, 2)]
    reshape x2, local copies, waits for them, and re-layouts: 2.35 us -> 4.25 us  [on_device(): spatial_lat.reshape(N_WIDE, QUAD, N_WIDE, QUAD).transpose(1, 0, 3, 2)]
    pallas_call x1, Pallas kernels: 4.23 us -> 2.53 us  [on_device(): call(forward_kernel, [VMEM] * 7, [((N_WIDE, RHS, LANES), F32)], [vmem((RO...]
    pallas_call x3 -> x4, Pallas kernels: 6.89 us -> 6.26 us  [the longest x1 4.77 us: on_device(): call(pack_kernel, [HBM] * 6, [((N_WIDE, PAYLOAD, LANES), BF16), ((1, OBS_...]
  transfers between devices with their start and end apart: 3 -> 2, of which waited for: 3 -> 2; matrix products, arithmetic and copies ran while one was open for 2% -> 5% of each run, Pallas kernels for 0% -> 0%
where the time goes in v3:
time: 141 us
  blocking collectives  92.9 us (66%)
  Pallas kernels  15.3 us (11%)
  starting transfers between devices  13.3 us (9%)
  waiting for transfers between devices  11.7 us (8%)
  local copies, waits for them, and re-layouts  7.04 us (5%)
    all_to_all x4, blocking collectives, exchange(): lax.all_to_all(array, axis, split_axis=0, concat_axis=0, tiled=True, axis...  92.9 us
    all_to_all x2, starting transfers between devices, exchange(): lax.all_to_all(array, axis, split_axis=0, concat_axis=0, tiled=True, axis...  13.3 us
    all_to_all x2, waiting for transfers between devices, exchange(): lax.all_to_all(array, axis, split_axis=0, concat_axis=0, tiled=True, axis...  11.7 us
    pallas_call x1, Pallas kernels, on_device(): call(pack_kernel, [HBM] * 6, [((N_WIDE, PAYLOAD, LANES), BF16), ((1, OBS_...  4.77 us
    reshape x2, local copies, waits for them, and re-layouts, on_device(): spatial_lat.reshape(N_WIDE, QUAD, N_WIDE, QUAD).transpose(1, 0, 3, 2)  4.25 us
    pallas_call x1, Pallas kernels, on_device(): call(adjoint_kernel, [VMEM], [((ROWS, LANES), BF16), ((META, SLOTS), F32)...  3.67 us
  transfers between devices with their start and end apart: 2, of which 2 were waited for; matrix products, arithmetic and copies ran while one was open for 5% of the time, Pallas kernels for 0%

profile of v3, /device:TPU:1, one launch (start us, length us, event | category | flops | bytes accessed | tf_op | source)
XLA Modules:
  0.0 140.9 jit_solution(9516891893263143019)
XLA Ops:
  0.6 4.8 %pack.1 = (bf16[32,176,128]{2,1,0:T(8,128)(2,1)}, s32[1,512]{1,0:T(1,128)}) custom-call(s32[1,512]{1,0:T(1,128)} %bitcast.20, s32[4,512]{1,0:T(4,128)} %bitcast.19, bf16[2048,128]{1,0:T(8,128)(2,1)} %bitcast.18, f32[8,512]{1,0:T(8,128)} %dir_ref.5, f32[8,512]{1,0:T(8,128)} %res_ref.3, f32[1,512]{1,0:T(1,128)} %bitcast.14), custom_call_target="tpu_custom_call" | custom-call | flops 671088640 | bytes 1310720 | tf_op jit(solution)/shard_map/pack/pallas_call | solution.py:429
  5.4 48.3 %all_to_all.30.recv_ref = bf16[32,176,128]{2,1,0:T(8,128)(2,1)S(1)} all-to-all(bf16[32,176,128]{2,1,0:T(8,128)(2,1)} %get-tuple-element.8), channel_id=1, replica_groups=mesh['wide'=32,'narrow'=8] {'wide'}, dimensions={0} | all-to-all | bytes 2883584 | tf_op jit(solution)/shard_map/route/all_to_all | solution.py:396
  53.7 3.7 %adjoint.1 = (bf16[1280,128]{1,0:T(8,128)(2,1)}, f32[48,1280]{1,0:T(8,128)S(1)}, bf16[4,1280,256]{2,1,0:T(8,128)(2,1)S(1)}) custom-call(bf16[32,176,128]{2,1,0:T(8,128)(2,1)S(1)} %all_to_all.30.recv_ref), custom_call_target="tpu_custom_call" | custom-call | flops 1677721600 | bytes 2621440 | tf_op jit(solution)/shard_map/adjoint/pallas_call | solution.py:463
  57.4 7.2 %all-to-all-start.1 = ((bf16[8,160,128]{2,1,0:T(8,128)(2,1)}), bf16[8,160,128]{2,1,0:T(8,128)(2,1)S(1)}, u32[]{:S(2)}, u32[]{:S(2)}) async-start(bf16[8,160,128]{2,1,0:T(8,128)(2,1)} %bitcast.5), calls=%async_computation.1 | async-start | bytes 655360 | tf_op jit(solution)/shard_map/to_rhs/all_to_all | solution.py:396
  64.6 0.0 copy-done.7
  64.6 3.2 %reshape.36 = bf16[32,4,32,4]{3,2,1,0:T(8,128)(2,1)} reshape(bf16[128,128]{1,0:T(8,128)(2,1)S(1)} %copy-done.7) | data formatting | bytes 65536 | tf_op jit(solution)/shard_map/lat_mix/reshape | solution.py:481
  67.8 2.7 %copy.14 = bf16[4,32,4,32]{3,2,1,0:T(4,128)(2,1)} copy(bf16[4,32,4,32]{2,3,0,1:T(8,128)(2,1)} %bitcast.17) | data formatting | bytes 65536 | tf_op jit(solution)/shard_map/lat_mix/transpose | solution.py:481
  70.5 1.0 reshape.37.mix_ref
  71.6 0.0 copy-start.1
  71.6 0.0 copy-start.2
  71.6 0.0 copy-start.4
  71.6 0.0 copy-start.6
  71.6 7.4 %all-to-all-done.1.flux_ref = bf16[8,160,128]{2,1,0:T(8,128)(2,1)S(1)} async-done(((bf16[8,160,128]{2,1,0:T(8,128)(2,1)}), bf16[8,160,128]{2,1,0:T(8,128)(2,1)S(1)}, u32[]{:S(2)}, u32[]{:S(2)}) %all-to-all-start.1) | async-done | bytes 327712 | tf_op jit(solution)/shard_map/to_rhs/all_to_all | solution.py:396
  79.0 0.4 lat_mix.1
  79.4 15.0 %all_to_all.31 = bf16[32,40,128]{2,1,0:T(8,128)(2,1)S(1)} all-to-all(bf16[32,40,128]{2,1,0:T(8,128)(2,1)S(1)} %bitcast.12), channel_id=1, replica_groups={{0,8,16,24,1,9,17,25,2,10,18,26,3,11,19,27,4,12,20,28,5,13,21,29,6,14,2..., dimensions={0} | all-to-all | bytes 655360 | tf_op jit(solution)/shard_map/to_days/all_to_all | solution.py:396
  94.4 0.0 copy-done
  94.4 0.5 day_mix.1
  94.9 15.8 %all_to_all.32 = bf16[32,40,128]{2,1,0:T(8,128)(2,1)S(1)} all-to-all(bf16[32,40,128]{2,1,0:T(8,128)(2,1)S(1)} %bitcast.11), channel_id=1, replica_groups=mesh['wide'=32,'narrow'=8] {'wide'}, dimensions={0} | all-to-all | bytes 655360 | tf_op jit(solution)/shard_map/to_windows/all_to_all | solution.py:396
  110.7 0.0 copy-done.1
  110.7 0.0 copy-done.2
  110.7 0.0 copy-done.4
  110.7 0.0 copy-done.6
  110.7 0.0 copy-start.5
  110.7 0.0 copy-start.3
  110.7 2.5 %forward.1 = f32[32,8,128]{2,1,0:T(8,128)S(1)} custom-call(bf16[128,128]{1,0:T(8,128)(2,1)S(1)} %copy-done.6, bf16[1280,128]{1,0:T(8,128)(2,1)S(1)} %bitcast.13, bf16[4,1280,256]{2,1,0:T(8,128)(2,1)S(1)} %get-tuple-element.10.foot_ref, f32[48,1280]{1,0:T(8,128)S(1)} %get-tuple-element.11.meta_ref, f32[8,512]{1,0:T(8,128)S(1)} %copy-done.1, ...), custom_call_target="tpu_custom_call" | custom-call | flops 1677721600 | bytes 2621440 | tf_op jit(solution)/shard_map/forward/pallas_call | solution.py:505
  113.2 13.8 %all_to_all.33.home_ref = f32[32,8,128]{2,1,0:T(8,128)S(1)} all-to-all(f32[32,8,128]{2,1,0:T(8,128)S(1)} %forward.1), channel_id=1, replica_groups=mesh['wide'=32,'narrow'=8] {'wide'}, dimensions={0} | all-to-all | bytes 262144 | tf_op jit(solution)/shard_map/home/all_to_all | solution.py:396
  127.0 0.6 gram_sum.1
  127.7 6.1 %all-to-all-start.5 = ((f32[8,8,128]{2,1,0:T(8,128)}), f32[8,8,128]{2,1,0:T(8,128)S(1)}, u32[]{:S(2)}, u32[]{:S(2)}) async-start(f32[8,8,128]{2,1,0:T(8,128)} %gram_sum.1), calls=%async_computation.5 | async-start | bytes 65536 | tf_op jit(solution)/shard_map/gram_sum/all_to_all | solution.py:396
  133.8 0.0 copy-done.5
  133.8 0.4 image.1.image_ref
  134.2 4.3 %all-to-all-done.5.gram_ref = f32[8,8,128]{2,1,0:T(8,128)S(1)} async-done(((f32[8,8,128]{2,1,0:T(8,128)}), f32[8,8,128]{2,1,0:T(8,128)S(1)}, u32[]{:S(2)}, u32[]{:S(2)}) %all-to-all-start.5) | async-done | bytes 32800 | tf_op jit(solution)/shard_map/gram_sum/all_to_all | solution.py:396
  138.5 2.4 %update.1 = (f32[8,512]{1,0:T(8,128)}, f32[8,512]{1,0:T(8,128)}, f32[8,512]{1,0:T(8,128)}) custom-call(f32[8,8,128]{2,1,0:T(8,128)S(1)} %all-to-all-done.5.gram_ref, f32[8,512]{1,0:T(8,128)S(1)} %copy-done.3, f32[8,512]{1,0:T(8,128)S(1)} %copy-done.2, f32[8,512]{1,0:T(8,128)S(1)} %copy-done.1, f32[8,512]{1,0:T(8,128)S(1)} %image.1.image_ref), custom_call_target="tpu_custom_call" | custom-call | flops 1179648 | bytes 114688 | tf_op jit(solution)/shard_map/update/pallas_call | solution.py:548
  (3 shorter events, 0.0 us)
Async XLA Ops:
  53.7 10.8 %copy-start.7 = (bf16[128,128]{1,0:T(8,128)(2,1)S(1)}, bf16[128,128]{1,0:T(8,128)(2,1)}, u32[]{:S(2)}) copy-start(bf16[128,128]{1,0:T(8,128)(2,1)} %param.18) | copy-start | bytes 98308
  57.4 21.6 %all-to-all-start.1 = ((bf16[8,160,128]{2,1,0:T(8,128)(2,1)}), bf16[8,160,128]{2,1,0:T(8,128)(2,1)S(1)}, u32[]{:S(2)}, u32[]{:S(2)}) async-start(bf16[8,160,128]{2,1,0:T(8,128)(2,1)} %bitcast.5), calls=%async_computation.1 | async-start | bytes 655360 | tf_op jit(solution)/shard_map/to_rhs/all_to_all | solution.py:396
  67.8 26.7 %copy-start = (bf16[320,320]{1,0:T(8,128)(2,1)S(1)}, bf16[320,320]{1,0:T(8,128)(2,1)}, u32[]{:S(2)}) copy-start(bf16[320,320]{1,0:T(8,128)(2,1)} %mix_ref.1) | copy-start | bytes 614404
  71.6 39.1 %copy-start.1 = (f32[8,512]{1,0:T(8,128)S(1)}, f32[8,512]{1,0:T(8,128)}, u32[]{:S(2)}) copy-start(f32[8,512]{1,0:T(8,128)} %dir_ref.5) | copy-start | bytes 49156
  71.6 39.1 %copy-start.2 = (f32[8,512]{1,0:T(8,128)S(1)}, f32[8,512]{1,0:T(8,128)}, u32[]{:S(2)}) copy-start(f32[8,512]{1,0:T(8,128)} %res_ref.3) | copy-start | bytes 49156
  71.6 39.1 %copy-start.4 = (f32[512]{0:T(512)S(1)}, f32[512]{0:T(512)}, u32[]{:S(2)}) copy-start(f32[512]{0:T(512)} %param.13) | copy-start | bytes 6148
  71.6 39.1 %copy-start.6 = (bf16[128,128]{1,0:T(8,128)(2,1)S(1)}, bf16[128,128]{1,0:T(8,128)(2,1)}, u32[]{:S(2)}) copy-start(bf16[128,128]{1,0:T(8,128)(2,1)} %lon_ref.1) | copy-start | bytes 98308
  110.7 23.1 %copy-start.5 = (s32[1,512]{1,0:T(1,128)S(1)}, s32[1,512]{1,0:T(1,128)}, u32[]{:S(2)}) copy-start(s32[1,512]{1,0:T(1,128)} %get-tuple-element.12.slot_ref) | copy-start | bytes 6148
  110.7 27.8 %copy-start.3 = (f32[8,512]{1,0:T(8,128)S(1)}, f32[8,512]{1,0:T(8,128)}, u32[]{:S(2)}) copy-start(f32[8,512]{1,0:T(8,128)} %sol_ref.1) | copy-start | bytes 49156
  127.7 10.9 %all-to-all-start.5 = ((f32[8,8,128]{2,1,0:T(8,128)}), f32[8,8,128]{2,1,0:T(8,128)S(1)}, u32[]{:S(2)}, u32[]{:S(2)}) async-start(f32[8,8,128]{2,1,0:T(8,128)} %gram_sum.1), calls=%async_computation.5 | async-start | bytes 65536 | tf_op jit(solution)/shard_map/gram_sum/all_to_all | solution.py:396

commit v4 on v3

--- a/solution.py
+++ b/solution.py
@@ -80,8 +80,9 @@
     res_hbm,
     err_hbm,
     send_hbm,
+    slot_hbm,
+    send_ref,
     slot_ref,
-    send_ref,
     window_ref,
     tiles_ref,
     foot_ref,
@@ -122,20 +123,9 @@
     position = jnp.sum(before * named_f, axis=0, keepdims=True).astype(I32)
     slot = owner * CAP + position
     slot_ref[...] = slot
+    slot_copy = pltpu.make_async_copy(slot_ref, slot_hbm, sems.at[6])
+    slot_copy.start()
     pick[...] = slot_matrix(slot)
-    group = 2 * LANES
-    share = group // NT
-    out_row = lax.broadcasted_iota(I32, (group, group), 0)
-    in_row = lax.broadcasted_iota(I32, (group, group), 1)
-    sort = jnp.where(in_row == out_row % share * NT + out_row // share, 1.0, 0.0).astype(BF16)
-    copies[1].wait()
-    for g in range(OBS_DEV // share):
-        rows = dot(sort, foot_ref[g * group : (g + 1) * group, :]).astype(BF16)
-        for k in range(NT):
-            by_tile[g * share : (g + 1) * share, k * LANES : (k + 1) * LANES] = rows[
-                k * share : (k + 1) * share, :
-            ]
-    moved[...] = dot(pick[...], by_tile[...])
     for copy in copies[2:]:
         copy.wait()
     tile = tiles_ref[...]
@@ -157,31 +147,46 @@
         axis=0,
     ).astype(BF16)
     meta[...] = dot_rows(values, pick[...])
+    group = 2 * LANES
+    share = group // NT
+    out_row = lax.broadcasted_iota(I32, (group, group), 0)
+    in_row = lax.broadcasted_iota(I32, (group, group), 1)
+    sort = jnp.where(in_row == out_row % share * NT + out_row // share, 1.0, 0.0).astype(BF16)
+    copies[1].wait()
+    for g in range(OBS_DEV // share):
+        rows = dot(sort, foot_ref[g * group : (g + 1) * group, :]).astype(BF16)
+        for k in range(NT):
+            by_tile[g * share : (g + 1) * share, k * LANES : (k + 1) * LANES] = rows[
+                k * share : (k + 1) * share, :
+            ]
+    lane = lax.broadcasted_iota(I32, (16, LANES), 1)
     sends = []
-    lane = lax.broadcasted_iota(I32, (16, LANES), 1)
-    for block in range(N_WIDE):
-        rows = slice(block * CAP, (block + 1) * CAP)
-        parts = [moved[rows, k * LANES : (k + 1) * LANES] for k in range(NT)]
-        send_ref[block, : NT * CAP, :] = jnp.concatenate(parts, axis=0).astype(BF16)
-        groups = [take_lanes(meta, 16 * g, 16, block) for g in range(3)]
-        joined = jnp.where(
-            lane < CAP,
-            groups[0],
-            jnp.where(
-                lane < 2 * CAP,
-                pltpu.roll(groups[1], CAP, 1),
-                jnp.where(lane < 3 * CAP, pltpu.roll(groups[2], 2 * CAP, 1), 0.0),
-            ),
+    for first in range(0, N_WIDE, SEND_BLOCKS):
+        part = slice(first * CAP, (first + SEND_BLOCKS) * CAP)
+        moved[part, :] = dot(pick[part, :], by_tile[...])
+        for block in range(first, first + SEND_BLOCKS):
+            rows = slice(block * CAP, (block + 1) * CAP)
+            parts = [moved[rows, k * LANES : (k + 1) * LANES] for k in range(NT)]
+            send_ref[block, : NT * CAP, :] = jnp.concatenate(parts, axis=0).astype(BF16)
+            groups = [take_lanes(meta, 16 * g, 16, block) for g in range(3)]
+            joined = jnp.where(
+                lane < CAP,
+                groups[0],
+                jnp.where(
+                    lane < 2 * CAP,
+                    pltpu.roll(groups[1], CAP, 1),
+                    jnp.where(lane < 3 * CAP, pltpu.roll(groups[2], 2 * CAP, 1), 0.0),
+                ),
+            )
+            send_ref[block, NT * CAP :, :] = joined.astype(BF16)
+        blocks = pl.ds(first, SEND_BLOCKS)
+        sends.append(
+            pltpu.make_async_copy(
+                send_ref.at[blocks], send_hbm.at[blocks], send_sems.at[first // SEND_BLOCKS]
+            )
         )
-        send_ref[block, NT * CAP :, :] = joined.astype(BF16)
-        if block % SEND_BLOCKS == SEND_BLOCKS - 1:
-            part = pl.ds(block + 1 - SEND_BLOCKS, SEND_BLOCKS)
-            sends.append(
-                pltpu.make_async_copy(
-                    send_ref.at[part], send_hbm.at[part], send_sems.at[block // SEND_BLOCKS]
-                )
-            )
-            sends[-1].start()
+        sends[-1].start()
+    slot_copy.wait()
     for send in sends:
         send.wait()
 
@@ -244,14 +249,16 @@
         rows_f[n * CELLS : (n + 1) * CELLS, :] = flux_ref[n ^ turn].astype(F32)
     for a in range(QUAD):
         for d in range(DAY_DEV):
-            columns[a * N_WIDE : (a + 1) * N_WIDE, d * LANES : (d + 1) * LANES] = rows_f[
+            columns[d, pl.ds(a, N_WIDE, stride=QUAD), :] = rows_f[
                 pl.ds(d * QUAD + a, N_WIDE, stride=CHUNK), :
-            ].astype(BF16)
-    mixed = dot(mix_ref[...], columns[...])
-    for a in range(QUAD):
-        for d in range(DAY_DEV):
-            rows_f[pl.ds(d * QUAD + a, N_WIDE, stride=CHUNK), :] = mixed[
-                a * N_WIDE : (a + 1) * N_WIDE, d * LANES : (d + 1) * LANES
+            ]
+    side_by_side = jnp.concatenate([columns[d].astype(BF16) for d in range(DAY_DEV)], axis=1)
+    mixed = dot(mix_ref[...], side_by_side)
+    for d in range(DAY_DEV):
+        columns[d] = mixed[:, d * LANES : (d + 1) * LANES]
+        for a in range(QUAD):
+            rows_f[pl.ds(d * QUAD + a, N_WIDE, stride=CHUNK), :] = columns[
+                d, pl.ds(a, N_WIDE, stride=QUAD), :
             ]
     out_ref[...] = rows_f[...].astype(BF16)
 
@@ -320,18 +327,6 @@
         send_ref[block] = jnp.where(lane < CAP, take_lanes(model, 0, RHS, block), gram)
 
 
-def gather_kernel(home_ref, slot_ref, dir_ref, err_ref, image_ref, lined):
-    lined[...] = jnp.zeros((RHS, SLOTS), F32)
-    lane = lax.broadcasted_iota(I32, (RHS, LANES), 1)
-    for block in range(N_WIDE):
-        add_lanes(lined, 0, RHS, block, jnp.where(lane < CAP, home_ref[block], 0.0))
-    high, rest = split_two(lined[...])
-    middle, low = split_two(rest)
-    parts = jnp.concatenate([high, middle, low], axis=0).astype(BF16)
-    placed = dot(parts, slot_matrix(slot_ref[...]))
-    image_ref[...] = placed[0:8] + placed[8:16] + placed[16:24] + err_ref[...] * dir_ref[...]
-
-
 def sum_kernel(home_ref, out_ref):
     total = home_ref[0]
     for block in range(1, N_WIDE):
@@ -355,7 +350,26 @@
     return [m[:, RHS:] for m in state]
 
 
-def update_kernel(gram_ref, sol_ref, res_ref, dir_ref, image_ref, sol_out, res_out, dir_out):
+def small_dot(left, right):
+    terms = [left[:, k : k + 1] * right[k : k + 1, :] for k in range(RHS)]
+    while len(terms) > 1:
+        terms = [a + b for a, b in zip(terms[::2], terms[1::2])]
+    return terms[0]
+
+
+def update_kernel(
+    gram_ref, home_ref, slot_ref, err_ref, sol_ref, res_ref, dir_ref, sol_out, res_out, dir_out, lined
+):
+    lined[...] = jnp.zeros((RHS, SLOTS), F32)
+    lane = lax.broadcasted_iota(I32, (RHS, LANES), 1)
+    for block in range(N_WIDE):
+        add_lanes(lined, 0, RHS, block, jnp.where(lane < CAP, home_ref[block], 0.0))
+    high, rest = split_two(lined[...])
+    middle, low = split_two(rest)
+    parts = jnp.concatenate([high, middle, low], axis=0).astype(BF16)
+    placed = dot(parts, slot_matrix(slot_ref[...]))
+    direction = dir_ref[...]
+    image = placed[0:8] + placed[8:16] + placed[16:24] + err_ref[...] * direction
     total = gram_ref[0]
     for n in range(1, N_NARROW):
         total = total + gram_ref[n]
@@ -363,17 +377,15 @@
     image_dir, dir_image, image_res, res_image, image_image, res_norm = [block(g) for g in range(6)]
     sym = 0.5 * (image_dir + dir_image)
     sym_inverse, norm_inverse = inverses([sym, res_norm])
-    step = dot(sym_inverse, res_norm, HIGHEST)
-    step_t = dot(res_norm, sym_inverse, HIGHEST)
-    crossed = dot(step_t, image_res, HIGHEST) + dot(res_image, step, HIGHEST)
-    squared = dot(dot(step_t, image_image, HIGHEST), step, HIGHEST)
-    norm_new = res_norm - crossed + squared
-    ratio_t = dot(norm_new, norm_inverse, HIGHEST)
-    direction = dir_ref[...]
-    sol_out[...] = sol_ref[...] + dot(step_t, direction, HIGHEST)
-    residual = res_ref[...] - dot(step_t, image_ref[...], HIGHEST)
+    step = small_dot(sym_inverse, res_norm)
+    step_t = small_dot(res_norm, sym_inverse)
+    sol_out[...] = sol_ref[...] + small_dot(step_t, direction)
+    residual = res_ref[...] - small_dot(step_t, image)
     res_out[...] = residual
-    dir_out[...] = residual + dot(ratio_t, direction, HIGHEST)
+    remaining = res_image - small_dot(step_t, image_image)
+    norm_new = res_norm - small_dot(step_t, image_res) - small_dot(remaining, step)
+    ratio_t = small_dot(norm_new, norm_inverse)
+    dir_out[...] = residual + small_dot(ratio_t, direction)
 
 
 VMEM = pl.BlockSpec(memory_space=pltpu.VMEM)
@@ -433,6 +445,7 @@
             [
                 vmem((N_WIDE, PAYLOAD, LANES), BF16),
                 vmem((1, OBS_DEV), I32),
+                vmem((1, OBS_DEV), I32),
                 vmem((NT, OBS_DEV), I32),
                 vmem((OBS_DEV * NT, LANES), BF16),
                 vmem((RHS, OBS_DEV), F32),
@@ -442,12 +455,12 @@
                 vmem((SLOTS, OBS_DEV), BF16),
                 vmem((SLOTS, NT * LANES), F32),
                 vmem((META, SLOTS), F32),
-                pltpu.SemaphoreType.DMA((6,)),
+                pltpu.SemaphoreType.DMA((7,)),
                 pltpu.SemaphoreType.DMA((N_WIDE // SEND_BLOCKS,)),
             ],
             2 * SLOTS * OBS_DEV * NT * LANES,
             2 * SLOTS * OBS_DEV,
-            [HBM, VMEM],
+            [HBM, HBM],
             VMEM_WHOLE,
         )(
             window.reshape(1, OBS_DEV),
@@ -477,17 +490,14 @@
     with jax.named_scope("to_rhs"):
         by_rhs = exchange(flux.reshape(N_NARROW, CELLS, LANES), BOTH, WINDOW_GROUPS)
     with jax.named_scope("lat_mix"):
-        lat_mix = (
-            spatial_lat.reshape(N_WIDE, QUAD, N_WIDE, QUAD).transpose(1, 0, 3, 2).reshape(LAT, LAT)
-        )
         (spread,) = call(
             lat_kernel,
             [VMEM, VMEM],
             [((ROWS, LANES), BF16)],
-            [vmem((ROWS, LANES), F32), vmem((LAT, DAY_DEV * LANES), BF16)],
+            [vmem((ROWS, LANES), F32), vmem((DAY_DEV, LAT, LANES), F32)],
             2 * LAT * LAT * DAY_DEV * LANES,
             4 * ROWS * LANES,
-        )(lat_mix, by_rhs)
+        )(spatial_lat, by_rhs)
     with jax.named_scope("to_days"):
         by_day = exchange(spread.reshape(N_WIDE, CHUNK, LANES), BOTH, PLANE_GROUPS)
     with jax.named_scope("day_mix"):
@@ -534,25 +544,16 @@
             4 * N_WIDE * RHS * LANES,
         )(home)
         grams = exchange(partial, "narrow")
-    with jax.named_scope("image"):
-        (image,) = call(
-            gather_kernel,
-            [VMEM] * 4,
-            [((RHS, OBS_DEV), F32)],
-            [vmem((RHS, SLOTS), F32)],
-            2 * 24 * SLOTS * OBS_DEV,
-            4 * SLOTS * RHS,
-        )(home, slot, direction, errors)
     with jax.named_scope("update"):
         return tuple(
             call(
                 update_kernel,
-                [VMEM] * 5,
+                [VMEM] * 7,
                 [((RHS, OBS_DEV), F32)] * 3,
-                [],
-                2 * 18 * 8 * 8 * OBS_DEV,
+                [vmem((RHS, SLOTS), F32)],
+                2 * 24 * SLOTS * OBS_DEV,
                 28 * RHS * OBS_DEV,
-            )(grams, solution, residual, direction, image)
+            )(grams, home, slot, errors, solution, residual, direction)
         )
 
 

time: 141 us -> 138 us (0.979)
  blocking collectives: 92.9 us -> 124 us
  starting transfers between devices: 13.3 us -> 0 us
  waiting for transfers between devices: 11.7 us -> 0 us
  local copies, waits for them, and re-layouts: 7.04 us -> 0.04 us
  Pallas kernels: 15.3 us -> 12.5 us
    all_to_all x4 -> x6, blocking collectives: 92.9 us -> 124 us  [exchange(): lax.all_to_all(array, axis, split_axis=0, concat_axis=0, tiled=True, axis...]
    all_to_all x2 -> x0, starting transfers between devices: 13.3 us -> none  [exchange(): lax.all_to_all(array, axis, split_axis=0, concat_axis=0, tiled=True, axis...]
    all_to_all x2 -> x0, waiting for transfers between devices: 11.7 us -> none  [exchange(): lax.all_to_all(array, axis, split_axis=0, concat_axis=0, tiled=True, axis...]
    reshape x2 -> x0, local copies, waits for them, and re-layouts: 4.25 us -> none  [on_device(): spatial_lat.reshape(N_WIDE, QUAD, N_WIDE, QUAD).transpose(1, 0, 3, 2)]
    transpose x1 -> x0, local copies, waits for them, and re-layouts: 2.74 us -> none  [on_device(): spatial_lat.reshape(N_WIDE, QUAD, N_WIDE, QUAD).transpose(1, 0, 3, 2)]
    pallas_call x2 -> x1, Pallas kernels: 2.85 us -> 1.85 us  [on_device(): call(update_kernel, [VMEM] * 7, [((RHS, OBS_DEV), F32)] * 3, [vmem((RHS,...]
  transfers between devices with their start and end apart: 2 -> 0, of which waited for: 2 -> 0; matrix products, arithmetic and copies ran while one was open for 5% -> 0% of each run, Pallas kernels for 0% -> 0%
where the time goes in v4:
time: 138 us
  blocking collectives  124 us (90%)
  Pallas kernels  12.5 us (9%)
    all_to_all x6, blocking collectives, exchange(): lax.all_to_all(array, axis, split_axis=0, concat_axis=0, tiled=True, axis...  124 us
    pallas_call x1, Pallas kernels, on_device(): call(pack_kernel, [HBM] * 6, [((N_WIDE, PAYLOAD, LANES), BF16), ((1, OBS_...  4.28 us
    pallas_call x1, Pallas kernels, on_device(): call(adjoint_kernel, [VMEM], [((ROWS, LANES), BF16), ((META, SLOTS), F32)...  2.93 us

profile of v4, /device:TPU:1, one launch (start us, length us, event | category | flops | bytes accessed | tf_op | source)
XLA Modules:
  0.0 137.8 jit_solution(295734730848239145)
XLA Ops:
  0.6 4.3 %pack.1 = (bf16[32,176,128]{2,1,0:T(8,128)(2,1)}, s32[1,512]{1,0:T(1,128)}) custom-call(s32[1,512]{1,0:T(1,128)} %bitcast.19, s32[4,512]{1,0:T(4,128)} %bitcast.18, bf16[2048,128]{1,0:T(8,128)(2,1)} %bitcast.17, f32[8,512]{1,0:T(8,128)} %dir_ref.3, f32[8,512]{1,0:T(8,128)} %res_ref.3, f32[1,512]{1,0:T(1,128)} %bitcast.14), custom_call_target="tpu_custom_call" | custom-call | flops 671088640 | bytes 1310720 | tf_op jit(solution)/shard_map/pack/pallas_call | solution.py:441
  4.9 48.3 %all_to_all.30.recv_ref = bf16[32,176,128]{2,1,0:T(8,128)(2,1)S(1)} all-to-all(bf16[32,176,128]{2,1,0:T(8,128)(2,1)} %get-tuple-element.8), channel_id=1, replica_groups=mesh['wide'=32,'narrow'=8] {'wide'}, dimensions={0} | all-to-all | bytes 2883584 | tf_op jit(solution)/shard_map/route/all_to_all | solution.py:408
  53.2 0.0 copy-start.1
  53.2 2.9 %adjoint.1 = (bf16[1280,128]{1,0:T(8,128)(2,1)S(1)}, f32[48,1280]{1,0:T(8,128)S(1)}, bf16[4,1280,256]{2,1,0:T(8,128)(2,1)S(1)}) custom-call(bf16[32,176,128]{2,1,0:T(8,128)(2,1)S(1)} %all_to_all.30.recv_ref), custom_call_target="tpu_custom_call" | custom-call | flops 1677721600 | bytes 2621440 | tf_op jit(solution)/shard_map/adjoint/pallas_call | solution.py:476
  56.1 0.0 copy-start
  56.2 21.6 %all_to_all.31.flux_ref = bf16[8,160,128]{2,1,0:T(8,128)(2,1)S(1)} all-to-all(bf16[8,160,128]{2,1,0:T(8,128)(2,1)S(1)} %bitcast.12), channel_id=1, replica_groups={{0,33,66,99,132,165,198,231},{8,41,74,107,140,173,206,239},{16,49,82,11..., dimensions={0} | all-to-all | bytes 655360 | tf_op jit(solution)/shard_map/to_rhs/all_to_all | solution.py:408
  77.7 0.0 copy-done.1
  77.7 0.0 copy-start.2
  77.7 0.0 copy-start.3
  77.7 0.0 copy-start.5
  77.8 0.0 copy-start.7
  77.8 0.5 lat_mix.1
  78.2 15.0 %all_to_all.32 = bf16[32,40,128]{2,1,0:T(8,128)(2,1)S(1)} all-to-all(bf16[32,40,128]{2,1,0:T(8,128)(2,1)S(1)} %bitcast.11), channel_id=1, replica_groups={{0,8,16,24,1,9,17,25,2,10,18,26,3,11,19,27,4,12,20,28,5,13,21,29,6,14,2..., dimensions={0} | all-to-all | bytes 655360 | tf_op jit(solution)/shard_map/to_days/all_to_all | solution.py:408
  93.2 0.0 copy-done
  93.2 0.5 day_mix.1
  93.7 15.8 %all_to_all.33 = bf16[32,40,128]{2,1,0:T(8,128)(2,1)S(1)} all-to-all(bf16[32,40,128]{2,1,0:T(8,128)(2,1)S(1)} %bitcast.10), channel_id=1, replica_groups=mesh['wide'=32,'narrow'=8] {'wide'}, dimensions={0} | all-to-all | bytes 655360 | tf_op jit(solution)/shard_map/to_windows/all_to_all | solution.py:408
  109.5 0.0 copy-done.2
  109.5 0.0 copy-done.3
  109.5 0.0 copy-done.5
  109.5 0.0 copy-done.7
  109.5 0.0 copy-start.4
  109.5 0.0 copy-start.6
  109.5 2.5 %forward.1 = f32[32,8,128]{2,1,0:T(8,128)S(1)} custom-call(bf16[128,128]{1,0:T(8,128)(2,1)S(1)} %copy-done.7, bf16[1280,128]{1,0:T(8,128)(2,1)S(1)} %bitcast.13, bf16[4,1280,256]{2,1,0:T(8,128)(2,1)S(1)} %get-tuple-element.10.foot_ref, f32[48,1280]{1,0:T(8,128)S(1)} %get-tuple-element.11.meta_ref, f32[8,512]{1,0:T(8,128)S(1)} %copy-done.2, ...), custom_call_target="tpu_custom_call" | custom-call | flops 1677721600 | bytes 2621440 | tf_op jit(solution)/shard_map/forward/pallas_call | solution.py:515
  112.0 13.8 %all_to_all.34.home_ref = f32[32,8,128]{2,1,0:T(8,128)S(1)} all-to-all(f32[32,8,128]{2,1,0:T(8,128)S(1)} %forward.1), channel_id=1, replica_groups=mesh['wide'=32,'narrow'=8] {'wide'}, dimensions={0} | all-to-all | bytes 262144 | tf_op jit(solution)/shard_map/home/all_to_all | solution.py:408
  125.9 10.1 %all_to_all.35.gram_ref = f32[8,8,128]{2,1,0:T(8,128)S(1)} all-to-all(f32[8,8,128]{2,1,0:T(8,128)S(1)} %gram_sum.1), channel_id=1, replica_groups=mesh['wide'=32,'narrow'=8] {'narrow'}, dimensions={0} | all-to-all | bytes 65536 | tf_op jit(solution)/shard_map/gram_sum/all_to_all | solution.py:408
  135.9 0.0 copy-done.4
  135.9 0.0 copy-done.6
  135.9 1.8 %update.1 = (f32[8,512]{1,0:T(8,128)}, f32[8,512]{1,0:T(8,128)}, f32[8,512]{1,0:T(8,128)}) custom-call(f32[8,8,128]{2,1,0:T(8,128)S(1)} %all_to_all.35.gram_ref, f32[32,8,128]{2,1,0:T(8,128)S(1)} %all_to_all.34.home_ref, s32[1,512]{1,0:T(1,128)S(1)} %copy-done.6, f32[1,512]{1,0:T(1,128)S(1)} %bitcast.16, f32[8,512]{1,0:T(8,128)S(1)} %copy-done.4, ...), custom_call_target="tpu_custom_call" | custom-call | flops 31457280 | bytes 114688 | tf_op jit(solution)/shard_map/update/pallas_call | solution.py:549
  (1 shorter events, 0.0 us)
Async XLA Ops:
  53.2 24.5 %copy-start.1 = (bf16[128,128]{1,0:T(8,128)(2,1)S(1)}, bf16[128,128]{1,0:T(8,128)(2,1)}, u32[]{:S(2)}) copy-start(bf16[128,128]{1,0:T(8,128)(2,1)} %mix_ref.2) | copy-start | bytes 98308
  56.1 37.1 %copy-start = (bf16[320,320]{1,0:T(8,128)(2,1)S(1)}, bf16[320,320]{1,0:T(8,128)(2,1)}, u32[]{:S(2)}) copy-start(bf16[320,320]{1,0:T(8,128)(2,1)} %mix_ref.3) | copy-start | bytes 614404
  77.7 31.7 %copy-start.2 = (f32[8,512]{1,0:T(8,128)S(1)}, f32[8,512]{1,0:T(8,128)}, u32[]{:S(2)}) copy-start(f32[8,512]{1,0:T(8,128)} %dir_ref.3) | copy-start | bytes 49156
  77.7 31.7 %copy-start.3 = (f32[8,512]{1,0:T(8,128)S(1)}, f32[8,512]{1,0:T(8,128)}, u32[]{:S(2)}) copy-start(f32[8,512]{1,0:T(8,128)} %res_ref.3) | copy-start | bytes 49156
  77.7 31.7 %copy-start.5 = (f32[512]{0:T(512)S(1)}, f32[512]{0:T(512)}, u32[]{:S(2)}) copy-start(f32[512]{0:T(512)} %param.13) | copy-start | bytes 6148
  77.8 31.7 %copy-start.7 = (bf16[128,128]{1,0:T(8,128)(2,1)S(1)}, bf16[128,128]{1,0:T(8,128)(2,1)}, u32[]{:S(2)}) copy-start(bf16[128,128]{1,0:T(8,128)(2,1)} %lon_ref.1) | copy-start | bytes 98308
  109.5 26.5 %copy-start.4 = (f32[8,512]{1,0:T(8,128)S(1)}, f32[8,512]{1,0:T(8,128)}, u32[]{:S(2)}) copy-start(f32[8,512]{1,0:T(8,128)} %sol_ref.1) | copy-start | bytes 49156
  109.5 26.4 %copy-start.6 = (s32[1,512]{1,0:T(1,128)S(1)}, s32[1,512]{1,0:T(1,128)}, u32[]{:S(2)}) copy-start(s32[1,512]{1,0:T(1,128)} %get-tuple-element.12.slot_ref) | copy-start | bytes 6148

commit v5 on v4

--- a/solution.py
+++ b/solution.py
@@ -30,7 +30,6 @@
 GRAM_AT = CAP
 SEND_BLOCKS = 8
 VMEM_LIMIT = 48 * 1024 * 1024
-VMEM_WHOLE = 63 * 1024 * 1024
 
 
 def dot_rows(left, right, precision=None):
@@ -43,6 +42,15 @@
     return lax.dot_general(
         left, right, (((1,), (0,)), ((), ())), precision=precision, preferred_element_type=F32
     )
+
+
+def here():
+    band = lax.axis_index("narrow")
+    return lax.axis_index("wide") >> 2, (band & 1) * (N_NARROW // 2) + (band >> 1)
+
+
+def band_of(turn):
+    return (turn & 3) * 2 + (turn >> 2)
 
 
 def lane_window(block):
@@ -79,8 +87,6 @@
     dir_hbm,
     res_hbm,
     err_hbm,
-    send_hbm,
-    slot_hbm,
     send_ref,
     slot_ref,
     window_ref,
@@ -94,7 +100,6 @@
     moved,
     meta,
     sems,
-    send_sems,
 ):
     copies = [
         pltpu.make_async_copy(source, target, sems.at[i])
@@ -116,15 +121,15 @@
     )
     earlier = jnp.where(earlier, 1.0, 0.0).astype(BF16)
     copies[0].wait()
-    owner = window_ref[...] ^ (lax.axis_index("narrow") * QUAD)
+    window = window_ref[...]
+    turn = here()[1]
+    owner = ((turn - (window >> 2)) & 7) * QUAD + (window & 3)
     named = lax.broadcasted_iota(I32, (N_WIDE, OBS_DEV), 0) == owner
     named_f = jnp.where(named, 1.0, 0.0)
     before = dot(named_f.astype(BF16), earlier)
     position = jnp.sum(before * named_f, axis=0, keepdims=True).astype(I32)
     slot = owner * CAP + position
     slot_ref[...] = slot
-    slot_copy = pltpu.make_async_copy(slot_ref, slot_hbm, sems.at[6])
-    slot_copy.start()
     pick[...] = slot_matrix(slot)
     for copy in copies[2:]:
         copy.wait()
@@ -160,7 +165,6 @@
                 k * share : (k + 1) * share, :
             ]
     lane = lax.broadcasted_iota(I32, (16, LANES), 1)
-    sends = []
     for first in range(0, N_WIDE, SEND_BLOCKS):
         part = slice(first * CAP, (first + SEND_BLOCKS) * CAP)
         moved[part, :] = dot(pick[part, :], by_tile[...])
@@ -179,16 +183,6 @@
                 ),
             )
             send_ref[block, NT * CAP :, :] = joined.astype(BF16)
-        blocks = pl.ds(first, SEND_BLOCKS)
-        sends.append(
-            pltpu.make_async_copy(
-                send_ref.at[blocks], send_hbm.at[blocks], send_sems.at[first // SEND_BLOCKS]
-            )
-        )
-        sends[-1].start()
-    slot_copy.wait()
-    for send in sends:
-        send.wait()
 
 
 def half_cell(ids):
@@ -235,18 +229,19 @@
             total[...] = product
         else:
             total[...] += product
+    plane, turn = here()
     for r in range(RHS):
         for side in range(2):
-            at = r * CELLS + side * HALF
-            flux_ref[at : at + HALF, :] = total[
+            at = side * HALF
+            flux_ref[(r + turn - plane) & 7, at : at + HALF, :] = total[
                 r * HALF : (r + 1) * HALF, side * LANES : (side + 1) * LANES
             ].astype(BF16)
 
 
 def lat_kernel(mix_ref, flux_ref, out_ref, rows_f, columns):
-    turn = (lax.axis_index("wide") >> 2) ^ lax.axis_index("narrow")
-    for n in range(N_NARROW):
-        rows_f[n * CELLS : (n + 1) * CELLS, :] = flux_ref[n ^ turn].astype(F32)
+    for t in range(N_NARROW):
+        n = band_of(t)
+        rows_f[n * CELLS : (n + 1) * CELLS, :] = flux_ref[t].astype(F32)
     for a in range(QUAD):
         for d in range(DAY_DEV):
             columns[d, pl.ds(a, N_WIDE, stride=QUAD), :] = rows_f[
@@ -264,9 +259,9 @@
 
 
 def day_kernel(mix_ref, flux_ref, out_ref, rows_f, columns):
-    turn_in, turn_out = lax.axis_index("wide") >> 2, lax.axis_index("narrow")
+    plane, turn = here()
     for h in range(N_NARROW):
-        rows_f[h * CELLS : (h + 1) * CELLS, :] = flux_ref[h ^ turn_in].astype(F32)
+        rows_f[h * CELLS : (h + 1) * CELLS, :] = flux_ref[band_of((h + plane) & 7)].astype(F32)
     for a in range(QUAD):
         columns[:, a * LANES : (a + 1) * LANES] = rows_f[
             pl.ds(a, DAYS, stride=QUAD), :
@@ -275,7 +270,7 @@
     for a in range(QUAD):
         rows_f[pl.ds(a, DAYS, stride=QUAD), :] = mixed[:, a * LANES : (a + 1) * LANES]
     for h in range(N_NARROW):
-        out_ref[h ^ turn_out] = rows_f[h * CELLS : (h + 1) * CELLS, :].astype(BF16)
+        out_ref[(turn - h) & 7] = rows_f[h * CELLS : (h + 1) * CELLS, :].astype(BF16)
 
 
 def forward_kernel(
@@ -392,14 +387,18 @@
 HBM = pl.BlockSpec(memory_space=pltpu.HBM)
 
 
-def call(kernel, places, outs, scratch, flops, moved, out_places=None, limit=VMEM_LIMIT):
+def in_hbm(array):
+    return pltpu.with_memory_space_constraint(array, pltpu.HBM)
+
+
+def call(kernel, places, outs, scratch, flops, moved):
     return pl.pallas_call(
         kernel,
         in_specs=places,
-        out_specs=out_places or [VMEM] * len(outs),
+        out_specs=[VMEM] * len(outs),
         out_shape=[jax.ShapeDtypeStruct(shape, dtype) for shape, dtype in outs],
         scratch_shapes=scratch,
-        compiler_params=pltpu.CompilerParams(vmem_limit_bytes=limit),
+        compiler_params=pltpu.CompilerParams(vmem_limit_bytes=VMEM_LIMIT),
         cost_estimate=pl.CostEstimate(flops=flops, bytes_accessed=moved, transcendentals=0),
     )
 
@@ -412,11 +411,10 @@
 
 BOTH = ("wide", "narrow")
 WINDOW_GROUPS = [
-    [((h ^ n) * QUAD + q) * N_NARROW + n for n in range(N_NARROW)]
+    [((turn - h) % N_NARROW * QUAD + q) * N_NARROW + band_of(turn) for turn in range(N_NARROW)]
     for h in range(N_NARROW)
     for q in range(QUAD)
 ]
-WINDOW_GROUPS = [sorted(group) for group in WINDOW_GROUPS]
 PLANE_GROUPS = [
     [(plane * QUAD + i % QUAD) * N_NARROW + i // QUAD for i in range(N_WIDE)]
     for plane in range(N_NARROW)
@@ -443,8 +441,6 @@
             [HBM] * 6,
             [((N_WIDE, PAYLOAD, LANES), BF16), ((1, OBS_DEV), I32)],
             [
-                vmem((N_WIDE, PAYLOAD, LANES), BF16),
-                vmem((1, OBS_DEV), I32),
                 vmem((1, OBS_DEV), I32),
                 vmem((NT, OBS_DEV), I32),
                 vmem((OBS_DEV * NT, LANES), BF16),
@@ -455,20 +451,17 @@
                 vmem((SLOTS, OBS_DEV), BF16),
                 vmem((SLOTS, NT * LANES), F32),
                 vmem((META, SLOTS), F32),
-                pltpu.SemaphoreType.DMA((7,)),
-                pltpu.SemaphoreType.DMA((N_WIDE // SEND_BLOCKS,)),
+                pltpu.SemaphoreType.DMA((6,)),
             ],
             2 * SLOTS * OBS_DEV * NT * LANES,
             2 * SLOTS * OBS_DEV,
-            [HBM, HBM],
-            VMEM_WHOLE,
         )(
-            window.reshape(1, OBS_DEV),
-            tiles.T,
-            footprint.reshape(OBS_DEV * NT, LANES),
-            direction,
-            residual,
-            errors,
+            in_hbm(window.reshape(1, OBS_DEV)),
+            in_hbm(tiles.T),
+            in_hbm(footprint.reshape(OBS_DEV * NT, LANES)),
+            in_hbm(direction),
+            in_hbm(residual),
+            in_hbm(errors),
         )
     with jax.named_scope("route"):
         routed = exchange(packed, "wide")
@@ -476,7 +469,11 @@
         flux, meta, foot = call(
             adjoint_kernel,
             [VMEM],
-            [((ROWS, LANES), BF16), ((META, SLOTS), F32), ((NT, SLOTS, 2 * LANES), BF16)],
+            [
+                ((N_NARROW, CELLS, LANES), BF16),
+                ((META, SLOTS), F32),
+                ((NT, SLOTS, 2 * LANES), BF16),
+            ],
             [
                 vmem((NT, SLOTS, LANES), F32),
                 vmem((SLOTS, NT * LANES), F32),
@@ -488,7 +485,7 @@
             4 * NT * SLOTS * LANES,
         )(routed)
     with jax.named_scope("to_rhs"):
-        by_rhs = exchange(flux.reshape(N_NARROW, CELLS, LANES), BOTH, WINDOW_GROUPS)
+        by_rhs = exchange(flux, BOTH, WINDOW_GROUPS)
     with jax.named_scope("lat_mix"):
         (spread,) = call(
             lat_kernel,

time: 138 us -> 136 us (0.986)
  no operation moved by 1% of the time
where the time goes in v5:
time: 136 us
  blocking collectives  123 us (90%)
  Pallas kernels  11.7 us (9%)
    all_to_all x6, blocking collectives, exchange(): lax.all_to_all(array, axis, split_axis=0, concat_axis=0, tiled=True, axis...  123 us
    pallas_call x1, Pallas kernels, on_device(): call(pack_kernel, [HBM] * 6, [((N_WIDE, PAYLOAD, LANES), BF16), ((1, OBS_...  3.48 us
    pallas_call x1, Pallas kernels, on_device(): call(adjoint_kernel, [VMEM], [((N_NARROW, CELLS, LANES), BF16), ((META, S...  2.92 us

profile of v5, /device:TPU:1, one launch (start us, length us, event | category | flops | bytes accessed | tf_op | source)
XLA Modules:
  0.0 135.8 jit_solution(10166585515012267150)
XLA Ops:
  0.6 3.5 %pack.1 = (bf16[32,176,128]{2,1,0:T(8,128)(2,1)S(1)}, s32[1,512]{1,0:T(1,128)S(1)}) custom-call(s32[1,512]{1,0:T(1,128)} %bitcast.17, s32[4,512]{1,0:T(4,128)} %bitcast.16, bf16[2048,128]{1,0:T(8,128)(2,1)} %bitcast.15, f32[8,512]{1,0:T(8,128)} %dir_ref.3, f32[8,512]{1,0:T(8,128)} %res_ref.3, f32[1,512]{1,0:T(1,128)} %bitcast.12), custom_call_target="tpu_custom_call" | custom-call | flops 671088640 | bytes 1310720 | tf_op jit(solution)/shard_map/pack/pallas_call | solution.py:439
  4.1 48.1 %all_to_all.30.recv_ref = bf16[32,176,128]{2,1,0:T(8,128)(2,1)S(1)} all-to-all(bf16[32,176,128]{2,1,0:T(8,128)(2,1)S(1)} %get-tuple-element.8), channel_id=1, replica_groups=mesh['wide'=32,'narrow'=8] {'wide'}, dimensions={0} | all-to-all | bytes 2883584 | tf_op jit(solution)/shard_map/route/all_to_all | solution.py:407
  52.2 0.0 copy-start.1
  52.2 2.9 %adjoint.1 = (bf16[8,160,128]{2,1,0:T(8,128)(2,1)S(1)}, f32[48,1280]{1,0:T(8,128)S(1)}, bf16[4,1280,256]{2,1,0:T(8,128)(2,1)S(1)}) custom-call(bf16[32,176,128]{2,1,0:T(8,128)(2,1)S(1)} %all_to_all.30.recv_ref), custom_call_target="tpu_custom_call" | custom-call | flops 1677721600 | bytes 2621440 | tf_op jit(solution)/shard_map/adjoint/pallas_call | solution.py:469
  55.1 0.0 copy-start
  55.1 19.1 %all_to_all.31.flux_ref = bf16[8,160,128]{2,1,0:T(8,128)(2,1)S(1)} all-to-all(bf16[8,160,128]{2,1,0:T(8,128)(2,1)S(1)} %get-tuple-element.9), channel_id=1, replica_groups={{0,34,68,102,129,163,197,231},{8,42,76,110,137,171,205,239},{16,50,84,1..., dimensions={0} | all-to-all | bytes 655360 | tf_op jit(solution)/shard_map/to_rhs/all_to_all | solution.py:407
  74.2 0.0 copy-done.1
  74.2 0.0 copy-start.2
  74.2 0.0 copy-start.3
  74.2 0.0 copy-start.5
  74.2 0.0 copy-start.6
  74.2 0.4 lat_mix.1
  74.7 16.4 %all_to_all.32 = bf16[32,40,128]{2,1,0:T(8,128)(2,1)S(1)} all-to-all(bf16[32,40,128]{2,1,0:T(8,128)(2,1)S(1)} %bitcast.10), channel_id=1, replica_groups={{0,8,16,24,1,9,17,25,2,10,18,26,3,11,19,27,4,12,20,28,5,13,21,29,6,14,2..., dimensions={0} | all-to-all | bytes 655360 | tf_op jit(solution)/shard_map/to_days/all_to_all | solution.py:407
  91.1 0.0 copy-done
  91.1 0.5 day_mix.1
  91.6 15.7 %all_to_all.33 = bf16[32,40,128]{2,1,0:T(8,128)(2,1)S(1)} all-to-all(bf16[32,40,128]{2,1,0:T(8,128)(2,1)S(1)} %bitcast.9), channel_id=1, replica_groups=mesh['wide'=32,'narrow'=8] {'wide'}, dimensions={0} | all-to-all | bytes 655360 | tf_op jit(solution)/shard_map/to_windows/all_to_all | solution.py:407
  107.3 0.0 copy-done.2
  107.3 0.0 copy-done.3
  107.3 0.0 copy-done.5
  107.3 0.0 copy-done.6
  107.3 0.0 copy-start.4
  107.3 2.5 %forward.1 = f32[32,8,128]{2,1,0:T(8,128)S(1)} custom-call(bf16[128,128]{1,0:T(8,128)(2,1)S(1)} %copy-done.6, bf16[1280,128]{1,0:T(8,128)(2,1)S(1)} %bitcast.11, bf16[4,1280,256]{2,1,0:T(8,128)(2,1)S(1)} %get-tuple-element.10.foot_ref, f32[48,1280]{1,0:T(8,128)S(1)} %get-tuple-element.11.meta_ref, f32[8,512]{1,0:T(8,128)S(1)} %copy-done.2, ...), custom_call_target="tpu_custom_call" | custom-call | flops 1677721600 | bytes 2621440 | tf_op jit(solution)/shard_map/forward/pallas_call | solution.py:512
  109.8 14.1 %all_to_all.34.home_ref = f32[32,8,128]{2,1,0:T(8,128)S(1)} all-to-all(f32[32,8,128]{2,1,0:T(8,128)S(1)} %forward.1), channel_id=1, replica_groups=mesh['wide'=32,'narrow'=8] {'wide'}, dimensions={0} | all-to-all | bytes 262144 | tf_op jit(solution)/shard_map/home/all_to_all | solution.py:407
  124.0 9.9 %all_to_all.35.gram_ref = f32[8,8,128]{2,1,0:T(8,128)S(1)} all-to-all(f32[8,8,128]{2,1,0:T(8,128)S(1)} %gram_sum.1), channel_id=1, replica_groups=mesh['wide'=32,'narrow'=8] {'narrow'}, dimensions={0} | all-to-all | bytes 65536 | tf_op jit(solution)/shard_map/gram_sum/all_to_all | solution.py:407
  133.9 0.0 copy-done.4
  133.9 1.8 %update.1 = (f32[8,512]{1,0:T(8,128)}, f32[8,512]{1,0:T(8,128)}, f32[8,512]{1,0:T(8,128)}) custom-call(f32[8,8,128]{2,1,0:T(8,128)S(1)} %all_to_all.35.gram_ref, f32[32,8,128]{2,1,0:T(8,128)S(1)} %all_to_all.34.home_ref, s32[1,512]{1,0:T(1,128)S(1)} %get-tuple-element.12.slot_ref, f32[1,512]{1,0:T(1,128)S(1)} %bitcast.14, f32[8,512]{1,0:T(8,128)S(1)} %copy-done.4, ...), custom_call_target="tpu_custom_call" | custom-call | flops 31457280 | bytes 114688 | tf_op jit(solution)/shard_map/update/pallas_call | solution.py:546
  (1 shorter events, 0.0 us)
Async XLA Ops:
  52.2 22.0 %copy-start.1 = (bf16[128,128]{1,0:T(8,128)(2,1)S(1)}, bf16[128,128]{1,0:T(8,128)(2,1)}, u32[]{:S(2)}) copy-start(bf16[128,128]{1,0:T(8,128)(2,1)} %mix_ref.2) | copy-start | bytes 98308
  55.1 36.0 %copy-start = (bf16[320,320]{1,0:T(8,128)(2,1)S(1)}, bf16[320,320]{1,0:T(8,128)(2,1)}, u32[]{:S(2)}) copy-start(bf16[320,320]{1,0:T(8,128)(2,1)} %mix_ref.3) | copy-start | bytes 614404
  74.2 33.0 %copy-start.2 = (f32[8,512]{1,0:T(8,128)S(1)}, f32[8,512]{1,0:T(8,128)}, u32[]{:S(2)}) copy-start(f32[8,512]{1,0:T(8,128)} %dir_ref.3) | copy-start | bytes 49156
  74.2 33.0 %copy-start.3 = (f32[8,512]{1,0:T(8,128)S(1)}, f32[8,512]{1,0:T(8,128)}, u32[]{:S(2)}) copy-start(f32[8,512]{1,0:T(8,128)} %res_ref.3) | copy-start | bytes 49156
  74.2 33.0 %copy-start.5 = (f32[512]{0:T(512)S(1)}, f32[512]{0:T(512)}, u32[]{:S(2)}) copy-start(f32[512]{0:T(512)} %param.13) | copy-start | bytes 6148
  74.2 33.0 %copy-start.6 = (bf16[128,128]{1,0:T(8,128)(2,1)S(1)}, bf16[128,128]{1,0:T(8,128)(2,1)}, u32[]{:S(2)}) copy-start(bf16[128,128]{1,0:T(8,128)(2,1)} %lon_ref.1) | copy-start | bytes 98308
  107.3 26.6 %copy-start.4 = (f32[8,512]{1,0:T(8,128)S(1)}, f32[8,512]{1,0:T(8,128)}, u32[]{:S(2)}) copy-start(f32[8,512]{1,0:T(8,128)} %sol_ref.1) | copy-start | bytes 49156

commit v6 on v5

--- a/solution.py
+++ b/solution.py
@@ -53,21 +53,31 @@
     return (turn & 3) * 2 + (turn >> 2)
 
 
-def lane_window(block):
-    start = min(block * CAP // LANES * LANES, SLOTS - 2 * LANES)
-    return start, block * CAP - start
-
-
-def take_lanes(ref, row, rows, block):
-    start, shift = lane_window(block)
-    part = ref[row : row + rows, start : start + 2 * LANES]
-    return pltpu.roll(part, (2 * LANES - shift) % (2 * LANES), 1)[:, :LANES]
-
-
-def add_lanes(ref, row, rows, block, piece):
-    start, shift = lane_window(block)
-    wide = jnp.concatenate([piece, jnp.zeros((rows, LANES), F32)], axis=1)
-    ref[row : row + rows, start : start + 2 * LANES] += pltpu.roll(wide, shift, 1)
+def take_lanes(columns, lane, block, target):
+    start = block * CAP
+    first = start // LANES
+    part = columns[first]
+    if (start + CAP - 1) // LANES != first:
+        part = jnp.where(lane >= start % LANES, part, columns[first + 1])
+    return pltpu.roll(part, (target - start) % LANES, 1)
+
+
+def join_lanes(pieces, source, lane):
+    turned = [
+        pltpu.roll(piece, (block * CAP - source) % LANES, 1) for block, piece in enumerate(pieces)
+    ]
+    columns = []
+    for start in range(0, SLOTS, LANES):
+        blocks = range(start // CAP, (start + LANES - 1) // CAP + 1)
+        column = turned[blocks[-1]]
+        for block in reversed(blocks[:-1]):
+            column = jnp.where(lane < (block + 1) * CAP - start, turned[block], column)
+        columns.append(column)
+    return columns
+
+
+def columns_of(ref, row, rows):
+    return [ref[row : row + rows, at : at + LANES] for at in range(0, SLOTS, LANES)]
 
 
 def split_two(value):
@@ -165,6 +175,7 @@
                 k * share : (k + 1) * share, :
             ]
     lane = lax.broadcasted_iota(I32, (16, LANES), 1)
+    groups = [columns_of(meta, 16 * g, 16) for g in range(3)]
     for first in range(0, N_WIDE, SEND_BLOCKS):
         part = slice(first * CAP, (first + SEND_BLOCKS) * CAP)
         moved[part, :] = dot(pick[part, :], by_tile[...])
@@ -172,16 +183,8 @@
             rows = slice(block * CAP, (block + 1) * CAP)
             parts = [moved[rows, k * LANES : (k + 1) * LANES] for k in range(NT)]
             send_ref[block, : NT * CAP, :] = jnp.concatenate(parts, axis=0).astype(BF16)
-            groups = [take_lanes(meta, 16 * g, 16, block) for g in range(3)]
-            joined = jnp.where(
-                lane < CAP,
-                groups[0],
-                jnp.where(
-                    lane < 2 * CAP,
-                    pltpu.roll(groups[1], CAP, 1),
-                    jnp.where(lane < 3 * CAP, pltpu.roll(groups[2], 2 * CAP, 1), 0.0),
-                ),
-            )
+            parts = [take_lanes(groups[g], lane, block, g * CAP) for g in range(3)]
+            joined = jnp.where(lane < CAP, parts[0], jnp.where(lane < 2 * CAP, parts[1], parts[2]))
             send_ref[block, NT * CAP :, :] = joined.astype(BF16)
 
 
@@ -192,16 +195,15 @@
 def adjoint_kernel(
     recv_ref, flux_ref, meta_ref, foot_ref, rows_f, sides, hot, weighted, total
 ):
-    meta_ref[...] = jnp.zeros((META, SLOTS), F32)
     lane = lax.broadcasted_iota(I32, (16, LANES), 1)
+    joined = [recv_ref[block, NT * CAP :, :].astype(F32) for block in range(N_WIDE)]
+    for g in range(3):
+        for c, column in enumerate(join_lanes(joined, g * CAP, lane)):
+            meta_ref[16 * g : 16 * (g + 1), c * LANES : (c + 1) * LANES] = column
     for block in range(N_WIDE):
         values = recv_ref[block, : NT * CAP, :].astype(F32)
         for k in range(NT):
             rows_f[k, block * CAP : (block + 1) * CAP, :] = values[k * CAP : (k + 1) * CAP, :]
-        joined = recv_ref[block, NT * CAP :, :].astype(F32)
-        for g in range(3):
-            piece = joined if g == 0 else pltpu.roll(joined, LANES - g * CAP, 1)
-            add_lanes(meta_ref, 16 * g, 16, block, jnp.where(lane < CAP, piece, 0.0))
     upper = jnp.where(meta_ref[8:16, :] >= HALF, 1.0, 0.0).astype(BF16)
     spread_to = lax.broadcasted_iota(I32, (8, NT * LANES), 1) // LANES
     spread_to = spread_to == lax.broadcasted_iota(I32, (8, NT * LANES), 0)
@@ -318,8 +320,9 @@
         axis=1,
     )
     lane = lax.broadcasted_iota(I32, (RHS, LANES), 1)
+    columns = columns_of(model, 0, RHS)
     for block in range(N_WIDE):
-        send_ref[block] = jnp.where(lane < CAP, take_lanes(model, 0, RHS, block), gram)
+        send_ref[block] = jnp.where(lane < CAP, take_lanes(columns, lane, block, 0), gram)
 
 
 def sum_kernel(home_ref, out_ref):
@@ -353,13 +356,11 @@
 
 
 def update_kernel(
-    gram_ref, home_ref, slot_ref, err_ref, sol_ref, res_ref, dir_ref, sol_out, res_out, dir_out, lined
+    gram_ref, home_ref, slot_ref, err_ref, sol_ref, res_ref, dir_ref, sol_out, res_out, dir_out
 ):
-    lined[...] = jnp.zeros((RHS, SLOTS), F32)
     lane = lax.broadcasted_iota(I32, (RHS, LANES), 1)
-    for block in range(N_WIDE):
-        add_lanes(lined, 0, RHS, block, jnp.where(lane < CAP, home_ref[block], 0.0))
-    high, rest = split_two(lined[...])
+    pieces = [home_ref[block] for block in range(N_WIDE)]
+    high, rest = split_two(jnp.concatenate(join_lanes(pieces, 0, lane), axis=1))
     middle, low = split_two(rest)
     parts = jnp.concatenate([high, middle, low], axis=0).astype(BF16)
     placed = dot(parts, slot_matrix(slot_ref[...]))
@@ -547,7 +548,7 @@
                 update_kernel,
                 [VMEM] * 7,
                 [((RHS, OBS_DEV), F32)] * 3,
-                [vmem((RHS, SLOTS), F32)],
+                [],
                 2 * 24 * SLOTS * OBS_DEV,
                 28 * RHS * OBS_DEV,
             )(grams, home, slot, errors, solution, residual, direction)

time: 136 us -> 136 us (level)
  no operation moved by 1% of the time
where the time goes in v6:
time: 136 us; the launch traced here: 135 us
  blocking collectives  123 us (90%)
  Pallas kernels  11.2 us (8%)
    all_to_all x6, blocking collectives, exchange(): lax.all_to_all(array, axis, split_axis=0, concat_axis=0, tiled=True, axis...  123 us
    pallas_call x1, Pallas kernels, on_device(): call(pack_kernel, [HBM] * 6, [((N_WIDE, PAYLOAD, LANES), BF16), ((1, OBS_...  3.09 us
    pallas_call x1, Pallas kernels, on_device(): call(adjoint_kernel, [VMEM], [((N_NARROW, CELLS, LANES), BF16), ((META, S...  2.78 us

profile of v6, /device:TPU:1, one launch (start us, length us, event | category | flops | bytes accessed | tf_op | source)
XLA Modules:
  0.0 135.2 jit_solution(13636633646647751525)
XLA Ops:
  0.6 3.1 %pack.1 = (bf16[32,176,128]{2,1,0:T(8,128)(2,1)S(1)}, s32[1,512]{1,0:T(1,128)S(1)}) custom-call(s32[1,512]{1,0:T(1,128)} %bitcast.17, s32[4,512]{1,0:T(4,128)} %bitcast.16, bf16[2048,128]{1,0:T(8,128)(2,1)} %bitcast.15, f32[8,512]{1,0:T(8,128)} %dir_ref.3, f32[8,512]{1,0:T(8,128)} %res_ref.3, f32[1,512]{1,0:T(1,128)} %bitcast.12), custom_call_target="tpu_custom_call" | custom-call | flops 671088640 | bytes 1310720 | tf_op jit(solution)/shard_map/pack/pallas_call | solution.py:440
  3.7 48.1 %all_to_all.30.recv_ref = bf16[32,176,128]{2,1,0:T(8,128)(2,1)S(1)} all-to-all(bf16[32,176,128]{2,1,0:T(8,128)(2,1)S(1)} %get-tuple-element.8), channel_id=1, replica_groups=mesh['wide'=32,'narrow'=8] {'wide'}, dimensions={0} | all-to-all | bytes 2883584 | tf_op jit(solution)/shard_map/route/all_to_all | solution.py:408
  51.8 0.0 copy-start.1
  51.8 2.8 %adjoint.1 = (bf16[8,160,128]{2,1,0:T(8,128)(2,1)S(1)}, f32[48,1280]{1,0:T(8,128)S(1)}, bf16[4,1280,256]{2,1,0:T(8,128)(2,1)S(1)}) custom-call(bf16[32,176,128]{2,1,0:T(8,128)(2,1)S(1)} %all_to_all.30.recv_ref), custom_call_target="tpu_custom_call" | custom-call | flops 1677721600 | bytes 2621440 | tf_op jit(solution)/shard_map/adjoint/pallas_call | solution.py:470
  54.6 0.0 copy-start
  54.6 19.1 %all_to_all.31.flux_ref = bf16[8,160,128]{2,1,0:T(8,128)(2,1)S(1)} all-to-all(bf16[8,160,128]{2,1,0:T(8,128)(2,1)S(1)} %get-tuple-element.9), channel_id=1, replica_groups={{0,34,68,102,129,163,197,231},{8,42,76,110,137,171,205,239},{16,50,84,1..., dimensions={0} | all-to-all | bytes 655360 | tf_op jit(solution)/shard_map/to_rhs/all_to_all | solution.py:408
  73.7 0.0 copy-done.1
  73.7 0.0 copy-start.2
  73.7 0.0 copy-start.3
  73.7 0.0 copy-start.5
  73.7 0.0 copy-start.6
  73.7 0.4 lat_mix.1
  74.2 16.4 %all_to_all.32 = bf16[32,40,128]{2,1,0:T(8,128)(2,1)S(1)} all-to-all(bf16[32,40,128]{2,1,0:T(8,128)(2,1)S(1)} %bitcast.10), channel_id=1, replica_groups={{0,8,16,24,1,9,17,25,2,10,18,26,3,11,19,27,4,12,20,28,5,13,21,29,6,14,2..., dimensions={0} | all-to-all | bytes 655360 | tf_op jit(solution)/shard_map/to_days/all_to_all | solution.py:408
  90.6 0.0 copy-done
  90.6 0.5 day_mix.1
  91.1 15.7 %all_to_all.33 = bf16[32,40,128]{2,1,0:T(8,128)(2,1)S(1)} all-to-all(bf16[32,40,128]{2,1,0:T(8,128)(2,1)S(1)} %bitcast.9), channel_id=1, replica_groups=mesh['wide'=32,'narrow'=8] {'wide'}, dimensions={0} | all-to-all | bytes 655360 | tf_op jit(solution)/shard_map/to_windows/all_to_all | solution.py:408
  106.7 0.0 copy-done.2
  106.7 0.0 copy-done.3
  106.7 0.0 copy-done.5
  106.7 0.0 copy-done.6
  106.7 0.0 copy-start.4
  106.8 2.5 %forward.1 = f32[32,8,128]{2,1,0:T(8,128)S(1)} custom-call(bf16[128,128]{1,0:T(8,128)(2,1)S(1)} %copy-done.6, bf16[1280,128]{1,0:T(8,128)(2,1)S(1)} %bitcast.11, bf16[4,1280,256]{2,1,0:T(8,128)(2,1)S(1)} %get-tuple-element.10.foot_ref, f32[48,1280]{1,0:T(8,128)S(1)} %get-tuple-element.11.meta_ref, f32[8,512]{1,0:T(8,128)S(1)} %copy-done.2, ...), custom_call_target="tpu_custom_call" | custom-call | flops 1677721600 | bytes 2621440 | tf_op jit(solution)/shard_map/forward/pallas_call | solution.py:513
  109.3 14.1 %all_to_all.34.home_ref = f32[32,8,128]{2,1,0:T(8,128)S(1)} all-to-all(f32[32,8,128]{2,1,0:T(8,128)S(1)} %forward.1), channel_id=1, replica_groups=mesh['wide'=32,'narrow'=8] {'wide'}, dimensions={0} | all-to-all | bytes 262144 | tf_op jit(solution)/shard_map/home/all_to_all | solution.py:408
  123.4 9.9 %all_to_all.35.gram_ref = f32[8,8,128]{2,1,0:T(8,128)S(1)} all-to-all(f32[8,8,128]{2,1,0:T(8,128)S(1)} %gram_sum.1), channel_id=1, replica_groups=mesh['wide'=32,'narrow'=8] {'narrow'}, dimensions={0} | all-to-all | bytes 65536 | tf_op jit(solution)/shard_map/gram_sum/all_to_all | solution.py:408
  133.4 0.0 copy-done.4
  133.4 1.8 %update.1 = (f32[8,512]{1,0:T(8,128)}, f32[8,512]{1,0:T(8,128)}, f32[8,512]{1,0:T(8,128)}) custom-call(f32[8,8,128]{2,1,0:T(8,128)S(1)} %all_to_all.35.gram_ref, f32[32,8,128]{2,1,0:T(8,128)S(1)} %all_to_all.34.home_ref, s32[1,512]{1,0:T(1,128)S(1)} %get-tuple-element.12.slot_ref, f32[1,512]{1,0:T(1,128)S(1)} %bitcast.14, f32[8,512]{1,0:T(8,128)S(1)} %copy-done.4, ...), custom_call_target="tpu_custom_call" | custom-call | flops 31457280 | bytes 114688 | tf_op jit(solution)/shard_map/update/pallas_call | solution.py:547
  (1 shorter events, 0.0 us)
Async XLA Ops:
  51.8 21.9 %copy-start.1 = (bf16[128,128]{1,0:T(8,128)(2,1)S(1)}, bf16[128,128]{1,0:T(8,128)(2,1)}, u32[]{:S(2)}) copy-start(bf16[128,128]{1,0:T(8,128)(2,1)} %mix_ref.2) | copy-start | bytes 98308
  54.6 36.0 %copy-start = (bf16[320,320]{1,0:T(8,128)(2,1)S(1)}, bf16[320,320]{1,0:T(8,128)(2,1)}, u32[]{:S(2)}) copy-start(bf16[320,320]{1,0:T(8,128)(2,1)} %mix_ref.3) | copy-start | bytes 614404
  73.7 33.0 %copy-start.2 = (f32[8,512]{1,0:T(8,128)S(1)}, f32[8,512]{1,0:T(8,128)}, u32[]{:S(2)}) copy-start(f32[8,512]{1,0:T(8,128)} %dir_ref.3) | copy-start | bytes 49156
  73.7 33.0 %copy-start.3 = (f32[8,512]{1,0:T(8,128)S(1)}, f32[8,512]{1,0:T(8,128)}, u32[]{:S(2)}) copy-start(f32[8,512]{1,0:T(8,128)} %res_ref.3) | copy-start | bytes 49156
  73.7 33.0 %copy-start.5 = (f32[512]{0:T(512)S(1)}, f32[512]{0:T(512)}, u32[]{:S(2)}) copy-start(f32[512]{0:T(512)} %param.13) | copy-start | bytes 6148
  73.7 33.0 %copy-start.6 = (bf16[128,128]{1,0:T(8,128)(2,1)S(1)}, bf16[128,128]{1,0:T(8,128)(2,1)}, u32[]{:S(2)}) copy-start(bf16[128,128]{1,0:T(8,128)(2,1)} %lon_ref.1) | copy-start | bytes 98308
  106.7 26.6 %copy-start.4 = (f32[8,512]{1,0:T(8,128)S(1)}, f32[8,512]{1,0:T(8,128)}, u32[]{:S(2)}) copy-start(f32[8,512]{1,0:T(8,128)} %sol_ref.1) | copy-start | bytes 49156

commit v7 on v6

--- a/solution.py
+++ b/solution.py
@@ -130,7 +130,8 @@
         I32, (OBS_DEV, OBS_DEV), 1
     )
     earlier = jnp.where(earlier, 1.0, 0.0).astype(BF16)
-    copies[0].wait()
+    for copy in copies:
+        copy.wait()
     window = window_ref[...]
     turn = here()[1]
     owner = ((turn - (window >> 2)) & 7) * QUAD + (window & 3)
@@ -141,8 +142,6 @@
     slot = owner * CAP + position
     slot_ref[...] = slot
     pick[...] = slot_matrix(slot)
-    for copy in copies[2:]:
-        copy.wait()
     tile = tiles_ref[...]
     day, row = tile >> 4, tile & 15
     cell = ((row >> 2) * CHUNK + day * QUAD + (row & 3)).astype(F32)
@@ -167,7 +166,6 @@
     out_row = lax.broadcasted_iota(I32, (group, group), 0)
     in_row = lax.broadcasted_iota(I32, (group, group), 1)
     sort = jnp.where(in_row == out_row % share * NT + out_row // share, 1.0, 0.0).astype(BF16)
-    copies[1].wait()
     for g in range(OBS_DEV // share):
         rows = dot(sort, foot_ref[g * group : (g + 1) * group, :]).astype(BF16)
         for k in range(NT):
@@ -193,40 +191,35 @@
 
 
 def adjoint_kernel(
-    recv_ref, flux_ref, meta_ref, foot_ref, rows_f, sides, hot, weighted, total
+    recv_ref, flux_ref, meta_ref, foot_ref, hot, weighted, total
 ):
     lane = lax.broadcasted_iota(I32, (16, LANES), 1)
     joined = [recv_ref[block, NT * CAP :, :].astype(F32) for block in range(N_WIDE)]
     for g in range(3):
         for c, column in enumerate(join_lanes(joined, g * CAP, lane)):
             meta_ref[16 * g : 16 * (g + 1), c * LANES : (c + 1) * LANES] = column
-    for block in range(N_WIDE):
-        values = recv_ref[block, : NT * CAP, :].astype(F32)
-        for k in range(NT):
-            rows_f[k, block * CAP : (block + 1) * CAP, :] = values[k * CAP : (k + 1) * CAP, :]
-    upper = jnp.where(meta_ref[8:16, :] >= HALF, 1.0, 0.0).astype(BF16)
-    spread_to = lax.broadcasted_iota(I32, (8, NT * LANES), 1) // LANES
-    spread_to = spread_to == lax.broadcasted_iota(I32, (8, NT * LANES), 0)
-    sides[...] = lax.dot_general(
-        upper,
-        jnp.where(spread_to, 1.0, 0.0).astype(BF16),
-        (((0,), (0,)), ((), ())),
-        preferred_element_type=F32,
-    )
+    upper = jnp.transpose(jnp.where(meta_ref[8:16, :] >= HALF, 1.0, 0.0))
     cells = lax.broadcasted_iota(I32, (HALF, SLOTS), 0)
     for k in range(NT):
-        is_upper = sides[:, k * LANES : (k + 1) * LANES] > 0.5
-        foot = rows_f[k]
-        foot_ref[k, :, :LANES] = jnp.where(is_upper, 0.0, foot).astype(BF16)
-        foot_ref[k, :, LANES:] = jnp.where(is_upper, foot, 0.0).astype(BF16)
-        hot[...] = jnp.where(cells == half_cell(meta_ref[8 + k : 9 + k, :]), 1.0, 0.0).astype(BF16)
+        low = k * CAP // 16 * 16
+        for pair in range(0, N_WIDE, 2):
+            rows = slice(pair * CAP, (pair + 2) * CAP)
+            pieces = [
+                recv_ref[block, low : low + 48, :].astype(F32)[k * CAP - low :][:CAP]
+                for block in (pair, pair + 1)
+            ]
+            foot = jnp.concatenate(pieces, axis=0)
+            is_upper = jnp.broadcast_to(upper[rows, k : k + 1], (2 * CAP, LANES)) > 0.5
+            foot_ref[k, rows, :LANES] = jnp.where(is_upper, 0.0, foot).astype(BF16)
+            foot_ref[k, rows, LANES:] = jnp.where(is_upper, foot, 0.0).astype(BF16)
+        hot[k] = jnp.where(cells == half_cell(meta_ref[8 + k : 9 + k, :]), 1.0, 0.0).astype(BF16)
         for r in range(RHS):
             row = jnp.broadcast_to(meta_ref[r : r + 1, :], (16, SLOTS)).astype(BF16)
             for t in range(HALF // 16):
-                weighted[r * HALF + t * 16 : r * HALF + (t + 1) * 16, :] = (
-                    hot[t * 16 : (t + 1) * 16, :] * row
+                weighted[k, r * HALF + t * 16 : r * HALF + (t + 1) * 16, :] = (
+                    hot[k, t * 16 : (t + 1) * 16, :] * row
                 )
-        product = dot(weighted[...], foot_ref[k])
+        product = dot(weighted[k], foot_ref[k])
         if k == 0:
             total[...] = product
         else:
@@ -476,10 +469,8 @@
                 ((NT, SLOTS, 2 * LANES), BF16),
             ],
             [
-                vmem((NT, SLOTS, LANES), F32),
-                vmem((SLOTS, NT * LANES), F32),
-                vmem((HALF, SLOTS), BF16),
-                vmem((ROWS // 2, SLOTS), BF16),
+                vmem((NT, HALF, SLOTS), BF16),
+                vmem((NT, ROWS // 2, SLOTS), BF16),
                 vmem((ROWS // 2, 2 * LANES), F32),
             ],
             2 * ROWS * NT * SLOTS * LANES,

time: 136 us -> 135 us (level)
  no operation moved by 1% of the time
where the time goes in v7:
time: 135 us
  blocking collectives  123 us (91%)
  Pallas kernels  10.8 us (8%)
    all_to_all x6, blocking collectives, exchange(): lax.all_to_all(array, axis, split_axis=0, concat_axis=0, tiled=True, axis...  123 us
    pallas_call x1, Pallas kernels, on_device(): call(pack_kernel, [HBM] * 6, [((N_WIDE, PAYLOAD, LANES), BF16), ((1, OBS_...  2.95 us

profile of v7, /device:TPU:1, one launch (start us, length us, event | category | flops | bytes accessed | tf_op | source)
XLA Modules:
  0.0 134.8 jit_solution(17461571159358789294)
XLA Ops:
  0.6 3.0 %pack.1 = (bf16[32,176,128]{2,1,0:T(8,128)(2,1)S(1)}, s32[1,512]{1,0:T(1,128)S(1)}) custom-call(s32[1,512]{1,0:T(1,128)} %bitcast.17, s32[4,512]{1,0:T(4,128)} %bitcast.16, bf16[2048,128]{1,0:T(8,128)(2,1)} %bitcast.15, f32[8,512]{1,0:T(8,128)} %dir_ref.3, f32[8,512]{1,0:T(8,128)} %res_ref.3, f32[1,512]{1,0:T(1,128)} %bitcast.12), custom_call_target="tpu_custom_call" | custom-call | flops 671088640 | bytes 1310720 | tf_op jit(solution)/shard_map/pack/pallas_call | solution.py:433
  3.6 48.1 %all_to_all.30.recv_ref = bf16[32,176,128]{2,1,0:T(8,128)(2,1)S(1)} all-to-all(bf16[32,176,128]{2,1,0:T(8,128)(2,1)S(1)} %get-tuple-element.8), channel_id=1, replica_groups=mesh['wide'=32,'narrow'=8] {'wide'}, dimensions={0} | all-to-all | bytes 2883584 | tf_op jit(solution)/shard_map/route/all_to_all | solution.py:401
  51.7 0.0 copy-start.1
  51.7 2.6 %adjoint.1 = (bf16[8,160,128]{2,1,0:T(8,128)(2,1)S(1)}, f32[48,1280]{1,0:T(8,128)S(1)}, bf16[4,1280,256]{2,1,0:T(8,128)(2,1)S(1)}) custom-call(bf16[32,176,128]{2,1,0:T(8,128)(2,1)S(1)} %all_to_all.30.recv_ref), custom_call_target="tpu_custom_call" | custom-call | flops 1677721600 | bytes 2621440 | tf_op jit(solution)/shard_map/adjoint/pallas_call | solution.py:463
  54.2 0.0 copy-start
  54.3 19.1 %all_to_all.31.flux_ref = bf16[8,160,128]{2,1,0:T(8,128)(2,1)S(1)} all-to-all(bf16[8,160,128]{2,1,0:T(8,128)(2,1)S(1)} %get-tuple-element.9), channel_id=1, replica_groups={{0,34,68,102,129,163,197,231},{8,42,76,110,137,171,205,239},{16,50,84,1..., dimensions={0} | all-to-all | bytes 655360 | tf_op jit(solution)/shard_map/to_rhs/all_to_all | solution.py:401
  73.3 0.0 copy-done.1
  73.3 0.0 copy-start.2
  73.3 0.0 copy-start.3
  73.3 0.0 copy-start.5
  73.3 0.0 copy-start.6
  73.4 0.4 lat_mix.1
  73.8 16.4 %all_to_all.32 = bf16[32,40,128]{2,1,0:T(8,128)(2,1)S(1)} all-to-all(bf16[32,40,128]{2,1,0:T(8,128)(2,1)S(1)} %bitcast.10), channel_id=1, replica_groups={{0,8,16,24,1,9,17,25,2,10,18,26,3,11,19,27,4,12,20,28,5,13,21,29,6,14,2..., dimensions={0} | all-to-all | bytes 655360 | tf_op jit(solution)/shard_map/to_days/all_to_all | solution.py:401
  90.2 0.0 copy-done
  90.2 0.5 day_mix.1
  90.7 15.7 %all_to_all.33 = bf16[32,40,128]{2,1,0:T(8,128)(2,1)S(1)} all-to-all(bf16[32,40,128]{2,1,0:T(8,128)(2,1)S(1)} %bitcast.9), channel_id=1, replica_groups=mesh['wide'=32,'narrow'=8] {'wide'}, dimensions={0} | all-to-all | bytes 655360 | tf_op jit(solution)/shard_map/to_windows/all_to_all | solution.py:401
  106.4 0.0 copy-done.2
  106.4 0.0 copy-done.3
  106.4 0.0 copy-done.5
  106.4 0.0 copy-done.6
  106.4 0.0 copy-start.4
  106.4 2.5 %forward.1 = f32[32,8,128]{2,1,0:T(8,128)S(1)} custom-call(bf16[128,128]{1,0:T(8,128)(2,1)S(1)} %copy-done.6, bf16[1280,128]{1,0:T(8,128)(2,1)S(1)} %bitcast.11, bf16[4,1280,256]{2,1,0:T(8,128)(2,1)S(1)} %get-tuple-element.10.foot_ref, f32[48,1280]{1,0:T(8,128)S(1)} %get-tuple-element.11.meta_ref, f32[8,512]{1,0:T(8,128)S(1)} %copy-done.2, ...), custom_call_target="tpu_custom_call" | custom-call | flops 1677721600 | bytes 2621440 | tf_op jit(solution)/shard_map/forward/pallas_call | solution.py:504
  108.9 14.1 %all_to_all.34.home_ref = f32[32,8,128]{2,1,0:T(8,128)S(1)} all-to-all(f32[32,8,128]{2,1,0:T(8,128)S(1)} %forward.1), channel_id=1, replica_groups=mesh['wide'=32,'narrow'=8] {'wide'}, dimensions={0} | all-to-all | bytes 262144 | tf_op jit(solution)/shard_map/home/all_to_all | solution.py:401
  123.1 9.9 %all_to_all.35.gram_ref = f32[8,8,128]{2,1,0:T(8,128)S(1)} all-to-all(f32[8,8,128]{2,1,0:T(8,128)S(1)} %gram_sum.1), channel_id=1, replica_groups=mesh['wide'=32,'narrow'=8] {'narrow'}, dimensions={0} | all-to-all | bytes 65536 | tf_op jit(solution)/shard_map/gram_sum/all_to_all | solution.py:401
  133.0 0.0 copy-done.4
  133.0 1.8 %update.1 = (f32[8,512]{1,0:T(8,128)}, f32[8,512]{1,0:T(8,128)}, f32[8,512]{1,0:T(8,128)}) custom-call(f32[8,8,128]{2,1,0:T(8,128)S(1)} %all_to_all.35.gram_ref, f32[32,8,128]{2,1,0:T(8,128)S(1)} %all_to_all.34.home_ref, s32[1,512]{1,0:T(1,128)S(1)} %get-tuple-element.12.slot_ref, f32[1,512]{1,0:T(1,128)S(1)} %bitcast.14, f32[8,512]{1,0:T(8,128)S(1)} %copy-done.4, ...), custom_call_target="tpu_custom_call" | custom-call | flops 31457280 | bytes 114688 | tf_op jit(solution)/shard_map/update/pallas_call | solution.py:538
  (1 shorter events, 0.0 us)
Async XLA Ops:
  51.7 21.6 %copy-start.1 = (bf16[128,128]{1,0:T(8,128)(2,1)S(1)}, bf16[128,128]{1,0:T(8,128)(2,1)}, u32[]{:S(2)}) copy-start(bf16[128,128]{1,0:T(8,128)(2,1)} %mix_ref.2) | copy-start | bytes 98308
  54.2 36.0 %copy-start = (bf16[320,320]{1,0:T(8,128)(2,1)S(1)}, bf16[320,320]{1,0:T(8,128)(2,1)}, u32[]{:S(2)}) copy-start(bf16[320,320]{1,0:T(8,128)(2,1)} %mix_ref.3) | copy-start | bytes 614404
  73.3 33.0 %copy-start.2 = (f32[8,512]{1,0:T(8,128)S(1)}, f32[8,512]{1,0:T(8,128)}, u32[]{:S(2)}) copy-start(f32[8,512]{1,0:T(8,128)} %dir_ref.3) | copy-start | bytes 49156
  73.3 33.0 %copy-start.3 = (f32[8,512]{1,0:T(8,128)S(1)}, f32[8,512]{1,0:T(8,128)}, u32[]{:S(2)}) copy-start(f32[8,512]{1,0:T(8,128)} %res_ref.3) | copy-start | bytes 49156
  73.3 33.0 %copy-start.5 = (f32[512]{0:T(512)S(1)}, f32[512]{0:T(512)}, u32[]{:S(2)}) copy-start(f32[512]{0:T(512)} %param.13) | copy-start | bytes 6148
  73.3 33.0 %copy-start.6 = (bf16[128,128]{1,0:T(8,128)(2,1)S(1)}, bf16[128,128]{1,0:T(8,128)(2,1)}, u32[]{:S(2)}) copy-start(bf16[128,128]{1,0:T(8,128)(2,1)} %lon_ref.1) | copy-start | bytes 98308
  106.4 26.6 %copy-start.4 = (f32[8,512]{1,0:T(8,128)S(1)}, f32[8,512]{1,0:T(8,128)}, u32[]{:S(2)}) copy-start(f32[8,512]{1,0:T(8,128)} %sol_ref.1) | copy-start | bytes 49156

commit v8 on v7

--- a/solution.py
+++ b/solution.py
@@ -242,15 +242,16 @@
             columns[d, pl.ds(a, N_WIDE, stride=QUAD), :] = rows_f[
                 pl.ds(d * QUAD + a, N_WIDE, stride=CHUNK), :
             ]
-    side_by_side = jnp.concatenate([columns[d].astype(BF16) for d in range(DAY_DEV)], axis=1)
+    side_by_side = [columns[d, :LAT, :].astype(BF16) for d in range(DAY_DEV)]
+    side_by_side = jnp.concatenate(side_by_side, axis=1)
     mixed = dot(mix_ref[...], side_by_side)
     for d in range(DAY_DEV):
-        columns[d] = mixed[:, d * LANES : (d + 1) * LANES]
+        columns[d, :LAT, :] = mixed[:, d * LANES : (d + 1) * LANES]
         for a in range(QUAD):
             rows_f[pl.ds(d * QUAD + a, N_WIDE, stride=CHUNK), :] = columns[
                 d, pl.ds(a, N_WIDE, stride=QUAD), :
             ]
-    out_ref[...] = rows_f[...].astype(BF16)
+    out_ref[...] = rows_f[:ROWS, :].astype(BF16)
 
 
 def day_kernel(mix_ref, flux_ref, out_ref, rows_f, columns):
@@ -483,7 +484,7 @@
             lat_kernel,
             [VMEM, VMEM],
             [((ROWS, LANES), BF16)],
-            [vmem((ROWS, LANES), F32), vmem((DAY_DEV, LAT, LANES), F32)],
+            [vmem((ROWS + CHUNK, LANES), F32), vmem((DAY_DEV, LAT + 8, LANES), F32)],
             2 * LAT * LAT * DAY_DEV * LANES,
             4 * ROWS * LANES,
         )(spatial_lat, by_rhs)
@@ -494,7 +495,7 @@
             day_kernel,
             [VMEM, VMEM],
             [((N_NARROW, CELLS, LANES), BF16)],
-            [vmem((ROWS, LANES), F32), vmem((DAYS, QUAD * LANES), BF16)],
+            [vmem((ROWS + 8, LANES), F32), vmem((DAYS, QUAD * LANES), BF16)],
             2 * DAYS * DAYS * QUAD * LANES,
             4 * ROWS * LANES,
         )(temporal, by_day.reshape(N_NARROW, CELLS, LANES))

time: 135 us -> 135 us (level)
  no operation moved by 1% of the time
where the time goes in v8:
time: 135 us
  blocking collectives  123 us (91%)
  Pallas kernels  10.8 us (8%)
    all_to_all x6, blocking collectives, exchange(): lax.all_to_all(array, axis, split_axis=0, concat_axis=0, tiled=True, axis...  123 us
    pallas_call x1, Pallas kernels, on_device(): call(pack_kernel, [HBM] * 6, [((N_WIDE, PAYLOAD, LANES), BF16), ((1, OBS_...  2.95 us

profile of v8, /device:TPU:1, one launch (start us, length us, event | category | flops | bytes accessed | tf_op | source)
XLA Modules:
  0.0 134.8 jit_solution(2304724789306355945)
XLA Ops:
  0.6 3.0 %pack.1 = (bf16[32,176,128]{2,1,0:T(8,128)(2,1)S(1)}, s32[1,512]{1,0:T(1,128)S(1)}) custom-call(s32[1,512]{1,0:T(1,128)} %bitcast.17, s32[4,512]{1,0:T(4,128)} %bitcast.16, bf16[2048,128]{1,0:T(8,128)(2,1)} %bitcast.15, f32[8,512]{1,0:T(8,128)} %dir_ref.3, f32[8,512]{1,0:T(8,128)} %res_ref.3, f32[1,512]{1,0:T(1,128)} %bitcast.12), custom_call_target="tpu_custom_call" | custom-call | flops 671088640 | bytes 1310720 | tf_op jit(solution)/shard_map/pack/pallas_call | solution.py:434
  3.6 48.1 %all_to_all.30.recv_ref = bf16[32,176,128]{2,1,0:T(8,128)(2,1)S(1)} all-to-all(bf16[32,176,128]{2,1,0:T(8,128)(2,1)S(1)} %get-tuple-element.8), channel_id=1, replica_groups=mesh['wide'=32,'narrow'=8] {'wide'}, dimensions={0} | all-to-all | bytes 2883584 | tf_op jit(solution)/shard_map/route/all_to_all | solution.py:402
  51.7 0.0 copy-start.1
  51.7 2.6 %adjoint.1 = (bf16[8,160,128]{2,1,0:T(8,128)(2,1)S(1)}, f32[48,1280]{1,0:T(8,128)S(1)}, bf16[4,1280,256]{2,1,0:T(8,128)(2,1)S(1)}) custom-call(bf16[32,176,128]{2,1,0:T(8,128)(2,1)S(1)} %all_to_all.30.recv_ref), custom_call_target="tpu_custom_call" | custom-call | flops 1677721600 | bytes 2621440 | tf_op jit(solution)/shard_map/adjoint/pallas_call | solution.py:464
  54.2 0.0 copy-start
  54.3 19.1 %all_to_all.31.flux_ref = bf16[8,160,128]{2,1,0:T(8,128)(2,1)S(1)} all-to-all(bf16[8,160,128]{2,1,0:T(8,128)(2,1)S(1)} %get-tuple-element.9), channel_id=1, replica_groups={{0,34,68,102,129,163,197,231},{8,42,76,110,137,171,205,239},{16,50,84,1..., dimensions={0} | all-to-all | bytes 655360 | tf_op jit(solution)/shard_map/to_rhs/all_to_all | solution.py:402
  73.3 0.0 copy-done.1
  73.3 0.0 copy-start.2
  73.3 0.0 copy-start.3
  73.3 0.0 copy-start.5
  73.3 0.0 copy-start.6
  73.4 0.4 lat_mix.1
  73.8 16.4 %all_to_all.32 = bf16[32,40,128]{2,1,0:T(8,128)(2,1)S(1)} all-to-all(bf16[32,40,128]{2,1,0:T(8,128)(2,1)S(1)} %bitcast.10), channel_id=1, replica_groups={{0,8,16,24,1,9,17,25,2,10,18,26,3,11,19,27,4,12,20,28,5,13,21,29,6,14,2..., dimensions={0} | all-to-all | bytes 655360 | tf_op jit(solution)/shard_map/to_days/all_to_all | solution.py:402
  90.2 0.0 copy-done
  90.2 0.5 day_mix.1
  90.7 15.7 %all_to_all.33 = bf16[32,40,128]{2,1,0:T(8,128)(2,1)S(1)} all-to-all(bf16[32,40,128]{2,1,0:T(8,128)(2,1)S(1)} %bitcast.9), channel_id=1, replica_groups=mesh['wide'=32,'narrow'=8] {'wide'}, dimensions={0} | all-to-all | bytes 655360 | tf_op jit(solution)/shard_map/to_windows/all_to_all | solution.py:402
  106.4 0.0 copy-done.2
  106.4 0.0 copy-done.3
  106.4 0.0 copy-done.5
  106.4 0.0 copy-done.6
  106.4 0.0 copy-start.4
  106.4 2.5 %forward.1 = f32[32,8,128]{2,1,0:T(8,128)S(1)} custom-call(bf16[128,128]{1,0:T(8,128)(2,1)S(1)} %copy-done.6, bf16[1280,128]{1,0:T(8,128)(2,1)S(1)} %bitcast.11, bf16[4,1280,256]{2,1,0:T(8,128)(2,1)S(1)} %get-tuple-element.10.foot_ref, f32[48,1280]{1,0:T(8,128)S(1)} %get-tuple-element.11.meta_ref, f32[8,512]{1,0:T(8,128)S(1)} %copy-done.2, ...), custom_call_target="tpu_custom_call" | custom-call | flops 1677721600 | bytes 2621440 | tf_op jit(solution)/shard_map/forward/pallas_call | solution.py:505
  108.9 14.1 %all_to_all.34.home_ref = f32[32,8,128]{2,1,0:T(8,128)S(1)} all-to-all(f32[32,8,128]{2,1,0:T(8,128)S(1)} %forward.1), channel_id=1, replica_groups=mesh['wide'=32,'narrow'=8] {'wide'}, dimensions={0} | all-to-all | bytes 262144 | tf_op jit(solution)/shard_map/home/all_to_all | solution.py:402
  123.1 9.9 %all_to_all.35.gram_ref = f32[8,8,128]{2,1,0:T(8,128)S(1)} all-to-all(f32[8,8,128]{2,1,0:T(8,128)S(1)} %gram_sum.1), channel_id=1, replica_groups=mesh['wide'=32,'narrow'=8] {'narrow'}, dimensions={0} | all-to-all | bytes 65536 | tf_op jit(solution)/shard_map/gram_sum/all_to_all | solution.py:402
  133.0 0.0 copy-done.4
  133.0 1.8 %update.1 = (f32[8,512]{1,0:T(8,128)}, f32[8,512]{1,0:T(8,128)}, f32[8,512]{1,0:T(8,128)}) custom-call(f32[8,8,128]{2,1,0:T(8,128)S(1)} %all_to_all.35.gram_ref, f32[32,8,128]{2,1,0:T(8,128)S(1)} %all_to_all.34.home_ref, s32[1,512]{1,0:T(1,128)S(1)} %get-tuple-element.12.slot_ref, f32[1,512]{1,0:T(1,128)S(1)} %bitcast.14, f32[8,512]{1,0:T(8,128)S(1)} %copy-done.4, ...), custom_call_target="tpu_custom_call" | custom-call | flops 31457280 | bytes 114688 | tf_op jit(solution)/shard_map/update/pallas_call | solution.py:539
  (1 shorter events, 0.0 us)
Async XLA Ops:
  51.7 21.6 %copy-start.1 = (bf16[128,128]{1,0:T(8,128)(2,1)S(1)}, bf16[128,128]{1,0:T(8,128)(2,1)}, u32[]{:S(2)}) copy-start(bf16[128,128]{1,0:T(8,128)(2,1)} %mix_ref.2) | copy-start | bytes 98308
  54.2 36.0 %copy-start = (bf16[320,320]{1,0:T(8,128)(2,1)S(1)}, bf16[320,320]{1,0:T(8,128)(2,1)}, u32[]{:S(2)}) copy-start(bf16[320,320]{1,0:T(8,128)(2,1)} %mix_ref.3) | copy-start | bytes 614404
  73.3 33.0 %copy-start.2 = (f32[8,512]{1,0:T(8,128)S(1)}, f32[8,512]{1,0:T(8,128)}, u32[]{:S(2)}) copy-start(f32[8,512]{1,0:T(8,128)} %dir_ref.3) | copy-start | bytes 49156
  73.3 33.0 %copy-start.3 = (f32[8,512]{1,0:T(8,128)S(1)}, f32[8,512]{1,0:T(8,128)}, u32[]{:S(2)}) copy-start(f32[8,512]{1,0:T(8,128)} %res_ref.3) | copy-start | bytes 49156
  73.3 33.0 %copy-start.5 = (f32[512]{0:T(512)S(1)}, f32[512]{0:T(512)}, u32[]{:S(2)}) copy-start(f32[512]{0:T(512)} %param.13) | copy-start | bytes 6148
  73.3 33.0 %copy-start.6 = (bf16[128,128]{1,0:T(8,128)(2,1)S(1)}, bf16[128,128]{1,0:T(8,128)(2,1)}, u32[]{:S(2)}) copy-start(bf16[128,128]{1,0:T(8,128)(2,1)} %lon_ref.1) | copy-start | bytes 98308
  106.4 26.6 %copy-start.4 = (f32[8,512]{1,0:T(8,128)S(1)}, f32[8,512]{1,0:T(8,128)}, u32[]{:S(2)}) copy-start(f32[8,512]{1,0:T(8,128)} %sol_ref.1) | copy-start | bytes 49156

commit v9 on v8

--- a/solution.py
+++ b/solution.py
@@ -198,20 +198,23 @@
     for g in range(3):
         for c, column in enumerate(join_lanes(joined, g * CAP, lane)):
             meta_ref[16 * g : 16 * (g + 1), c * LANES : (c + 1) * LANES] = column
-    upper = jnp.transpose(jnp.where(meta_ref[8:16, :] >= HALF, 1.0, 0.0))
+    upper = jnp.where(meta_ref[8:12, :] >= HALF, 1.0, 0.0)
+    code = (upper[0:1] + 2.0 * upper[1:2]) + (4.0 * upper[2:3] + 8.0 * upper[3:4])
+    code = jnp.transpose(jnp.broadcast_to(code, (8, SLOTS)))
+    for pair in range(0, N_WIDE, 2):
+        rows = slice(pair * CAP, (pair + 2) * CAP)
+        bits = jnp.broadcast_to(code[rows, 0:1], (2 * CAP, LANES)).astype(I32)
+        first, second = [
+            recv_ref[block, : NT * CAP, :].astype(F32) for block in (pair, pair + 1)
+        ]
+        for k in range(NT):
+            part = slice(k * CAP, (k + 1) * CAP)
+            foot = jnp.concatenate([first[part], second[part]], axis=0)
+            is_upper = (bits & (1 << k)) != 0
+            foot_ref[k, rows, :LANES] = jnp.where(is_upper, 0.0, foot).astype(BF16)
+            foot_ref[k, rows, LANES:] = jnp.where(is_upper, foot, 0.0).astype(BF16)
     cells = lax.broadcasted_iota(I32, (HALF, SLOTS), 0)
     for k in range(NT):
-        low = k * CAP // 16 * 16
-        for pair in range(0, N_WIDE, 2):
-            rows = slice(pair * CAP, (pair + 2) * CAP)
-            pieces = [
-                recv_ref[block, low : low + 48, :].astype(F32)[k * CAP - low :][:CAP]
-                for block in (pair, pair + 1)
-            ]
-            foot = jnp.concatenate(pieces, axis=0)
-            is_upper = jnp.broadcast_to(upper[rows, k : k + 1], (2 * CAP, LANES)) > 0.5
-            foot_ref[k, rows, :LANES] = jnp.where(is_upper, 0.0, foot).astype(BF16)
-            foot_ref[k, rows, LANES:] = jnp.where(is_upper, foot, 0.0).astype(BF16)
         hot[k] = jnp.where(cells == half_cell(meta_ref[8 + k : 9 + k, :]), 1.0, 0.0).astype(BF16)
         for r in range(RHS):
             row = jnp.broadcast_to(meta_ref[r : r + 1, :], (16, SLOTS)).astype(BF16)

time: 135 us -> 135 us (level)
  no operation moved by 1% of the time
where the time goes in v9:
time: 135 us
  blocking collectives  123 us (91%)
  Pallas kernels  11 us (8%)
    all_to_all x6, blocking collectives, exchange(): lax.all_to_all(array, axis, split_axis=0, concat_axis=0, tiled=True, axis...  123 us
    pallas_call x1, Pallas kernels, on_device(): call(pack_kernel, [HBM] * 6, [((N_WIDE, PAYLOAD, LANES), BF16), ((1, OBS_...  2.95 us
    pallas_call x1, Pallas kernels, on_device(): call(adjoint_kernel, [VMEM], [((N_NARROW, CELLS, LANES), BF16), ((META, S...  2.71 us

profile of v9, /device:TPU:1, one launch (start us, length us, event | category | flops | bytes accessed | tf_op | source)
XLA Modules:
  0.0 135.0 jit_solution(1171676228572277779)
XLA Ops:
  0.6 3.0 %pack.1 = (bf16[32,176,128]{2,1,0:T(8,128)(2,1)S(1)}, s32[1,512]{1,0:T(1,128)S(1)}) custom-call(s32[1,512]{1,0:T(1,128)} %bitcast.17, s32[4,512]{1,0:T(4,128)} %bitcast.16, bf16[2048,128]{1,0:T(8,128)(2,1)} %bitcast.15, f32[8,512]{1,0:T(8,128)} %dir_ref.3, f32[8,512]{1,0:T(8,128)} %res_ref.3, f32[1,512]{1,0:T(1,128)} %bitcast.12), custom_call_target="tpu_custom_call" | custom-call | flops 671088640 | bytes 1310720 | tf_op jit(solution)/shard_map/pack/pallas_call | solution.py:437
  3.6 48.1 %all_to_all.30.recv_ref = bf16[32,176,128]{2,1,0:T(8,128)(2,1)S(1)} all-to-all(bf16[32,176,128]{2,1,0:T(8,128)(2,1)S(1)} %get-tuple-element.8), channel_id=1, replica_groups=mesh['wide'=32,'narrow'=8] {'wide'}, dimensions={0} | all-to-all | bytes 2883584 | tf_op jit(solution)/shard_map/route/all_to_all | solution.py:405
  51.7 0.0 copy-start.1
  51.7 2.7 %adjoint.1 = (bf16[8,160,128]{2,1,0:T(8,128)(2,1)S(1)}, f32[48,1280]{1,0:T(8,128)S(1)}, bf16[4,1280,256]{2,1,0:T(8,128)(2,1)S(1)}) custom-call(bf16[32,176,128]{2,1,0:T(8,128)(2,1)S(1)} %all_to_all.30.recv_ref), custom_call_target="tpu_custom_call" | custom-call | flops 1677721600 | bytes 2621440 | tf_op jit(solution)/shard_map/adjoint/pallas_call | solution.py:467
  54.4 0.0 copy-start
  54.4 19.1 %all_to_all.31.flux_ref = bf16[8,160,128]{2,1,0:T(8,128)(2,1)S(1)} all-to-all(bf16[8,160,128]{2,1,0:T(8,128)(2,1)S(1)} %get-tuple-element.9), channel_id=1, replica_groups={{0,34,68,102,129,163,197,231},{8,42,76,110,137,171,205,239},{16,50,84,1..., dimensions={0} | all-to-all | bytes 655360 | tf_op jit(solution)/shard_map/to_rhs/all_to_all | solution.py:405
  73.5 0.0 copy-done.1
  73.5 0.0 copy-start.2
  73.5 0.0 copy-start.3
  73.5 0.0 copy-start.5
  73.5 0.0 copy-start.6
  73.5 0.4 lat_mix.1
  74.0 16.4 %all_to_all.32 = bf16[32,40,128]{2,1,0:T(8,128)(2,1)S(1)} all-to-all(bf16[32,40,128]{2,1,0:T(8,128)(2,1)S(1)} %bitcast.10), channel_id=1, replica_groups={{0,8,16,24,1,9,17,25,2,10,18,26,3,11,19,27,4,12,20,28,5,13,21,29,6,14,2..., dimensions={0} | all-to-all | bytes 655360 | tf_op jit(solution)/shard_map/to_days/all_to_all | solution.py:405
  90.4 0.0 copy-done
  90.4 0.5 day_mix.1
  90.8 15.7 %all_to_all.33 = bf16[32,40,128]{2,1,0:T(8,128)(2,1)S(1)} all-to-all(bf16[32,40,128]{2,1,0:T(8,128)(2,1)S(1)} %bitcast.9), channel_id=1, replica_groups=mesh['wide'=32,'narrow'=8] {'wide'}, dimensions={0} | all-to-all | bytes 655360 | tf_op jit(solution)/shard_map/to_windows/all_to_all | solution.py:405
  106.5 0.0 copy-done.2
  106.5 0.0 copy-done.3
  106.5 0.0 copy-done.5
  106.5 0.0 copy-done.6
  106.5 0.0 copy-start.4
  106.5 2.5 %forward.1 = f32[32,8,128]{2,1,0:T(8,128)S(1)} custom-call(bf16[128,128]{1,0:T(8,128)(2,1)S(1)} %copy-done.6, bf16[1280,128]{1,0:T(8,128)(2,1)S(1)} %bitcast.11, bf16[4,1280,256]{2,1,0:T(8,128)(2,1)S(1)} %get-tuple-element.10.foot_ref, f32[48,1280]{1,0:T(8,128)S(1)} %get-tuple-element.11.meta_ref, f32[8,512]{1,0:T(8,128)S(1)} %copy-done.2, ...), custom_call_target="tpu_custom_call" | custom-call | flops 1677721600 | bytes 2621440 | tf_op jit(solution)/shard_map/forward/pallas_call | solution.py:508
  109.1 14.1 %all_to_all.34.home_ref = f32[32,8,128]{2,1,0:T(8,128)S(1)} all-to-all(f32[32,8,128]{2,1,0:T(8,128)S(1)} %forward.1), channel_id=1, replica_groups=mesh['wide'=32,'narrow'=8] {'wide'}, dimensions={0} | all-to-all | bytes 262144 | tf_op jit(solution)/shard_map/home/all_to_all | solution.py:405
  123.2 9.9 %all_to_all.35.gram_ref = f32[8,8,128]{2,1,0:T(8,128)S(1)} all-to-all(f32[8,8,128]{2,1,0:T(8,128)S(1)} %gram_sum.1), channel_id=1, replica_groups=mesh['wide'=32,'narrow'=8] {'narrow'}, dimensions={0} | all-to-all | bytes 65536 | tf_op jit(solution)/shard_map/gram_sum/all_to_all | solution.py:405
  133.2 0.0 copy-done.4
  133.2 1.8 %update.1 = (f32[8,512]{1,0:T(8,128)}, f32[8,512]{1,0:T(8,128)}, f32[8,512]{1,0:T(8,128)}) custom-call(f32[8,8,128]{2,1,0:T(8,128)S(1)} %all_to_all.35.gram_ref, f32[32,8,128]{2,1,0:T(8,128)S(1)} %all_to_all.34.home_ref, s32[1,512]{1,0:T(1,128)S(1)} %get-tuple-element.12.slot_ref, f32[1,512]{1,0:T(1,128)S(1)} %bitcast.14, f32[8,512]{1,0:T(8,128)S(1)} %copy-done.4, ...), custom_call_target="tpu_custom_call" | custom-call | flops 31457280 | bytes 114688 | tf_op jit(solution)/shard_map/update/pallas_call | solution.py:542
  (1 shorter events, 0.0 us)
Async XLA Ops:
  51.7 21.8 %copy-start.1 = (bf16[128,128]{1,0:T(8,128)(2,1)S(1)}, bf16[128,128]{1,0:T(8,128)(2,1)}, u32[]{:S(2)}) copy-start(bf16[128,128]{1,0:T(8,128)(2,1)} %mix_ref.2) | copy-start | bytes 98308
  54.4 36.0 %copy-start = (bf16[320,320]{1,0:T(8,128)(2,1)S(1)}, bf16[320,320]{1,0:T(8,128)(2,1)}, u32[]{:S(2)}) copy-start(bf16[320,320]{1,0:T(8,128)(2,1)} %mix_ref.3) | copy-start | bytes 614404
  73.5 33.0 %copy-start.2 = (f32[8,512]{1,0:T(8,128)S(1)}, f32[8,512]{1,0:T(8,128)}, u32[]{:S(2)}) copy-start(f32[8,512]{1,0:T(8,128)} %dir_ref.3) | copy-start | bytes 49156
  73.5 33.0 %copy-start.3 = (f32[8,512]{1,0:T(8,128)S(1)}, f32[8,512]{1,0:T(8,128)}, u32[]{:S(2)}) copy-start(f32[8,512]{1,0:T(8,128)} %res_ref.3) | copy-start | bytes 49156
  73.5 33.0 %copy-start.5 = (f32[512]{0:T(512)S(1)}, f32[512]{0:T(512)}, u32[]{:S(2)}) copy-start(f32[512]{0:T(512)} %param.13) | copy-start | bytes 6148
  73.5 33.0 %copy-start.6 = (bf16[128,128]{1,0:T(8,128)(2,1)S(1)}, bf16[128,128]{1,0:T(8,128)(2,1)}, u32[]{:S(2)}) copy-start(bf16[128,128]{1,0:T(8,128)(2,1)} %lon_ref.1) | copy-start | bytes 98308
  106.5 26.6 %copy-start.4 = (f32[8,512]{1,0:T(8,128)S(1)}, f32[8,512]{1,0:T(8,128)}, u32[]{:S(2)}) copy-start(f32[8,512]{1,0:T(8,128)} %sol_ref.1) | copy-start | bytes 49156
